TPU v7x, 512 devices: a whole 4x4x16 slice. The times are simulated.
512 devices in a mesh: gz: 128 (over z, y, core), pa: 4 (over x).
Axes of the slice: x: 4, y: 4, z: 16, core: 2. Of those that a mesh axis runs over, the one named last changes fastest.
Arguments:
- velocity: float32 [3, 128, 192, 512], P(None, 'gz', None, 'pa'), may hold values from -4 to 4
- viscosity: float32 [128, 192, 512], P('gz', None, 'pa'), may hold values from 0.2 to 2
- parcels: float32 [524288, 16], P(('gz', 'pa')), may hold values from -4 to 4, as said below
- dest_rank: int32 [524288, 1], P(('gz', 'pa')), may hold values from 0 to 127; in each aligned block of 1024 rows (0 to 1023, 1024 to 2047, ...) at most 24 rows name the same one
- dest_cell: int32 [524288], P(('gz', 'pa')), may hold values from 0 to 24575
- counts: int32 [512], P(('gz', 'pa')), may hold values from 1 to 1024, 393216 in all
Outputs:
- velocity_out: float32 [3, 128, 192, 512], P(None, 'gz', None, 'pa')
- parcels_out: float32 [1572864, 16], P(('gz', 'pa'))
Inputs may be any that keep to these rules, and one draw needn't show every extreme that they name: `dest_rank`: among the 1024 rows of one device no slab is named more than 24 times, and some block names one slab exactly 24 times. `counts`: some device has all 1024 rows live. `parcels`: columns 4 k + 3 hold positive drag rates.
All inputs are finite; a program needn't handle non-finite values.
Results may differ from a plain program's by a relative error of at most 0.0011.
Values sent between devices are 32-bit elements; how exact they have to be, the bound alone decides.
No kernel may reach another device: no remote copies, remote signals or barrier semaphores. Data moves between devices by JAX's collectives and lax.ppermute only.
A program may use at most 64 MiB of HBM per device.

v0:
```python
import functools
import math

import jax
import jax.numpy as jnp
import numpy as np
from jax import lax
from jax.experimental import pallas as pl
from jax.experimental.pallas import tpu as pltpu
from jax.sharding import PartitionSpec as P

NR = 192
NTH = 512
time_step = 0.1
shift_plane = 0.0001
step_angle = 2.0 * math.pi / NTH
LANES = 128
FEATURES = 16
f32 = jnp.float32
bf16 = jnp.bfloat16


def cas(numbers):
    phase = 2.0 * np.pi / NTH * (numbers % NTH)
    return np.cos(phase) + np.sin(phase)


def split_table(table):
    high = table.astype(jnp.bfloat16)
    low = (table - high.astype(np.float64)).astype(jnp.bfloat16)
    return high, low


@functools.cache
def forward_tables(ring, columns):
    out = []
    for me in range(ring):
        angles = me * columns + np.arange(columns)
        modes = np.concatenate([(me + hop) % ring * columns + np.arange(columns) for hop in range(ring)])
        plain = cas(angles[:, None] * modes[None, :])
        ahead = cas((angles[:, None] + 1) * modes[None, :])
        behind = cas((angles[:, None] - 1) * modes[None, :])
        out.append(np.concatenate(split_table(np.concatenate([plain, behind - ahead], 0)), 1))
    return np.stack(out)


@functools.cache
def inverse_tables(ring, columns):
    out = []
    for me in range(ring):
        angles = me * columns + np.arange(columns)
        modes = np.concatenate([(me - hop) % ring * columns + np.arange(columns) for hop in range(ring)])
        plain = cas(modes[:, None] * angles[None, :]) * (0.5 / NTH)
        ahead = cas(modes[:, None] * (angles[None, :] + 1)) / NTH
        behind = cas(modes[:, None] * (angles[None, :] - 1)) / NTH
        out.append(np.concatenate(split_table(plain) + split_table(ahead - behind), 1))
    return np.stack(out)


@functools.cache
def reduction_tables(ring, columns):
    radius = NR + np.arange(NR) + 0.5
    arc = 1.0 / (radius * step_angle) ** 2
    up = (radius + 0.5) / radius
    down = (radius - 0.5) / radius
    up[-1] = 0.0
    down[0] = 0.0
    modes = np.arange(NTH)
    spectrum = 2.0 - 2.0 * np.cos(step_angle * modes)
    diagonal = shift_plane + arc[:, None] * spectrum[None, :] + up[:, None] + down[:, None]
    lower = np.broadcast_to(-down[:, None], diagonal.shape)
    upper = np.broadcast_to(-up[:, None], diagonal.shape)

    def moved(x, by, fill):
        filled = np.full((abs(by),) + x.shape[1:], fill)
        return np.concatenate([filled, x[:-by]], 0) if by > 0 else np.concatenate([x[-by:], filled], 0)

    tables, stride = [], 1
    while stride < NR:
        low = lower / moved(diagonal, stride, 1.0)
        high = upper / moved(diagonal, -stride, 1.0)
        diagonal = diagonal - low * moved(upper, stride, 0.0) - high * moved(lower, -stride, 0.0)
        lower = -low * moved(lower, stride, 0.0)
        upper = -high * moved(upper, -stride, 0.0)
        tables += [low, high]
        stride *= 2
    tables.append(1.0 / diagonal)
    stacked = np.stack(tables).astype(np.float32)
    return np.ascontiguousarray(stacked.reshape(len(tables), NR, ring, columns).transpose(2, 0, 1, 3))


def pieces(x, count):
    out = []
    for _ in range(count):
        part = x.astype(bf16).astype(f32)
        out.append(part)
        x = x - part
    return out


def dot(a, b, contract):
    return lax.dot_general(a, b, (contract, ((), ())), preferred_element_type=f32)


def iota(shape, dim):
    return lax.broadcasted_iota(jnp.int32, shape, dim)


def pack_kernel(capacity, slabs, counts, parcels, target, cell, velocity, viscosity, send, first, last, spread, hot):
    rows = parcels.shape[1]
    width = 256
    live = iota((1, rows), 1) < counts[0]
    wanted = jnp.where(live, target[...], -1)
    cells = cell[...]
    line = (cells // LANES + 1).astype(f32)
    column = (cells % LANES).astype(f32)
    earlier = (iota((width, width), 0) < iota((width, width), 1)).astype(bf16)
    ones = jnp.ones((width, width), bf16)
    features = FEATURES * capacity
    total = features + 2 * capacity
    passed = None
    for block in range(rows // width):
        here = slice(block * width, (block + 1) * width)
        mine = iota((slabs, width), 0) == wanted[:, here]
        mark = mine.astype(f32)
        before = dot(mark.astype(bf16), earlier, ((1,), (0,)))
        if passed is not None:
            before = before + dot(passed.astype(bf16), ones, ((1,), (0,)))
        passed = mark if passed is None else passed + mark
        slot = jnp.sum(mark * before, axis=0, keepdims=True).astype(jnp.int32)
        chosen = iota((capacity, width), 0) == slot
        hot[:, here] = mark.astype(bf16)
        split = pieces(parcels[:, here], 3)

        def placed(row):
            return jnp.where(chosen, row, 0.0)

        for k, part in enumerate(split):
            base = 0 if k == 0 else total + (k - 1) * features
            for f in range(0, FEATURES, 2):
                pair = jnp.concatenate([placed(part[f : f + 1]), placed(part[f + 1 : f + 2])], 0)
                spread[base + f * capacity : base + (f + 2) * capacity, here] = pair.astype(bf16)
        pair = jnp.concatenate([placed(line[:, here]), placed(column[:, here])], 0)
        spread[features:total, here] = pair.astype(bf16)
    out = dot(spread[...], hot[...], ((1,), (1,)))
    values = out[:features] + (out[total : total + features] + out[total + features :])
    filler = jnp.zeros((send.shape[0] // slabs * LANES - total, slabs), f32)
    whole = jnp.concatenate([values, out[features:total], filler], 0)
    lines = send.shape[0] // slabs
    for c in range(lines):
        send[pl.ds(c, slabs, stride=lines), :] = whole[c * LANES : (c + 1) * LANES].T
    fields = jnp.concatenate([velocity[...], viscosity[...]], 0)
    for b in range(fields.shape[0] // LANES):
        turned = fields[b * LANES : (b + 1) * LANES].T
        first[b : b + 1, :] = turned[:1]
        last[b : b + 1, :] = turned[LANES - 1 :]


def shifted(x, by):
    length = x.shape[0]
    if by % 8 == 0:
        filled = jnp.zeros((abs(by),) + x.shape[1:], x.dtype)
        return jnp.concatenate([filled, x[:-by]], 0) if by > 0 else jnp.concatenate([x[-by:], filled], 0)
    rolled = pltpu.roll(x, by % length, 0)
    row = iota(x.shape, 0)
    inside = row >= by if by > 0 else row < length + by
    return jnp.where(inside, rolled, 0.0)


def momentum_kernel(
    capacity, slabs, received, velocity, viscosity, below_u, above_u, below_n, above_n, left, right, tables,
    ustar, outgoing, moved, table, line_hot, pulled, pushed, sem,
):
    me = lax.axis_index("pa")
    fetch = pltpu.make_async_copy(tables.at[me], table, sem)
    fetch.start()
    lines = received.shape[0] // slabs
    radii, columns = viscosity.shape
    turned = jnp.concatenate([received[pl.ds(c, slabs, stride=lines), :].T for c in range(lines)], 0)
    features = FEATURES * capacity
    line_of = turned[features : features + capacity].astype(jnp.int32) - 1
    column_of = turned[features + capacity : features + 2 * capacity].astype(jnp.int32)
    speeds = [velocity[c * radii : (c + 1) * radii, :] for c in range(3)]
    across = jnp.concatenate([s.T for s in speeds], 0)
    halves = jnp.concatenate([p.astype(bf16) for p in pieces(across, 2)], 1)
    group = 2
    for j in range(0, capacity, group):
        here = slice(j * LANES, (j + group) * LANES)
        lane_line = jnp.concatenate([line_of[s : s + 1] for s in range(j, j + group)], 1)
        lane_column = jnp.concatenate([column_of[s : s + 1] for s in range(j, j + group)], 1)
        hot = (iota((radii, group * LANES), 0) == lane_line).astype(bf16)
        line_hot[:, here] = hot
        picked = dot(halves, jnp.concatenate([hot, hot], 0), ((1,), (0,)))
        match = iota((columns, group * LANES), 0) == lane_column
        for c in range(3):
            got = jnp.sum(jnp.where(match, picked[c * columns : (c + 1) * columns], 0.0), axis=0, keepdims=True)
            for s in range(group):
                pulled[c, j + s : j + s + 1, :] = got[:, s * LANES : (s + 1) * LANES]
    fluid = [pulled[c] for c in range(3)]
    drag = [jnp.zeros_like(fluid[0]) for _ in range(3)]
    for k in range(4):
        rate = turned[(4 * k + 3) * capacity : (4 * k + 4) * capacity]
        weight = time_step * rate
        scale = 1.0 / (1.0 + weight)
        moved[(4 * k + 3) * capacity : (4 * k + 4) * capacity, :] = rate
        for c in range(3):
            at = (4 * k + c) * capacity
            after = (turned[at : at + capacity] + weight * fluid[c]) * scale
            moved[at : at + capacity, :] = after
            drag[c] = drag[c] + rate * (after - fluid[c])
    drag = [d.astype(bf16).astype(f32) for d in drag]
    for j in range(capacity):
        match = iota((columns, LANES), 0) == column_of[j : j + 1]
        for c in range(3):
            pushed[c * columns : (c + 1) * columns, j * LANES : (j + 1) * LANES] = jnp.where(
                match, drag[c][j : j + 1], 0.0
            ).astype(bf16)
    deposit = dot(line_hot[...], pushed[...], ((1,), (1,)))

    radius = iota((radii, columns), 0).astype(f32) + (NR + 0.5)
    arc = 1.0 / (radius * step_angle) ** 2
    lane = iota((radii, columns), 1)
    edges = [e[...].T for e in (left, right)]

    def column(side, field):
        parts, row = [], field * radii
        while row < (field + 1) * radii:
            block, inner = divmod(row, LANES)
            stop = min(LANES, inner + (field + 1) * radii - row)
            parts.append(edges[side][inner:stop, block : block + 1])
            row += stop - inner
        return jnp.concatenate(parts, 0)

    def around(field, x, below, above):
        return (
            above,
            below,
            shifted(x, -1),
            shifted(x, 1),
            jnp.where(lane == columns - 1, column(1, field), pltpu.roll(x, columns - 1, 1)),
            jnp.where(lane == 0, column(0, field), pltpu.roll(x, 1, 1)),
        )

    weights = (0.5, 0.5, 0.5 * (radius + 0.5) / radius, 0.5 * (radius - 0.5) / radius, 0.5 * arc, 0.5 * arc)
    nu = viscosity[...]
    faces = [w * (nu + n) for w, n in zip(weights, around(3, nu, below_n[...], above_n[...]))]
    stars = []
    for c in range(3):
        rows = slice(c * radii, (c + 1) * radii)
        u = speeds[c]
        total = deposit[:, c * columns : (c + 1) * columns]
        for face, beside in zip(faces, around(c, u, below_u[rows, :], above_u[rows, :])):
            total = total + face * (beside - u)
        star = u + time_step * total
        ustar[rows, :] = star
        stars.append(star)
    row = iota((radii, columns), 0)
    flux = jnp.where(row < radii - 1, (radius + 0.5) * 0.5 * (stars[1] + shifted(stars[1], -1)), 0.0)
    inverse = 1.0 / radius
    outward = (shifted(flux, 1) - flux) * inverse
    turning = stars[2] * (inverse * (-0.5 / step_angle))
    high, low = [p.astype(bf16) for p in pieces(jnp.concatenate([outward, turning], 1), 2)]
    fetch.wait()
    wide = table.shape[1] // 2
    contract = ((1,), (0,))
    modes = dot(high, table[:, :wide], contract) + (
        dot(high, table[:, wide:], contract) + dot(low, table[:, :wide], contract)
    )
    for hop in range(wide // columns):
        outgoing[hop] = modes[:, hop * columns : (hop + 1) * columns]


def solve_kernel(own, one, two, three, tables, out, table, sem):
    me = lax.axis_index("pa")
    count = table.shape[0]
    fetches = [pltpu.make_async_copy(tables.at[me, k], table.at[k], sem.at[k]) for k in range(count)]
    for fetch in fetches:
        fetch.start()
    x = (own[...] + one[...]) + (two[...] + three[...])
    radii, columns = x.shape
    radius = iota((radii, columns), 0).astype(f32) + (NR + 0.5)
    total = sum(NR + i + 0.5 for i in range(NR))
    mean = jnp.sum(radius * x, axis=0, keepdims=True) * (1.0 / total)
    constant = (lax.broadcasted_iota(jnp.int32, (1, columns), 1) == 0) & (me == 0)
    x = x - jnp.where(constant, mean, 0.0)
    stride, k = 1, 0
    while stride < radii:
        fetches[k].wait()
        fetches[k + 1].wait()
        x = x - table[k] * shifted(x, stride) - table[k + 1] * shifted(x, -stride)
        stride *= 2
        k += 2
    fetches[k].wait()
    out[...] = x * table[k]


def project_kernel(own, one, two, three, ustar, tables, out, table, sem):
    me = lax.axis_index("pa")
    fetch = pltpu.make_async_copy(tables.at[me], table, sem)
    fetch.start()
    radii, columns = own.shape
    row = iota((radii, columns), 0)

    def gradient(x):
        above = jnp.where(row == radii - 1, x, pltpu.roll(x, radii - 1, 0))
        below = jnp.where(row == 0, x, pltpu.roll(x, 1, 0))
        return above - below

    values = [r[...] for r in (own, one, two, three)]
    slopes = [gradient(x) for x in values]
    contract = ((1,), (0,))

    def product(parts, at):
        high, low = [p.astype(bf16) for p in pieces(jnp.concatenate(parts, 1), 2)]
        table_high = table[:, at : at + columns]
        table_low = table[:, at + columns : at + 2 * columns]
        return dot(high, table_high, contract) + (dot(high, table_low, contract) + dot(low, table_high, contract))

    fetch.wait()
    out[:radii, :] = ustar[:radii, :]
    out[radii : 2 * radii, :] = ustar[radii : 2 * radii, :] - product(slopes, 0)
    radius = row.astype(f32) + (NR + 0.5)
    out[2 * radii :, :] = ustar[2 * radii :, :] - product(values, 2 * columns) * (0.5 / step_angle / radius)


def place_kernel(capacity, slabs, moved, out):
    rows = slabs * capacity
    width = 768
    split = jnp.concatenate([p.astype(bf16) for p in pieces(moved[...], 3)], 1)
    for start in range(0, rows, width):
        place = start + iota((slabs, width), 1)
        hot = (place // capacity == iota((slabs, width), 0)).astype(bf16)
        spread = dot(split, jnp.concatenate([hot, hot, hot], 0), ((1,), (0,)))
        match = (start + iota((capacity, width), 1)) % capacity == iota((capacity, width), 0)
        for f in range(FEATURES):
            block = spread[f * capacity : (f + 1) * capacity]
            out[f : f + 1, start : start + width] = jnp.sum(jnp.where(match, block, 0.0), axis=0, keepdims=True)


def shape(*dims):
    return jax.ShapeDtypeStruct(dims, f32)


def params(mib):
    return pltpu.CompilerParams(vmem_limit_bytes=mib * 1024 * 1024)


def body(velocity, viscosity, parcels, dest_rank, dest_cell, counts):
    slabs = lax.axis_size("gz")
    ring = lax.axis_size("pa")
    planes, radii, columns = viscosity.shape
    block = parcels.shape[0]
    capacity = 3 * block // slabs
    lines = -(-(FEATURES + 2) * capacity // LANES)
    vmem = pl.BlockSpec(memory_space=pltpu.VMEM)
    smem = pl.BlockSpec(memory_space=pltpu.SMEM)
    anywhere = pl.BlockSpec(memory_space=pl.ANY)
    upward = [(i, i + 1) for i in range(slabs - 1)]
    downward = [(i + 1, i) for i in range(slabs - 1)]
    u = velocity.reshape(3 * radii, columns)
    nu = viscosity.reshape(radii, columns)
    below_u = lax.ppermute(u, "gz", upward)
    above_u = lax.ppermute(u, "gz", downward)
    below_n = lax.ppermute(nu, "gz", upward)
    above_n = lax.ppermute(nu, "gz", downward)

    edge_rows = 8
    features = FEATURES * capacity
    send, first, last = pl.pallas_call(
        functools.partial(pack_kernel, capacity, slabs),
        out_shape=(shape(slabs * lines, LANES), shape(edge_rows, LANES), shape(edge_rows, LANES)),
        in_specs=[smem] + [vmem] * 5,
        out_specs=(vmem,) * 3,
        scratch_shapes=[pltpu.VMEM((3 * features + 2 * capacity, block), bf16), pltpu.VMEM((slabs, block), bf16)],
        compiler_params=params(32),
        name="pack",
    )(counts, parcels.T, dest_rank.reshape(1, block), dest_cell.reshape(1, block), u, nu)

    def turn(x, hop):
        return lax.ppermute(x, "pa", [(i, (i + hop) % ring) for i in range(ring)])

    left = turn(last, 1)
    right = turn(first, ring - 1)
    received = lax.all_to_all(
        send.reshape(slabs, lines, LANES), "gz", split_axis=0, concat_axis=0, tiled=True
    ).reshape(slabs * lines, LANES)

    forward = jnp.asarray(forward_tables(ring, columns))
    ustar, outgoing, moved = pl.pallas_call(
        functools.partial(momentum_kernel, capacity, slabs),
        out_shape=(shape(3 * radii, columns), shape(ring, radii, columns), shape(features, slabs)),
        in_specs=[vmem] * 9 + [anywhere],
        out_specs=(vmem,) * 3,
        scratch_shapes=[
            pltpu.VMEM(forward.shape[1:], bf16),
            pltpu.VMEM((radii, capacity * slabs), bf16),
            pltpu.VMEM((3, capacity, slabs), f32),
            pltpu.VMEM((3 * columns, capacity * slabs), bf16),
            pltpu.SemaphoreType.DMA,
        ],
        compiler_params=params(40),
        name="momentum",
    )(received, u, nu, below_u, above_u, below_n, above_n, left, right, forward)

    parts = [outgoing[0]] + [turn(outgoing[hop], hop) for hop in range(1, ring)]
    factors = jnp.asarray(reduction_tables(ring, columns))
    potential = pl.pallas_call(
        solve_kernel,
        out_shape=shape(radii, columns),
        in_specs=[vmem] * 4 + [anywhere],
        out_specs=vmem,
        scratch_shapes=[pltpu.VMEM(factors.shape[1:], f32), pltpu.SemaphoreType.DMA((factors.shape[1],))],
        compiler_params=params(24),
        name="solve",
    )(*parts, factors)

    gathered = [potential] + [turn(potential, hop) for hop in range(1, ring)]
    parcels_out = pl.pallas_call(
        functools.partial(place_kernel, capacity, slabs),
        out_shape=shape(FEATURES, slabs * capacity),
        in_specs=[vmem],
        out_specs=vmem,
        compiler_params=params(32),
        name="place",
    )(moved)
    backward = jnp.asarray(inverse_tables(ring, columns))
    velocity_out = pl.pallas_call(
        project_kernel,
        out_shape=shape(3 * radii, columns),
        in_specs=[vmem] * 5 + [anywhere],
        out_specs=vmem,
        scratch_shapes=[pltpu.VMEM(backward.shape[1:], bf16), pltpu.SemaphoreType.DMA],
        compiler_params=params(24),
        name="project",
    )(*gathered, ustar, backward)
    return velocity_out.reshape(velocity.shape), parcels_out.T


def solution(mesh):
    in_specs = (
        P(None, "gz", None, "pa"),
        P("gz", None, "pa"),
        P(("gz", "pa"), None),
        P(("gz", "pa"), None),
        P(("gz", "pa")),
        P(("gz", "pa")),
    )
    out_specs = (P(None, "gz", None, "pa"), P(("gz", "pa"), None))
    return jax.shard_map(body, mesh=mesh, in_specs=in_specs, out_specs=out_specs, check_vma=False)
```

profile of v0, /device:TPU:32, one launch (start us, length us, event | category | flops | bytes accessed | tf_op | source)
XLA Modules:
  0.0 94.5 jit_solution(4039702454488541080)
XLA Ops:
  5.3 1.8 %pack.1 = (f32[512,128]{1,0:T(8,128)}, f32[8,128]{1,0:T(8,128)S(1)}, f32[8,128]{1,0:T(8,128)S(1)}) custom-call(s32[1]{0:T(128)S(6)} %copy.12.counts, f32[16,1024]{1,0:T(8,128)S(1)} %bitcast.28, s32[1,1024]{1,0:T(1,128)S(1)} %bitcast.29, s32[1,1024]{1,0:T(1,128)S(1)} %bitcast.30, f32[576,128]{1,0:T(8,128)S(1)} %bitcast.21, f32[192,128]{1,0:T(8,128)S(1)} %bitcast.26), custom_call_target="tpu_custom_call" | custom-call | tf_op jit(solution)/shard_map/pack/pallas_call | solution.py:369
  7.2 19.2 %all-to-all-start = ((f32[128,4,128]{2,1,0:T(4,128)}), f32[128,4,128]{2,1,0:T(4,128)S(1)}, u32[]{:S(2)}, u32[]{:S(2)}) async-start(f32[128,4,128]{2,1,0:T(4,128)} %bitcast.5), calls=%async_computation | async-start | bytes 524288 | tf_op jit(solution)/shard_map/all_to_all | solution.py:384
  26.3 4.3 %collective-permute-start.1 = (f32[576,128]{1,0:T(8,128)}, f32[576,128]{1,0:T(8,128)S(1)}, u32[]{:S(2)}, u32[]{:S(2)}) collective-permute-start(f32[576,128]{1,0:T(8,128)} %bitcast.19), channel_id=1, source_target_pairs={{4,0},{8,4},{12,8},{16,12},{20,16},{24,20},{28,24},{32,28},{36,32}... | collective-permute-start | bytes 884744 | tf_op jit(solution)/shard_map/ppermute | solution.py:363
  30.7 1.9 %collective-permute-start = (f32[576,128]{1,0:T(8,128)}, f32[576,128]{1,0:T(8,128)S(1)}, u32[]{:S(2)}, u32[]{:S(2)}) collective-permute-start(f32[576,128]{1,0:T(8,128)} %bitcast.20), channel_id=1, source_target_pairs={{0,4},{4,8},{8,12},{12,16},{16,20},{20,24},{24,28},{28,32},{32,36}... | collective-permute-start | bytes 884744 | tf_op jit(solution)/shard_map/ppermute | solution.py:362
  32.6 5.8 %collective-permute-start.3 = (f32[192,128]{1,0:T(8,128)}, f32[192,128]{1,0:T(8,128)S(1)}, u32[]{:S(2)}, u32[]{:S(2)}) collective-permute-start(f32[192,128]{1,0:T(8,128)} %bitcast.24), channel_id=1, source_target_pairs={{4,0},{8,4},{12,8},{16,12},{20,16},{24,20},{28,24},{32,28},{36,32}... | collective-permute-start | bytes 294920 | tf_op jit(solution)/shard_map/ppermute | solution.py:365
  38.4 1.9 %collective-permute-start.2 = (f32[192,128]{1,0:T(8,128)}, f32[192,128]{1,0:T(8,128)S(1)}, u32[]{:S(2)}, u32[]{:S(2)}) collective-permute-start(f32[192,128]{1,0:T(8,128)} %bitcast.25), channel_id=1, source_target_pairs={{0,4},{4,8},{8,12},{12,16},{16,20},{20,24},{24,28},{28,32},{32,36}... | collective-permute-start | bytes 294920 | tf_op jit(solution)/shard_map/ppermute | solution.py:364
  40.3 3.4 %collective-permute-start.4 = (f32[8,128]{1,0:T(8,128)S(1)}, f32[8,128]{1,0:T(8,128)S(1)}, u32[]{:S(2)}, u32[]{:S(2)}) collective-permute-start(f32[8,128]{1,0:T(8,128)S(1)} %get-tuple-element.9), channel_id=1, source_target_pairs={{0,1},{1,2},{2,3},{3,0},{4,5},{5,6},{6,7},{7,4},{8,9},{9,10},{10,1... | collective-permute-start | bytes 12296 | tf_op jit(solution)/shard_map/ppermute | solution.py:380
  43.7 3.3 %collective-permute-done.4.left = f32[8,128]{1,0:T(8,128)S(1)} collective-permute-done((f32[8,128]{1,0:T(8,128)S(1)}, f32[8,128]{1,0:T(8,128)S(1)}, u32[]{:S(2)}, u32[]{:S(2)}) %collective-permute-start.4) | collective-permute-done | bytes 4128 | tf_op jit(solution)/shard_map/ppermute | solution.py:380
  47.0 3.4 %collective-permute-start.5 = (f32[8,128]{1,0:T(8,128)S(1)}, f32[8,128]{1,0:T(8,128)S(1)}, u32[]{:S(2)}, u32[]{:S(2)}) collective-permute-start(f32[8,128]{1,0:T(8,128)S(1)} %get-tuple-element.10), channel_id=1, source_target_pairs={{0,3},{1,0},{2,1},{3,2},{4,7},{5,4},{6,5},{7,6},{8,11},{9,8},{10,9... | collective-permute-start | bytes 12296 | tf_op jit(solution)/shard_map/ppermute | solution.py:380
  50.5 2.0 %collective-permute-done.5.right = f32[8,128]{1,0:T(8,128)S(1)} collective-permute-done((f32[8,128]{1,0:T(8,128)S(1)}, f32[8,128]{1,0:T(8,128)S(1)}, u32[]{:S(2)}, u32[]{:S(2)}) %collective-permute-start.5) | collective-permute-done | bytes 4128 | tf_op jit(solution)/shard_map/ppermute | solution.py:380
  52.6 1.6 %copy-done.1 = bf16[4,256,1024]{2,1,0:T(8,128)(2,1)S(1)} copy-done((bf16[4,256,1024]{2,1,0:T(8,128)(2,1)S(1)}, bf16[4,256,1024]{2,1,0:T(8,128)(2,1)}, u32[]{:S(2)}) %copy-start.1) | copy-done | bytes 2097176
  56.0 3.6 %momentum.1 = (f32[576,128]{1,0:T(8,128)S(1)}, f32[4,192,128]{2,1,0:T(8,128)S(1)}, f32[384,128]{1,0:T(8,128)S(1)}) custom-call(f32[512,128]{1,0:T(8,128)S(1)} %bitcast.23, f32[576,128]{1,0:T(8,128)S(1)} %bitcast.22, f32[192,128]{1,0:T(8,128)S(1)} %bitcast.27, f32[576,128]{1,0:T(8,128)S(1)} %collective-permute-done.below_u, ...), custom_call_target="tpu_custom_call" | custom-call | tf_op jit(solution)/shard_map/momentum/pallas_call | solution.py:389
  59.6 4.7 %collective-permute-start.8 = (f32[192,128]{1,0:T(8,128)S(1)}, f32[192,128]{1,0:T(8,128)S(1)}, u32[]{:S(2)}, u32[]{:S(2)}) collective-permute-start(f32[192,128]{1,0:T(8,128)S(1)} %get-tuple-element.16), channel_id=1, source_target_pairs={{0,3},{1,0},{2,1},{3,2},{4,7},{5,4},{6,5},{7,6},{8,11},{9,8},{10,9... | collective-permute-start | bytes 294920 | tf_op jit(solution)/shard_map/ppermute | solution.py:380
  64.3 1.9 %collective-permute-start.7 = (f32[192,128]{1,0:T(8,128)S(1)}, f32[192,128]{1,0:T(8,128)S(1)}, u32[]{:S(2)}, u32[]{:S(2)}) collective-permute-start(f32[192,128]{1,0:T(8,128)S(1)} %get-tuple-element.17), channel_id=1, source_target_pairs={{0,2},{1,3},{2,0},{3,1},{4,6},{5,7},{6,4},{7,5},{8,10},{9,11},{10,... | collective-permute-start | bytes 294920 | tf_op jit(solution)/shard_map/ppermute | solution.py:380
  66.2 2.8 %collective-permute-start.6 = (f32[192,128]{1,0:T(8,128)S(1)}, f32[192,128]{1,0:T(8,128)S(1)}, u32[]{:S(2)}, u32[]{:S(2)}) collective-permute-start(f32[192,128]{1,0:T(8,128)S(1)} %get-tuple-element.18), channel_id=1, source_target_pairs={{0,1},{1,2},{2,3},{3,0},{4,5},{5,6},{6,7},{7,4},{8,9},{9,10},{10,1... | collective-permute-start | bytes 294920 | tf_op jit(solution)/shard_map/ppermute | solution.py:380
  69.0 3.3 %collective-permute-done.7.two = f32[192,128]{1,0:T(8,128)S(1)} collective-permute-done((f32[192,128]{1,0:T(8,128)S(1)}, f32[192,128]{1,0:T(8,128)S(1)}, u32[]{:S(2)}, u32[]{:S(2)}) %collective-permute-start.7) | collective-permute-done | bytes 98336 | tf_op jit(solution)/shard_map/ppermute | solution.py:380
  72.3 1.6 %collective-permute-done.6.one = f32[192,128]{1,0:T(8,128)S(1)} collective-permute-done((f32[192,128]{1,0:T(8,128)S(1)}, f32[192,128]{1,0:T(8,128)S(1)}, u32[]{:S(2)}, u32[]{:S(2)}) %collective-permute-start.6) | collective-permute-done | bytes 98336 | tf_op jit(solution)/shard_map/ppermute | solution.py:380
  73.9 2.9 %copy-done = f32[4,17,192,128]{3,2,1,0:T(8,128)S(1)} copy-done((f32[4,17,192,128]{3,2,1,0:T(8,128)S(1)}, f32[4,17,192,128]{3,2,1,0:T(8,128)}, u32[]{:S(2)}) %copy-start) | copy-done | bytes 6684696
  76.8 2.5 %solve.1.own = f32[192,128]{1,0:T(8,128)S(1)} custom-call(f32[192,128]{1,0:T(8,128)S(1)} %get-tuple-element.19.own, f32[192,128]{1,0:T(8,128)S(1)} %collective-permute-done.6.one, f32[192,128]{1,0:T(8,128)S(1)} %collective-permute-done.7.two, f32[192,128]{1,0:T(8,128)S(1)} %collective-permute-done.8.three, f32[4,17,192,128]{3,2,1,0:T(8,128)S(1)} %copy-done), custom_call_target="tpu_custom_call" | custom-call | tf_op jit(solution)/shard_map/solve/pallas_call | solution.py:407
  79.4 2.8 %collective-permute-start.11 = (f32[192,128]{1,0:T(8,128)S(1)}, f32[192,128]{1,0:T(8,128)S(1)}, u32[]{:S(2)}, u32[]{:S(2)}) collective-permute-start(f32[192,128]{1,0:T(8,128)S(1)} %solve.1.own), channel_id=1, source_target_pairs={{0,3},{1,0},{2,1},{3,2},{4,7},{5,4},{6,5},{7,6},{8,11},{9,8},{10,9... | collective-permute-start | bytes 294920 | tf_op jit(solution)/shard_map/ppermute | solution.py:380
  82.1 3.4 %collective-permute-start.10 = (f32[192,128]{1,0:T(8,128)S(1)}, f32[192,128]{1,0:T(8,128)S(1)}, u32[]{:S(2)}, u32[]{:S(2)}) collective-permute-start(f32[192,128]{1,0:T(8,128)S(1)} %solve.1.own), channel_id=1, source_target_pairs={{0,2},{1,3},{2,0},{3,1},{4,6},{5,7},{6,4},{7,5},{8,10},{9,11},{10,... | collective-permute-start | bytes 294920 | tf_op jit(solution)/shard_map/ppermute | solution.py:380
  85.5 3.3 %collective-permute-start.9 = (f32[192,128]{1,0:T(8,128)S(1)}, f32[192,128]{1,0:T(8,128)S(1)}, u32[]{:S(2)}, u32[]{:S(2)}) collective-permute-start(f32[192,128]{1,0:T(8,128)S(1)} %solve.1.own), channel_id=1, source_target_pairs={{0,1},{1,2},{2,3},{3,0},{4,5},{5,6},{6,7},{7,4},{8,9},{9,10},{10,1... | collective-permute-start | bytes 294920 | tf_op jit(solution)/shard_map/ppermute | solution.py:380
  88.8 2.2 %place.1 = f32[16,3072]{1,0:T(8,128)} custom-call(f32[384,128]{1,0:T(8,128)S(1)} %get-tuple-element.13.moved), custom_call_target="tpu_custom_call" | custom-call | tf_op jit(solution)/shard_map/place/pallas_call | solution.py:418
  91.0 2.2 %collective-permute-done.9.one = f32[192,128]{1,0:T(8,128)S(1)} collective-permute-done((f32[192,128]{1,0:T(8,128)S(1)}, f32[192,128]{1,0:T(8,128)S(1)}, u32[]{:S(2)}, u32[]{:S(2)}) %collective-permute-start.9) | collective-permute-done | bytes 98336 | tf_op jit(solution)/shard_map/ppermute | solution.py:380
  (28 shorter events, 7.3 us)
Async XLA Ops:
  1.3 1.0 %copy-start.3 = (f32[3,1,192,128]{3,2,1,0:T(8,128)S(1)}, f32[3,1,192,128]{3,2,1,0:T(8,128)}, u32[]{:S(2)}) copy-start(f32[3,1,192,128]{3,2,1,0:T(8,128)} %param.9) | copy-start | bytes 884740
  2.2 0.9 copy-start.5
  3.1 0.8 copy-start.7
  4.0 0.7 copy-start.8
  4.7 0.7 copy-start.9
  7.2 45.4 %all-to-all-start = ((f32[128,4,128]{2,1,0:T(4,128)}), f32[128,4,128]{2,1,0:T(4,128)S(1)}, u32[]{:S(2)}, u32[]{:S(2)}) async-start(f32[128,4,128]{2,1,0:T(4,128)} %bitcast.5), calls=%async_computation | async-start | bytes 524288 | tf_op jit(solution)/shard_map/all_to_all | solution.py:384
  26.3 26.2 %collective-permute-start.1 = (f32[576,128]{1,0:T(8,128)}, f32[576,128]{1,0:T(8,128)S(1)}, u32[]{:S(2)}, u32[]{:S(2)}) collective-permute-start(f32[576,128]{1,0:T(8,128)} %bitcast.19), channel_id=1, source_target_pairs={{4,0},{8,4},{12,8},{16,12},{20,16},{24,20},{28,24},{32,28},{36,32}... | collective-permute-start | bytes 884744 | tf_op jit(solution)/shard_map/ppermute | solution.py:363
  30.7 21.8 %collective-permute-start = (f32[576,128]{1,0:T(8,128)}, f32[576,128]{1,0:T(8,128)S(1)}, u32[]{:S(2)}, u32[]{:S(2)}) collective-permute-start(f32[576,128]{1,0:T(8,128)} %bitcast.20), channel_id=1, source_target_pairs={{0,4},{4,8},{8,12},{12,16},{16,20},{20,24},{24,28},{28,32},{32,36}... | collective-permute-start | bytes 884744 | tf_op jit(solution)/shard_map/ppermute | solution.py:362
  32.6 19.9 %collective-permute-start.3 = (f32[192,128]{1,0:T(8,128)}, f32[192,128]{1,0:T(8,128)S(1)}, u32[]{:S(2)}, u32[]{:S(2)}) collective-permute-start(f32[192,128]{1,0:T(8,128)} %bitcast.24), channel_id=1, source_target_pairs={{4,0},{8,4},{12,8},{16,12},{20,16},{24,20},{28,24},{32,28},{36,32}... | collective-permute-start | bytes 294920 | tf_op jit(solution)/shard_map/ppermute | solution.py:365
  38.4 14.1 %collective-permute-start.2 = (f32[192,128]{1,0:T(8,128)}, f32[192,128]{1,0:T(8,128)S(1)}, u32[]{:S(2)}, u32[]{:S(2)}) collective-permute-start(f32[192,128]{1,0:T(8,128)} %bitcast.25), channel_id=1, source_target_pairs={{0,4},{4,8},{8,12},{12,16},{16,20},{20,24},{24,28},{28,32},{32,36}... | collective-permute-start | bytes 294920 | tf_op jit(solution)/shard_map/ppermute | solution.py:364
  40.3 6.7 %collective-permute-start.4 = (f32[8,128]{1,0:T(8,128)S(1)}, f32[8,128]{1,0:T(8,128)S(1)}, u32[]{:S(2)}, u32[]{:S(2)}) collective-permute-start(f32[8,128]{1,0:T(8,128)S(1)} %get-tuple-element.9), channel_id=1, source_target_pairs={{0,1},{1,2},{2,3},{3,0},{4,5},{5,6},{6,7},{7,4},{8,9},{9,10},{10,1... | collective-permute-start | bytes 12296 | tf_op jit(solution)/shard_map/ppermute | solution.py:380
  47.0 5.5 %collective-permute-start.5 = (f32[8,128]{1,0:T(8,128)S(1)}, f32[8,128]{1,0:T(8,128)S(1)}, u32[]{:S(2)}, u32[]{:S(2)}) collective-permute-start(f32[8,128]{1,0:T(8,128)S(1)} %get-tuple-element.10), channel_id=1, source_target_pairs={{0,3},{1,0},{2,1},{3,2},{4,7},{5,4},{6,5},{7,6},{8,11},{9,8},{10,9... | collective-permute-start | bytes 12296 | tf_op jit(solution)/shard_map/ppermute | solution.py:380
  52.5 1.6 %copy-start.1 = (bf16[4,256,1024]{2,1,0:T(8,128)(2,1)S(1)}, bf16[4,256,1024]{2,1,0:T(8,128)(2,1)}, u32[]{:S(2)}) copy-start(bf16[4,256,1024]{2,1,0:T(8,128)(2,1)} %constant.6.clone.tables) | copy-start | bytes 6291460
  54.1 1.0 %copy-start.4 = (f32[3,1,192,128]{3,2,1,0:T(8,128)S(1)}, f32[3,1,192,128]{3,2,1,0:T(8,128)}, u32[]{:S(2)}) copy-start(f32[3,1,192,128]{3,2,1,0:T(8,128)} %param.9) | copy-start | bytes 884740
  55.1 0.9 copy-start.6
  59.6 9.4 %collective-permute-start.8 = (f32[192,128]{1,0:T(8,128)S(1)}, f32[192,128]{1,0:T(8,128)S(1)}, u32[]{:S(2)}, u32[]{:S(2)}) collective-permute-start(f32[192,128]{1,0:T(8,128)S(1)} %get-tuple-element.16), channel_id=1, source_target_pairs={{0,3},{1,0},{2,1},{3,2},{4,7},{5,4},{6,5},{7,6},{8,11},{9,8},{10,9... | collective-permute-start | bytes 294920 | tf_op jit(solution)/shard_map/ppermute | solution.py:380
  64.3 8.0 %collective-permute-start.7 = (f32[192,128]{1,0:T(8,128)S(1)}, f32[192,128]{1,0:T(8,128)S(1)}, u32[]{:S(2)}, u32[]{:S(2)}) collective-permute-start(f32[192,128]{1,0:T(8,128)S(1)} %get-tuple-element.17), channel_id=1, source_target_pairs={{0,2},{1,3},{2,0},{3,1},{4,6},{5,7},{6,4},{7,5},{8,10},{9,11},{10,... | collective-permute-start | bytes 294920 | tf_op jit(solution)/shard_map/ppermute | solution.py:380
  66.2 7.7 %collective-permute-start.6 = (f32[192,128]{1,0:T(8,128)S(1)}, f32[192,128]{1,0:T(8,128)S(1)}, u32[]{:S(2)}, u32[]{:S(2)}) collective-permute-start(f32[192,128]{1,0:T(8,128)S(1)} %get-tuple-element.18), channel_id=1, source_target_pairs={{0,1},{1,2},{2,3},{3,0},{4,5},{5,6},{6,7},{7,4},{8,9},{9,10},{10,1... | collective-permute-start | bytes 294920 | tf_op jit(solution)/shard_map/ppermute | solution.py:380
  73.9 2.9 %copy-start = (f32[4,17,192,128]{3,2,1,0:T(8,128)S(1)}, f32[4,17,192,128]{3,2,1,0:T(8,128)}, u32[]{:S(2)}) copy-start(f32[4,17,192,128]{3,2,1,0:T(8,128)} %constant.7.clone.tables) | copy-start | bytes 20054020
  76.8 16.4 %copy-start.2 = (bf16[4,512,512]{2,1,0:T(8,128)(2,1)S(1)}, bf16[4,512,512]{2,1,0:T(8,128)(2,1)}, u32[]{:S(2)}) copy-start(bf16[4,512,512]{2,1,0:T(8,128)(2,1)} %constant.8.clone.tables) | copy-start | bytes 6291460
  79.4 11.6 %collective-permute-start.11 = (f32[192,128]{1,0:T(8,128)S(1)}, f32[192,128]{1,0:T(8,128)S(1)}, u32[]{:S(2)}, u32[]{:S(2)}) collective-permute-start(f32[192,128]{1,0:T(8,128)S(1)} %solve.1.own), channel_id=1, source_target_pairs={{0,3},{1,0},{2,1},{3,2},{4,7},{5,4},{6,5},{7,6},{8,11},{9,8},{10,9... | collective-permute-start | bytes 294920 | tf_op jit(solution)/shard_map/ppermute | solution.py:380
  82.1 8.9 %collective-permute-start.10 = (f32[192,128]{1,0:T(8,128)S(1)}, f32[192,128]{1,0:T(8,128)S(1)}, u32[]{:S(2)}, u32[]{:S(2)}) collective-permute-start(f32[192,128]{1,0:T(8,128)S(1)} %solve.1.own), channel_id=1, source_target_pairs={{0,2},{1,3},{2,0},{3,1},{4,6},{5,7},{6,4},{7,5},{8,10},{9,11},{10,... | collective-permute-start | bytes 294920 | tf_op jit(solution)/shard_map/ppermute | solution.py:380
  85.5 7.7 %collective-permute-start.9 = (f32[192,128]{1,0:T(8,128)S(1)}, f32[192,128]{1,0:T(8,128)S(1)}, u32[]{:S(2)}, u32[]{:S(2)}) collective-permute-start(f32[192,128]{1,0:T(8,128)S(1)} %solve.1.own), channel_id=1, source_target_pairs={{0,1},{1,2},{2,3},{3,0},{4,5},{5,6},{6,7},{7,4},{8,9},{9,10},{10,1... | collective-permute-start | bytes 294920 | tf_op jit(solution)/shard_map/ppermute | solution.py:380
where the time goes:
time: 95.3 us; the launch traced here: 94.5 us
  starting transfers between devices  58.8 us (62%)
  waiting for transfers between devices  12.5 us (13%)
  Pallas kernels  11.4 us (12%)
  local copies, waits for them, and re-layouts  10.4 us (11%)
  between operations  1.46 us (2%)
    ppermute x8, starting transfers between devices, turn(): return lax.ppermute(x, 'pa', [(i, (i + hop) % ring) for i in range(ring)])  25.7 us
    all_to_all x1, starting transfers between devices, body(): lax.all_to_all(send.reshape(slabs, lines, LANES), 'gz', split_axis=0, con...  19.2 us
    ppermute x8, waiting for transfers between devices, turn(): return lax.ppermute(x, 'pa', [(i, (i + hop) % ring) for i in range(ring)])  12.5 us
    unnamed x20, local copies, waits for them, and re-layouts  10.4 us
    ppermute x1, starting transfers between devices, body(): above_n = lax.ppermute(nu, 'gz', downward)  5.75 us
    ppermute x1, starting transfers between devices, body(): above_u = lax.ppermute(u, 'gz', downward)  4.34 us
    pallas_call x1, Pallas kernels, body(): pl.pallas_call(functools.partial(momentum_kernel, capacity, slabs), out_s...  3.56 us
    pallas_call x1, Pallas kernels, body(): pl.pallas_call(solve_kernel, out_shape=shape(radii, columns), in_specs=[v...  2.52 us
  transfers between devices with their start and end apart: 13, of which 5 were waited for; matrix products, arithmetic and copies ran while one was open for 0% of the time, Pallas kernels for 2%

commit v1 on v0

v1 whole, which is shorter than its diff:
```python
import functools
import math

import jax
import jax.numpy as jnp
import numpy as np
from jax import lax
from jax.experimental import pallas as pl
from jax.experimental.pallas import tpu as pltpu
from jax.sharding import PartitionSpec as P

NR = 192
NTH = 512
time_step = 0.1
shift_plane = 0.0001
step_angle = 2.0 * math.pi / NTH
LANES = 128
FEATURES = 16
SUBLANES = 8
EDGE_ROWS = 12
f32 = jnp.float32
bf16 = jnp.bfloat16


def cas(numbers):
    phase = 2.0 * np.pi / NTH * (numbers % NTH)
    return np.cos(phase) + np.sin(phase)


def paired_modes():
    half = NTH // 2
    return np.concatenate([np.arange(half), [half], NTH - np.arange(1, half)])


@functools.cache
def transform_table(ring, columns):
    modes = paired_modes()[None, :]
    plain = cas(np.arange(NTH)[:, None] * modes)
    last = np.arange(ring)[:, None] * columns + columns - 1

    def wave(offset):
        return cas((last + offset) * modes)

    faces = np.zeros((LANES, NTH))
    faces[ring : 2 * ring] = wave(0) - wave(1)
    faces[2 * ring : 3 * ring] = wave(-1) - wave(1) - wave(0) + wave(2)
    faces[8 * ring : 9 * ring] = wave(0)
    faces[9 * ring : 10 * ring] = wave(1)
    table = np.concatenate([plain, faces], 0)
    high = table.astype(jnp.bfloat16)
    low = (table - high.astype(np.float64)).astype(jnp.bfloat16)
    return np.concatenate([high, low], 1)


@functools.cache
def solve_tables():
    radius = NR + np.arange(NR) + 0.5
    arc = 1.0 / (radius * step_angle) ** 2
    up = (radius + 0.5) / radius
    down = (radius - 0.5) / radius
    up[-1] = 0.0
    down[0] = 0.0
    spectrum = 2.0 - 2.0 * np.cos(step_angle * paired_modes())
    diagonal = shift_plane + arc[:, None] * spectrum[None, :] + up[:, None] + down[:, None]
    lower = np.broadcast_to(-down[:, None], diagonal.shape)
    upper = np.broadcast_to(-up[:, None], diagonal.shape)

    def moved(x, by, fill):
        filled = np.full((abs(by),) + x.shape[1:], fill)
        return np.concatenate([filled, x[:-by]], 0) if by > 0 else np.concatenate([x[-by:], filled], 0)

    tables, stride = [], 1
    while stride < SUBLANES:
        low = lower / moved(diagonal, stride, 1.0)
        high = upper / moved(diagonal, -stride, 1.0)
        diagonal = diagonal - low * moved(upper, stride, 0.0) - high * moved(lower, -stride, 0.0)
        lower = -low * moved(lower, stride, 0.0)
        upper = -high * moved(upper, -stride, 0.0)
        tables += [low, high]
        stride *= 2
    multiplier = np.zeros_like(diagonal)
    pivot = diagonal.copy()
    for i in range(SUBLANES, NR):
        multiplier[i] = lower[i] / pivot[i - SUBLANES]
        pivot[i] = diagonal[i] - multiplier[i] * upper[i - SUBLANES]
    tables += [multiplier, 1.0 / pivot, upper / pivot]
    return np.ascontiguousarray(np.stack(tables)[:, :, : 3 * NTH // 4]).astype(np.float32)


@functools.cache
def sine_row():
    row = 2.0 * np.sin(step_angle * np.arange(NTH // 2))
    return np.broadcast_to(row, (SUBLANES, NTH // 2)).astype(np.float32)


def pieces(x, count):
    out = []
    for _ in range(count):
        part = x.astype(bf16).astype(f32)
        out.append(part)
        x = x - part
    return out


def dot(a, b, contract=((1,), (0,))):
    return lax.dot_general(a, b, (contract, ((), ())), preferred_element_type=f32)


def iota(shape, dim):
    return lax.broadcasted_iota(jnp.int32, shape, dim)


def shifted(x, by):
    length = x.shape[0]
    rolled = pltpu.roll(x, by % length, 0)
    row = iota(x.shape, 0)
    return jnp.where(row >= by if by > 0 else row < length + by, rolled, 0.0)


def pack_kernel(
    capacity, slabs, counts_in, parcels_in, target_in, cell_in, velocity_in, viscosity_in, send, fields,
    counts, parcels, target, cell, spread, hot, sems,
):
    radii3 = velocity_in.shape[0]
    copies = [
        pltpu.make_async_copy(source, target_ref, sems.at[k])
        for k, (source, target_ref) in enumerate(
            (
                (counts_in, counts),
                (target_in, target),
                (parcels_in, parcels),
                (cell_in, cell),
                (velocity_in, fields.at[:radii3]),
                (viscosity_in, fields.at[radii3:]),
            )
        )
    ]
    for copy in copies:
        copy.start()
    rows = parcels.shape[1]
    width = 256
    earlier = (iota((width, width), 0) < iota((width, width), 1)).astype(bf16)
    ones = jnp.ones((width, width), bf16)
    features = FEATURES * capacity
    total = features + 2 * capacity
    copies[0].wait()
    copies[1].wait()
    live = iota((1, rows), 1) < counts[0]
    wanted = jnp.where(live, target[...], -1)
    copies[2].wait()
    copies[3].wait()
    cells = cell[...]
    line = (cells // LANES + 1).astype(f32)
    column = (cells % LANES).astype(f32)
    passed = None
    for block in range(rows // width):
        here = slice(block * width, (block + 1) * width)
        mine = iota((slabs, width), 0) == wanted[:, here]
        mark = mine.astype(f32)
        before = dot(mark.astype(bf16), earlier)
        if passed is not None:
            before = before + dot(passed.astype(bf16), ones)
        passed = mark if passed is None else passed + mark
        slot = jnp.sum(mark * before, axis=0, keepdims=True).astype(jnp.int32)
        chosen = iota((capacity, width), 0) == slot
        hot[:, here] = mark.astype(bf16)
        split = pieces(parcels[:, here], 3)

        def placed(row):
            return jnp.where(chosen, row, 0.0)

        for k, part in enumerate(split):
            base = 0 if k == 0 else total + (k - 1) * features
            for f in range(0, FEATURES, 2):
                pair = jnp.concatenate([placed(part[f : f + 1]), placed(part[f + 1 : f + 2])], 0)
                spread[base + f * capacity : base + (f + 2) * capacity, here] = pair.astype(bf16)
        pair = jnp.concatenate([placed(line[:, here]), placed(column[:, here])], 0)
        spread[features:total, here] = pair.astype(bf16)
    out = dot(spread[...], hot[...], ((1,), (1,)))
    values = out[:features] + (out[total : total + features] + out[total + features :])
    filler = jnp.zeros((send.shape[0] // slabs * LANES - total, slabs), f32)
    whole = jnp.concatenate([values, out[features:total], filler], 0)
    lines = send.shape[0] // slabs
    for c in range(lines):
        send[pl.ds(c, slabs, stride=lines), :] = whole[c * LANES : (c + 1) * LANES].T
    copies[4].wait()
    copies[5].wait()


def stencil_kernel(fields, near, far, partial, across, edges):
    radii = fields.shape[0] // 4
    columns = fields.shape[1]
    radius = iota((radii, columns), 0).astype(f32) + (NR + 0.5)
    arc = 1.0 / (radius * step_angle) ** 2
    lane = iota((radii, columns), 1)
    own = [fields[c * radii : (c + 1) * radii, :] for c in range(4)]

    def around(c):
        x = own[c]
        return (
            near[c * radii : (c + 1) * radii, :],
            far[c * radii : (c + 1) * radii, :],
            shifted(x, -1),
            shifted(x, 1),
            pltpu.roll(x, columns - 1, 1),
            pltpu.roll(x, 1, 1),
        )

    weights = (
        0.5,
        0.5,
        0.5 * (radius + 0.5) / radius,
        0.5 * (radius - 0.5) / radius,
        jnp.where(lane == columns - 1, 0.0, 0.5 * arc),
        jnp.where(lane == 0, 0.0, 0.5 * arc),
    )
    faces = [w * (own[3] + n) for w, n in zip(weights, around(3))]
    for c in range(3):
        u = own[c]
        total = jnp.zeros_like(u)
        for face, beside in zip(faces, around(c)):
            total = total + face * (beside - u)
        partial[c * radii : (c + 1) * radii, :] = u + time_step * total
    edges[...] = jnp.zeros_like(edges)
    for c in range(4):
        put_edges(edges, own[c], c, 4 + c)
        if c < 3:
            across[c * columns : (c + 1) * columns, :] = own[c].T


def put_edges(edges, x, first, last):
    turned = x.T
    for part in range(2):
        piece = turned[:, part * LANES : min((part + 1) * LANES, x.shape[0])]
        width = piece.shape[1]
        edges[part * EDGE_ROWS + first : part * EDGE_ROWS + first + 1, :width] = piece[:1]
        edges[part * EDGE_ROWS + last : part * EDGE_ROWS + last + 1, :width] = piece[LANES - 1 :]


def momentum_kernel(
    capacity, slabs, received, partial, across, edges_in, ustar, payload, moved, line_hot, pulled, pushed, edges
):
    lines = received.shape[0] // slabs
    radii = partial.shape[0] // 3
    columns = partial.shape[1]
    turned = jnp.concatenate([received[pl.ds(c, slabs, stride=lines), :].T for c in range(lines)], 0)
    features = FEATURES * capacity
    line_of = turned[features : features + capacity].astype(jnp.int32) - 1
    column_of = turned[features + capacity : features + 2 * capacity].astype(jnp.int32)
    halves = jnp.concatenate([p.astype(bf16) for p in pieces(across[...], 2)], 1)
    group = 2
    for j in range(0, capacity, group):
        here = slice(j * LANES, (j + group) * LANES)
        lane_line = jnp.concatenate([line_of[s : s + 1] for s in range(j, j + group)], 1)
        lane_column = jnp.concatenate([column_of[s : s + 1] for s in range(j, j + group)], 1)
        hot = (iota((radii, group * LANES), 0) == lane_line).astype(bf16)
        line_hot[:, here] = hot
        picked = dot(halves, jnp.concatenate([hot, hot], 0))
        match = iota((columns, group * LANES), 0) == lane_column
        for c in range(3):
            got = jnp.sum(jnp.where(match, picked[c * columns : (c + 1) * columns], 0.0), axis=0, keepdims=True)
            for s in range(group):
                pulled[c, j + s : j + s + 1, :] = got[:, s * LANES : (s + 1) * LANES]
    fluid = [pulled[c] for c in range(3)]
    drag = [jnp.zeros_like(fluid[0]) for _ in range(3)]
    for k in range(4):
        rate = turned[(4 * k + 3) * capacity : (4 * k + 4) * capacity]
        weight = time_step * rate
        scale = 1.0 / (1.0 + weight)
        moved[(4 * k + 3) * capacity : (4 * k + 4) * capacity, :] = rate
        for c in range(3):
            at = (4 * k + c) * capacity
            after = (turned[at : at + capacity] + weight * fluid[c]) * scale
            moved[at : at + capacity, :] = after
            drag[c] = drag[c] + rate * (after - fluid[c])
    drag = [d.astype(bf16).astype(f32) for d in drag]
    for j in range(capacity):
        match = iota((columns, LANES), 0) == column_of[j : j + 1]
        for c in range(3):
            pushed[c * columns : (c + 1) * columns, j * LANES : (j + 1) * LANES] = jnp.where(
                match, drag[c][j : j + 1], 0.0
            ).astype(bf16)
    deposit = dot(line_hot[...], pushed[...], ((1,), (1,)))
    stars = []
    for c in range(3):
        rows = slice(c * radii, (c + 1) * radii)
        star = partial[rows, :] + time_step * deposit[:, c * columns : (c + 1) * columns]
        ustar[rows, :] = star
        stars.append(star)
    row = iota((radii, columns), 0)
    lane = iota((radii, columns), 1)
    radius = row.astype(f32) + (NR + 0.5)
    flux = jnp.where(row < radii - 1, (radius + 0.5) * 0.5 * (stars[1] + shifted(stars[1], -1)), 0.0)
    ahead = jnp.where(lane == columns - 1, 0.0, pltpu.roll(stars[2], columns - 1, 1))
    behind = jnp.where(lane == 0, 0.0, pltpu.roll(stars[2], 1, 1))
    source = (shifted(flux, 1) - flux - (0.5 / step_angle) * (ahead - behind)) / radius
    edges[...] = edges_in[...]
    put_edges(edges, stars[2], 8, 9)
    for q in range(payload.shape[0]):
        payload[q, :radii, :] = source
        payload[q, radii:, :] = edges[...]


def project_kernel(gathered, ustar, transform_in, solve_in, sines_in, out, transform, solve, sines, state, sems):
    me = lax.axis_index("pa")
    fetches = [pltpu.make_async_copy(transform_in, transform, sems.at[0])]
    fetches += [pltpu.make_async_copy(solve_in.at[k], solve.at[k], sems.at[1 + k]) for k in range(solve.shape[0])]
    fetches.append(pltpu.make_async_copy(sines_in, sines, sems.at[1 + solve.shape[0]]))
    for fetch in fetches:
        fetch.start()
    ring = gathered.shape[0]
    radii = out.shape[0] // 3
    columns = out.shape[1]

    def turned(part):
        base = radii + part * EDGE_ROWS
        rows = []
        for c in range(10):
            for q in range(ring):
                source = (q + 1) % ring if c < 4 or c == 8 else q
                rows.append(gathered[source, base + c : base + c + 1, :])
        rows.append(jnp.zeros((LANES - len(rows), LANES), f32))
        return jnp.concatenate(rows, 0).T

    sides = jnp.concatenate([turned(0), turned(1)[: radii - LANES]], 0)
    row = iota((radii, LANES), 0)
    lane = iota((radii, LANES), 1)
    radius = row.astype(f32) + (NR + 0.5)
    inverse = 1.0 / radius

    def lanes_from(x, by):
        return pltpu.roll(x, LANES - by, 1)

    other = lanes_from(sides, 4 * ring)
    both = sides + other
    face = jnp.where(
        lane < ring, lanes_from(both, 3 * ring), jnp.where(lane < 2 * ring, lanes_from(both, 2 * ring), lanes_from(both, ring))
    )
    arc = inverse * inverse * (0.5 * time_step / step_angle**2)
    crossing = jnp.where(lane < 3 * ring, arc * face * (sides - other), 0.0)
    flux = jnp.where(row < radii - 1, (radius + 0.5) * 0.5 * (crossing + shifted(crossing, -1)), 0.0)
    outward = (shifted(flux, 1) - flux) * inverse
    turning = inverse * (0.5 / step_angle)
    coefficients = jnp.where(
        lane < 2 * ring,
        outward,
        jnp.where(lane < 3 * ring, -crossing * turning, jnp.where(lane < 9 * ring, -sides * turning, sides * turning)),
    )
    used = ((lane >= ring) & (lane < 3 * ring)) | ((lane >= 8 * ring) & (lane < 10 * ring))
    coefficients = jnp.where(used, coefficients, 0.0)

    width = 3 * columns
    wide_row = iota((LANES, width), 0)
    wide_lane = iota((LANES, width), 1)
    before = lax.rem(me + ring - 1, ring)
    inside = wide_lane % columns
    at = wide_lane // columns * ring
    pick = jnp.where((inside == columns - 1) & (wide_row == at + me), 1.0, 0.0) - jnp.where(
        (inside == 0) & (wide_row == at + before), 1.0, 0.0
    )
    pick = pick.astype(bf16)
    crossing_parts = [p.astype(bf16) for p in pieces(crossing, 2)]
    delta = dot(crossing_parts[0], pick) + dot(crossing_parts[1], pick)

    values = jnp.concatenate([gathered[q, :radii, :] for q in range(ring)] + [coefficients], 1)
    high, low = [p.astype(bf16) for p in pieces(values, 2)]
    fetches[0].wait()
    table_high = transform[:, :NTH]
    table_low = transform[:, NTH:]
    modes = dot(high, table_high) + (dot(high, table_low) + dot(low, table_high))

    total = sum(NR + i + 0.5 for i in range(NR))
    blocks = [modes[:, b * LANES : (b + 1) * LANES] for b in range(ring)]
    mean = jnp.sum(radius * blocks[0], axis=0, keepdims=True) * (1.0 / total)
    blocks[0] = blocks[0] - jnp.where(iota((1, LANES), 1) == 0, mean, 0.0)
    held = (0, 1, 2, 1)
    for fetch in fetches[1:7]:
        fetch.wait()
    for b in range(ring):
        x = blocks[b]
        cols = slice(held[b] * LANES, (held[b] + 1) * LANES)
        stride, k = 1, 0
        while stride < SUBLANES:
            x = (
                x
                - solve[k, :, cols] * pltpu.roll(x, stride, 0)
                - solve[k + 1, :, cols] * pltpu.roll(x, radii - stride, 0)
            )
            stride *= 2
            k += 2
        state[:, b * LANES : (b + 1) * LANES] = x
    for fetch in fetches[7:]:
        fetch.wait()

    def factors(k, rows):
        return jnp.concatenate([solve[k, rows, : 3 * LANES], solve[k, rows, LANES : 2 * LANES]], 1)

    steps = radii // SUBLANES
    y = state[:SUBLANES, :]
    for v in range(1, steps):
        rows = slice(v * SUBLANES, (v + 1) * SUBLANES)
        y = state[rows, :] - factors(6, rows) * y
        state[rows, :] = y
    x = y * factors(7, slice((steps - 1) * SUBLANES, steps * SUBLANES))
    state[(steps - 1) * SUBLANES :, :] = x
    for v in range(steps - 2, -1, -1):
        rows = slice(v * SUBLANES, (v + 1) * SUBLANES)
        x = state[rows, :] * factors(7, rows) - factors(8, rows) * x
        state[rows, :] = x

    potential = [state[:, b * LANES : (b + 1) * LANES] for b in range(ring)]

    def gradient(x):
        above = jnp.where(row == radii - 1, x, pltpu.roll(x, radii - 1, 0))
        below = jnp.where(row == 0, x, pltpu.roll(x, 1, 0))
        return above - below

    half = ring // 2
    sine = [sines[:1, b * LANES : (b + 1) * LANES] for b in range(half)]
    turns = [-sine[b] * potential[b + half] for b in range(half)] + [sine[b] * potential[b] for b in range(half)]
    both = jnp.concatenate(
        [jnp.concatenate([gradient(x) for x in potential], 1), jnp.concatenate(turns, 1)], 0
    )
    high, low = [p.astype(bf16) for p in pieces(both, 2)]
    mine = pl.ds(pl.multiple_of(me * columns, columns), columns)
    own_high = transform[mine, :NTH]
    own_low = transform[mine, NTH:]
    across = ((1,), (1,))
    result = dot(high, own_high, across) + (dot(high, own_low, across) + dot(low, own_high, across))
    out[:radii, :] = ustar[:radii, :] + delta[:, :columns]
    out[radii : 2 * radii, :] = ustar[radii : 2 * radii, :] + delta[:, columns : 2 * columns] - result[:radii] * (0.5 / NTH)
    out[2 * radii :, :] = ustar[2 * radii :, :] + delta[:, 2 * columns :] - result[radii:] * (turning * (1.0 / NTH))


def place_kernel(capacity, slabs, moved, out):
    rows = slabs * capacity
    width = 768
    split = jnp.concatenate([p.astype(bf16) for p in pieces(moved[...], 3)], 1)
    for start in range(0, rows, width):
        place = start + iota((slabs, width), 1)
        hot = (place // capacity == iota((slabs, width), 0)).astype(bf16)
        spread = dot(split, jnp.concatenate([hot, hot, hot], 0))
        match = (start + iota((capacity, width), 1)) % capacity == iota((capacity, width), 0)
        for f in range(FEATURES):
            block = spread[f * capacity : (f + 1) * capacity]
            out[f : f + 1, start : start + width] = jnp.sum(jnp.where(match, block, 0.0), axis=0, keepdims=True)


def shape(*dims):
    return jax.ShapeDtypeStruct(dims, f32)


def params(mib):
    return pltpu.CompilerParams(vmem_limit_bytes=mib * 1024 * 1024)


def cost(microseconds):
    return pl.CostEstimate(flops=0, bytes_accessed=int(microseconds * 3.0e6), transcendentals=0)


def body(velocity, viscosity, parcels, dest_rank, dest_cell, counts):
    slabs = lax.axis_size("gz")
    ring = lax.axis_size("pa")
    planes, radii, columns = viscosity.shape
    block = parcels.shape[0]
    capacity = 3 * block // slabs
    lines = -(-(FEATURES + 2) * capacity // LANES)
    vmem = pl.BlockSpec(memory_space=pltpu.VMEM)
    hbm = pl.BlockSpec(memory_space=pltpu.HBM)
    u = velocity.reshape(3 * radii, columns)
    nu = viscosity.reshape(radii, columns)
    features = FEATURES * capacity
    send, fields = pl.pallas_call(
        functools.partial(pack_kernel, capacity, slabs),
        out_shape=(shape(slabs * lines, LANES), shape(4 * radii, columns)),
        in_specs=[hbm] * 6,
        out_specs=(vmem,) * 2,
        scratch_shapes=[
            pltpu.SMEM((1,), jnp.int32),
            pltpu.VMEM((FEATURES, block), f32),
            pltpu.VMEM((1, block), jnp.int32),
            pltpu.VMEM((1, block), jnp.int32),
            pltpu.VMEM((3 * features + 2 * capacity, block), bf16),
            pltpu.VMEM((slabs, block), bf16),
            pltpu.SemaphoreType.DMA((6,)),
        ],
        compiler_params=params(32),
        cost_estimate=cost(3),
        name="pack",
    )(counts, parcels.T, dest_rank.reshape(1, block), dest_cell.reshape(1, block), u, nu)
    received = lax.all_to_all(
        send.reshape(slabs, lines, LANES), "gz", split_axis=0, concat_axis=0, tiled=True
    ).reshape(slabs * lines, LANES)

    near = lax.ppermute(fields, "gz", [(i, i ^ 1) for i in range(slabs)])
    pairs = [(i, i + 1) for i in range(1, slabs - 1, 2)]
    far = lax.ppermute(fields, "gz", pairs + [(j, i) for i, j in pairs])
    partial, across, edges = pl.pallas_call(
        stencil_kernel,
        out_shape=(shape(3 * radii, columns), shape(3 * columns, radii), shape(2 * EDGE_ROWS, LANES)),
        in_specs=[vmem] * 3,
        out_specs=(vmem,) * 3,
        compiler_params=params(16),
        cost_estimate=cost(2),
        name="stencil",
    )(fields, near, far)

    ustar, payload, moved = pl.pallas_call(
        functools.partial(momentum_kernel, capacity, slabs),
        out_shape=(
            shape(3 * radii, columns),
            shape(ring, radii + 2 * EDGE_ROWS, columns),
            shape(features, slabs),
        ),
        in_specs=[vmem] * 4,
        out_specs=(vmem,) * 3,
        scratch_shapes=[
            pltpu.VMEM((radii, capacity * slabs), bf16),
            pltpu.VMEM((3, capacity, slabs), f32),
            pltpu.VMEM((3 * columns, capacity * slabs), bf16),
            pltpu.VMEM((2 * EDGE_ROWS, LANES), f32),
        ],
        compiler_params=params(32),
        cost_estimate=cost(4),
        name="momentum",
    )(received, partial, across, edges)

    gathered = lax.all_to_all(payload, "pa", split_axis=0, concat_axis=0, tiled=True)
    parcels_out = pl.pallas_call(
        functools.partial(place_kernel, capacity, slabs),
        out_shape=shape(FEATURES, slabs * capacity),
        in_specs=[vmem],
        out_specs=vmem,
        compiler_params=params(32),
        cost_estimate=cost(3),
        name="place",
    )(moved)
    transform = jnp.asarray(transform_table(ring, columns))
    factors = jnp.asarray(solve_tables())
    sines = jnp.asarray(sine_row())
    velocity_out = pl.pallas_call(
        project_kernel,
        out_shape=shape(3 * radii, columns),
        in_specs=[vmem] * 2 + [hbm] * 3,
        out_specs=vmem,
        scratch_shapes=[
            pltpu.VMEM(transform.shape, bf16),
            pltpu.VMEM(factors.shape, f32),
            pltpu.VMEM(sines.shape, f32),
            pltpu.VMEM((radii, NTH), f32),
            pltpu.SemaphoreType.DMA((factors.shape[0] + 2,)),
        ],
        compiler_params=params(32),
        cost_estimate=cost(5),
        name="project",
    )(gathered, ustar, transform, factors, sines)
    return velocity_out.reshape(velocity.shape), parcels_out.T


def solution(mesh):
    in_specs = (
        P(None, "gz", None, "pa"),
        P("gz", None, "pa"),
        P(("gz", "pa"), None),
        P(("gz", "pa"), None),
        P(("gz", "pa")),
        P(("gz", "pa")),
    )
    out_specs = (P(None, "gz", None, "pa"), P(("gz", "pa"), None))
    return jax.shard_map(body, mesh=mesh, in_specs=in_specs, out_specs=out_specs, check_vma=False)
```

time: 95.3 us -> 75.3 us (0.79)
  starting transfers between devices: 58.8 us -> 29.7 us
  waiting for transfers between devices: 12.5 us -> 20.2 us
  local copies, waits for them, and re-layouts: 10.4 us -> 11.8 us
    ppermute x12 -> x2, starting transfers between devices: 39.6 us -> 6.25 us  [the longest x1 4.33 us: body(): far = lax.ppermute(fields, 'gz', pairs + [(j, i) for i, j in pairs])]
    all_to_all x0 -> x1, waiting for transfers between devices: none -> 5.89 us  [body(): lax.all_to_all(payload, 'pa', split_axis=0, concat_axis=0, tiled=True)]
    all_to_all x0 -> x1, starting transfers between devices: none -> 4.29 us  [body(): lax.all_to_all(payload, 'pa', split_axis=0, concat_axis=0, tiled=True)]
    pallas_call x1, Pallas kernels: 1.31 us -> 3.56 us  [body(): pl.pallas_call(project_kernel, out_shape=shape(3 * radii, columns), in_sp...]
    all_to_all x1, waiting for transfers between devices: 0.01 us -> 2.15 us  [body(): lax.all_to_all(send.reshape(slabs, lines, LANES), 'gz', split_axis=0, con...]
    pallas_call x1, Pallas kernels: 2.52 us -> 0.47 us  [body(): pl.pallas_call(stencil_kernel, out_shape=(shape(3 * radii, columns), shap...]
    unnamed x20 -> x30, local copies, waits for them, and re-layouts: 10.4 us -> 11.8 us
    ppermute x12 -> x2, waiting for transfers between devices: 12.5 us -> 12.1 us  [the longest x1 12.1 us: body(): far = lax.ppermute(fields, 'gz', pairs + [(j, i) for i, j in pairs])]
  transfers between devices with their start and end apart: 13 -> 4, of which waited for: 5 -> 3; matrix products, arithmetic and copies ran while one was open for 0% -> 0% of each run, Pallas kernels for 2% -> 4%
where the time goes in v1:
time: 75.3 us; the launch traced here: 74.7 us
  starting transfers between devices  29.7 us (39%)
  waiting for transfers between devices  20.2 us (27%)
  local copies, waits for them, and re-layouts  11.8 us (16%)
  Pallas kernels  11.4 us (15%)
  between operations  1.51 us (2%)
    all_to_all x1, starting transfers between devices, body(): lax.all_to_all(send.reshape(slabs, lines, LANES), 'gz', split_axis=0, con...  19.2 us
    ppermute x1, waiting for transfers between devices, body(): far = lax.ppermute(fields, 'gz', pairs + [(j, i) for i, j in pairs])  12.1 us
    unnamed x30, local copies, waits for them, and re-layouts  11.8 us
    all_to_all x1, waiting for transfers between devices, body(): lax.all_to_all(payload, 'pa', split_axis=0, concat_axis=0, tiled=True)  5.89 us
    ppermute x1, starting transfers between devices, body(): far = lax.ppermute(fields, 'gz', pairs + [(j, i) for i, j in pairs])  4.33 us
    all_to_all x1, starting transfers between devices, body(): lax.all_to_all(payload, 'pa', split_axis=0, concat_axis=0, tiled=True)  4.29 us
    pallas_call x1, Pallas kernels, body(): pl.pallas_call(project_kernel, out_shape=shape(3 * radii, columns), in_sp...  3.56 us
    pallas_call x1, Pallas kernels, body(): pl.pallas_call(functools.partial(momentum_kernel, capacity, slabs), out_s...  3.5 us
  transfers between devices with their start and end apart: 4, of which 3 were waited for; matrix products, arithmetic and copies ran while one was open for 0% of the time, Pallas kernels for 4%

profile of v1, /device:TPU:32, one launch (start us, length us, event | category | flops | bytes accessed | tf_op | source)
XLA Modules:
  0.0 74.7 jit_solution(72624910910201648)
XLA Ops:
  1.4 1.0 %copy-done.4 = f32[3,1,192,128]{3,2,1,0:T(8,128)S(1)} copy-done((f32[3,1,192,128]{3,2,1,0:T(8,128)S(1)}, f32[3,1,192,128]{3,2,1,0:T(8,128)}, u32[]{:S(2)}) %copy-start.4) | copy-done | bytes 294936
  2.4 0.9 %copy-done.10 = f32[1,192,128]{2,1,0:T(8,128)S(1)} copy-done((f32[1,192,128]{2,1,0:T(8,128)S(1)}, f32[1,192,128]{2,1,0:T(8,128)}, u32[]{:S(2)}) %copy-start.10) | copy-done | bytes 98328
  3.3 0.8 %copy-done.11 = f32[1024,16]{0,1:T(8,128)S(1)} copy-done((f32[1024,16]{0,1:T(8,128)S(1)}, f32[1024,16]{0,1:T(8,128)}, u32[]{:S(2)}) %copy-start.11) | copy-done | bytes 65560
  4.1 0.7 copy-done.13
  4.8 0.7 copy-done.14
  5.5 1.8 %pack.1 = (f32[512,128]{1,0:T(8,128)S(1)}, f32[768,128]{1,0:T(8,128)S(1)}) custom-call(s32[1]{0:T(128)S(6)} %copy.12.counts_in, f32[16,1024]{1,0:T(8,128)S(1)} %bitcast.15, s32[1,1024]{1,0:T(1,128)S(1)} %bitcast.16, s32[1,1024]{1,0:T(1,128)S(1)} %bitcast.17, f32[576,128]{1,0:T(8,128)S(1)} %bitcast.12, f32[192,128]{1,0:T(8,128)S(1)} %bitcast.14), custom_call_target="tpu_custom_call" | custom-call | bytes 9000000 | tf_op jit(solution)/shard_map/pack/pallas_call | solution.py:473
  7.3 0.7 copy-done.7
  8.0 19.2 %all-to-all-start = ((f32[128,4,128]{2,1,0:T(4,128)}), f32[128,4,128]{2,1,0:T(4,128)S(1)}, u32[]{:S(2)}, u32[]{:S(2)}) async-start(f32[128,4,128]{2,1,0:T(4,128)} %bitcast.13), calls=%async_computation | async-start | bytes 524288 | tf_op jit(solution)/shard_map/all_to_all | solution.py:491
  27.2 4.3 %collective-permute-start.1 = (f32[768,128]{1,0:T(8,128)S(1)}, f32[768,128]{1,0:T(8,128)S(1)}, u32[]{:S(2)}, u32[]{:S(2)}) collective-permute-start(f32[768,128]{1,0:T(8,128)S(1)} %get-tuple-element.11.fields), channel_id=1, source_target_pairs={{4,8},{12,16},{20,24},{28,32},{36,40},{44,48},{52,56},{60,64},{68,... | collective-permute-start | bytes 1179656 | tf_op jit(solution)/shard_map/ppermute | solution.py:497
  31.5 1.9 %collective-permute-start = (f32[768,128]{1,0:T(8,128)S(1)}, f32[768,128]{1,0:T(8,128)S(1)}, u32[]{:S(2)}, u32[]{:S(2)}) collective-permute-start(f32[768,128]{1,0:T(8,128)S(1)} %get-tuple-element.11.fields), channel_id=1, source_target_pairs={{0,4},{4,0},{8,12},{12,8},{16,20},{20,16},{24,28},{28,24},{32,36},... | collective-permute-start | bytes 1179656 | tf_op jit(solution)/shard_map/ppermute | solution.py:495
  33.4 12.1 %collective-permute-done.1.far = f32[768,128]{1,0:T(8,128)S(1)} collective-permute-done((f32[768,128]{1,0:T(8,128)S(1)}, f32[768,128]{1,0:T(8,128)S(1)}, u32[]{:S(2)}, u32[]{:S(2)}) %collective-permute-start.1) | collective-permute-done | bytes 393248 | tf_op jit(solution)/shard_map/ppermute | solution.py:497
  46.1 0.7 copy-done.2
  46.8 0.7 copy-done.5
  47.5 2.2 %all-to-all-done = f32[128,4,128]{2,1,0:T(4,128)S(1)} async-done(((f32[128,4,128]{2,1,0:T(4,128)}), f32[128,4,128]{2,1,0:T(4,128)S(1)}, u32[]{:S(2)}, u32[]{:S(2)}) %all-to-all-start) | async-done | bytes 262176 | tf_op jit(solution)/shard_map/all_to_all | solution.py:491
  49.7 1.0 %copy-done.3 = f32[384,192]{1,0:T(8,128)S(1)} copy-done((f32[384,192]{1,0:T(8,128)S(1)}, f32[384,192]{1,0:T(8,128)}, u32[]{:S(2)}) %copy-start.3) | copy-done | bytes 294936
  50.7 1.0 %copy-done.6 = f32[576,128]{1,0:T(8,128)S(1)} copy-done((f32[576,128]{1,0:T(8,128)S(1)}, f32[576,128]{1,0:T(8,128)}, u32[]{:S(2)}) %copy-start.6) | copy-done | bytes 294936
  51.6 3.5 %momentum.1 = (f32[576,128]{1,0:T(8,128)S(1)}, f32[4,216,128]{2,1,0:T(8,128)}, f32[384,128]{1,0:T(8,128)S(1)}) custom-call(f32[512,128]{1,0:T(8,128)S(1)} %bitcast.11, f32[576,128]{1,0:T(8,128)S(1)} %copy-done.6, f32[384,192]{1,0:T(8,128)S(1)} %copy-done.3, f32[24,128]{1,0:T(8,128)S(1)} %get-tuple-element.14.edges_in), custom_call_target="tpu_custom_call" | custom-call | bytes 12000000 | tf_op jit(solution)/shard_map/momentum/pallas_call | solution.py:508
  55.8 4.3 %all-to-all-start.1 = ((f32[4,216,128]{2,1,0:T(8,128)}), f32[4,216,128]{2,1,0:T(8,128)S(1)}, u32[]{:S(2)}, u32[]{:S(2)}) async-start(f32[4,216,128]{2,1,0:T(8,128)} %get-tuple-element.15), calls=%async_computation.1 | async-start | bytes 884736 | tf_op jit(solution)/shard_map/all_to_all | solution.py:528
  60.1 0.9 %copy-done.9 = f32[384,128]{1,0:T(8,128)S(1)} copy-done((f32[384,128]{1,0:T(8,128)S(1)}, f32[384,128]{1,0:T(8,128)}, u32[]{:S(2)}) %copy-start.9) | copy-done | bytes 196632
  61.0 2.1 %place.1 = f32[16,3072]{1,0:T(8,128)} custom-call(f32[384,128]{1,0:T(8,128)S(1)} %copy-done.9), custom_call_target="tpu_custom_call" | custom-call | bytes 9000000 | tf_op jit(solution)/shard_map/place/pallas_call | solution.py:529
  63.2 5.9 %all-to-all-done.1.gathered = f32[4,216,128]{2,1,0:T(8,128)S(1)} async-done(((f32[4,216,128]{2,1,0:T(8,128)}), f32[4,216,128]{2,1,0:T(8,128)S(1)}, u32[]{:S(2)}, u32[]{:S(2)}) %all-to-all-start.1) | async-done | bytes 442400 | tf_op jit(solution)/shard_map/all_to_all | solution.py:528
  69.1 1.3 %copy-done.1 = bf16[640,1024]{1,0:T(8,128)(2,1)S(1)} copy-done((bf16[640,1024]{1,0:T(8,128)(2,1)S(1)}, bf16[640,1024]{1,0:T(8,128)(2,1)}, u32[]{:S(2)}) %copy-start.1) | copy-done | bytes 1310744
  70.4 0.7 copy-done.12
  71.1 3.6 %project.1 = f32[576,128]{1,0:T(8,128)} custom-call(f32[4,216,128]{2,1,0:T(8,128)S(1)} %all-to-all-done.1.gathered, f32[576,128]{1,0:T(8,128)S(1)} %get-tuple-element.16.ustar, bf16[640,1024]{1,0:T(8,128)(2,1)S(1)} %copy-done.1, f32[9,192,384]{2,1,0:T(8,128)S(1)} %copy-done, f32[8,256]{1,0:T(8,128)S(1)} %copy-done.12), custom_call_target="tpu_custom_call" | custom-call | bytes 15000000 | tf_op jit(solution)/shard_map/project/pallas_call | solution.py:541
  (19 shorter events, 1.2 us)
Async XLA Ops:
  0.6 68.4 %copy-start = (f32[9,192,384]{2,1,0:T(8,128)S(1)}, f32[9,192,384]{2,1,0:T(8,128)}, u32[]{:S(2)}) copy-start(f32[9,192,384]{2,1,0:T(8,128)} %constant.7.clone.solve_in) | copy-start | bytes 7962628
  1.4 1.0 %copy-start.4 = (f32[3,1,192,128]{3,2,1,0:T(8,128)S(1)}, f32[3,1,192,128]{3,2,1,0:T(8,128)}, u32[]{:S(2)}) copy-start(f32[3,1,192,128]{3,2,1,0:T(8,128)} %param.9) | copy-start | bytes 884740
  2.4 0.9 %copy-start.10 = (f32[1,192,128]{2,1,0:T(8,128)S(1)}, f32[1,192,128]{2,1,0:T(8,128)}, u32[]{:S(2)}) copy-start(f32[1,192,128]{2,1,0:T(8,128)} %param.10) | copy-start | bytes 294916
  3.3 0.8 %copy-start.11 = (f32[1024,16]{0,1:T(8,128)S(1)}, f32[1024,16]{0,1:T(8,128)}, u32[]{:S(2)}) copy-start(f32[1024,16]{0,1:T(8,128)} %param.11) | copy-start | bytes 196612
  4.1 0.7 copy-start.13
  4.8 0.7 copy-start.14
  7.3 0.7 copy-start.7
  8.0 41.7 %all-to-all-start = ((f32[128,4,128]{2,1,0:T(4,128)}), f32[128,4,128]{2,1,0:T(4,128)S(1)}, u32[]{:S(2)}, u32[]{:S(2)}) async-start(f32[128,4,128]{2,1,0:T(4,128)} %bitcast.13), calls=%async_computation | async-start | bytes 524288 | tf_op jit(solution)/shard_map/all_to_all | solution.py:491
  27.2 18.4 %collective-permute-start.1 = (f32[768,128]{1,0:T(8,128)S(1)}, f32[768,128]{1,0:T(8,128)S(1)}, u32[]{:S(2)}, u32[]{:S(2)}) collective-permute-start(f32[768,128]{1,0:T(8,128)S(1)} %get-tuple-element.11.fields), channel_id=1, source_target_pairs={{4,8},{12,16},{20,24},{28,32},{36,40},{44,48},{52,56},{60,64},{68,... | collective-permute-start | bytes 1179656 | tf_op jit(solution)/shard_map/ppermute | solution.py:497
  31.5 14.1 %collective-permute-start = (f32[768,128]{1,0:T(8,128)S(1)}, f32[768,128]{1,0:T(8,128)S(1)}, u32[]{:S(2)}, u32[]{:S(2)}) collective-permute-start(f32[768,128]{1,0:T(8,128)S(1)} %get-tuple-element.11.fields), channel_id=1, source_target_pairs={{0,4},{4,0},{8,12},{12,8},{16,20},{20,16},{24,28},{28,24},{32,36},... | collective-permute-start | bytes 1179656 | tf_op jit(solution)/shard_map/ppermute | solution.py:495
  46.1 0.8 %copy-start.2 = (f32[384,192]{1,0:T(8,128)}, f32[384,192]{1,0:T(8,128)S(1)}, u32[]{:S(2)}) copy-start(f32[384,192]{1,0:T(8,128)S(1)} %get-tuple-element.13.across) | copy-start | bytes 884740
  46.8 0.7 copy-start.5
  49.7 1.0 %copy-start.3 = (f32[384,192]{1,0:T(8,128)S(1)}, f32[384,192]{1,0:T(8,128)}, u32[]{:S(2)}) copy-start(f32[384,192]{1,0:T(8,128)} %copy-done.2) | copy-start | bytes 884740
  50.7 1.0 %copy-start.6 = (f32[576,128]{1,0:T(8,128)S(1)}, f32[576,128]{1,0:T(8,128)}, u32[]{:S(2)}) copy-start(f32[576,128]{1,0:T(8,128)} %copy-done.5) | copy-start | bytes 884740
  55.1 0.7 copy-start.8
  55.8 13.3 %all-to-all-start.1 = ((f32[4,216,128]{2,1,0:T(8,128)}), f32[4,216,128]{2,1,0:T(8,128)S(1)}, u32[]{:S(2)}, u32[]{:S(2)}) async-start(f32[4,216,128]{2,1,0:T(8,128)} %get-tuple-element.15), calls=%async_computation.1 | async-start | bytes 884736 | tf_op jit(solution)/shard_map/all_to_all | solution.py:528
  60.1 0.9 %copy-start.9 = (f32[384,128]{1,0:T(8,128)S(1)}, f32[384,128]{1,0:T(8,128)}, u32[]{:S(2)}) copy-start(f32[384,128]{1,0:T(8,128)} %copy-done.8) | copy-start | bytes 589828
  69.1 1.3 %copy-start.1 = (bf16[640,1024]{1,0:T(8,128)(2,1)S(1)}, bf16[640,1024]{1,0:T(8,128)(2,1)}, u32[]{:S(2)}) copy-start(bf16[640,1024]{1,0:T(8,128)(2,1)} %constant.6.clone.transform_in) | copy-start | bytes 3932164
  70.4 0.7 copy-start.12

commit v2 on v1

--- a/solution.py
+++ b/solution.py
@@ -451,7 +451,7 @@
 
 
 def params(mib):
-    return pltpu.CompilerParams(vmem_limit_bytes=mib * 1024 * 1024)
+    return pltpu.CompilerParams(vmem_limit_bytes=int(mib * 1024 * 1024))
 
 
 def cost(microseconds):
@@ -484,7 +484,7 @@
             pltpu.VMEM((slabs, block), bf16),
             pltpu.SemaphoreType.DMA((6,)),
         ],
-        compiler_params=params(32),
+        compiler_params=params(60),
         cost_estimate=cost(3),
         name="pack",
     )(counts, parcels.T, dest_rank.reshape(1, block), dest_cell.reshape(1, block), u, nu)
@@ -520,7 +520,7 @@
             pltpu.VMEM((3 * columns, capacity * slabs), bf16),
             pltpu.VMEM((2 * EDGE_ROWS, LANES), f32),
         ],
-        compiler_params=params(32),
+        compiler_params=params(16),
         cost_estimate=cost(4),
         name="momentum",
     )(received, partial, across, edges)
@@ -531,7 +531,7 @@
         out_shape=shape(FEATURES, slabs * capacity),
         in_specs=[vmem],
         out_specs=vmem,
-        compiler_params=params(32),
+        compiler_params=params(16),
         cost_estimate=cost(3),
         name="place",
     )(moved)
@@ -550,7 +550,7 @@
             pltpu.VMEM((radii, NTH), f32),
             pltpu.SemaphoreType.DMA((factors.shape[0] + 2,)),
         ],
-        compiler_params=params(32),
+        compiler_params=params(52),
         cost_estimate=cost(5),
         name="project",
     )(gathered, ustar, transform, factors, sines)

time: 75.3 us -> 66.7 us (0.89)
  local copies, waits for them, and re-layouts: 11.8 us -> 1 us
  waiting for transfers between devices: 20.2 us -> 21.6 us
  Pallas kernels: 11.4 us -> 12.8 us
    unnamed x30 -> x4, local copies, waits for them, and re-layouts: 11.8 us -> 1 us
    pallas_call x1, Pallas kernels: 1.75 us -> 2.9 us  [body(): pl.pallas_call(functools.partial(pack_kernel, capacity, slabs), out_shape...]
    all_to_all x1, waiting for transfers between devices: 5.89 us -> 6.83 us  [body(): lax.all_to_all(payload, 'pa', split_axis=0, concat_axis=0, tiled=True)]
where the time goes in v2:
time: 66.7 us; the launch traced here: 66.4 us
  starting transfers between devices  29.7 us (45%)
  waiting for transfers between devices  21.6 us (32%)
  Pallas kernels  12.8 us (19%)
  between operations  1.34 us (2%)
  local copies, waits for them, and re-layouts  1 us (1%)
    all_to_all x1, starting transfers between devices, body(): lax.all_to_all(send.reshape(slabs, lines, LANES), 'gz', split_axis=0, con...  19.2 us
    ppermute x1, waiting for transfers between devices, body(): far = lax.ppermute(fields, 'gz', pairs + [(j, i) for i, j in pairs])  12.1 us
    all_to_all x1, waiting for transfers between devices, body(): lax.all_to_all(payload, 'pa', split_axis=0, concat_axis=0, tiled=True)  6.83 us
    ppermute x1, starting transfers between devices, body(): far = lax.ppermute(fields, 'gz', pairs + [(j, i) for i, j in pairs])  4.33 us
    all_to_all x1, starting transfers between devices, body(): lax.all_to_all(payload, 'pa', split_axis=0, concat_axis=0, tiled=True)  4.29 us
    pallas_call x1, Pallas kernels, body(): pl.pallas_call(project_kernel, out_shape=shape(3 * radii, columns), in_sp...  3.74 us
    pallas_call x1, Pallas kernels, body(): pl.pallas_call(functools.partial(momentum_kernel, capacity, slabs), out_s...  3.48 us
    pallas_call x1, Pallas kernels, body(): pl.pallas_call(functools.partial(pack_kernel, capacity, slabs), out_shape...  2.9 us
  transfers between devices with their start and end apart: 4, of which 3 were waited for; matrix products, arithmetic and copies ran while one was open for 0% of the time, Pallas kernels for 4%

profile of v2, /device:TPU:32, one launch (start us, length us, event | category | flops | bytes accessed | tf_op | source)
XLA Modules:
  0.0 66.4 jit_solution(9853215355328102458)
XLA Ops:
  0.6 0.0 copy-start.1
  1.3 2.9 %pack.1 = (f32[512,128]{1,0:T(8,128)}, f32[768,128]{1,0:T(8,128)}) custom-call(s32[1]{0:T(128)S(6)} %copy.12.counts_in, f32[16,1024]{1,0:T(8,128)} %bitcast.17, s32[1,1024]{1,0:T(1,128)} %bitcast.18, s32[1,1024]{1,0:T(1,128)} %bitcast.19, f32[576,128]{1,0:T(8,128)} %bitcast.13, f32[192,128]{1,0:T(8,128)} %bitcast.16), custom_call_target="tpu_custom_call" | custom-call | bytes 9000000 | tf_op jit(solution)/shard_map/pack/pallas_call | solution.py:473
  4.2 19.2 %all-to-all-start = ((f32[128,4,128]{2,1,0:T(4,128)}), f32[128,4,128]{2,1,0:T(4,128)S(1)}, u32[]{:S(2)}, u32[]{:S(2)}) async-start(f32[128,4,128]{2,1,0:T(4,128)} %bitcast.14), calls=%async_computation | async-start | bytes 524288 | tf_op jit(solution)/shard_map/all_to_all | solution.py:491
  23.4 4.3 %collective-permute-start.1 = (f32[768,128]{1,0:T(8,128)}, f32[768,128]{1,0:T(8,128)S(1)}, u32[]{:S(2)}, u32[]{:S(2)}) collective-permute-start(f32[768,128]{1,0:T(8,128)} %get-tuple-element.11.fields), channel_id=1, source_target_pairs={{4,8},{12,16},{20,24},{28,32},{36,40},{44,48},{52,56},{60,64},{68,... | collective-permute-start | bytes 1179656 | tf_op jit(solution)/shard_map/ppermute | solution.py:497
  27.7 1.9 %collective-permute-start = (f32[768,128]{1,0:T(8,128)}, f32[768,128]{1,0:T(8,128)S(1)}, u32[]{:S(2)}, u32[]{:S(2)}) collective-permute-start(f32[768,128]{1,0:T(8,128)} %get-tuple-element.11.fields), channel_id=1, source_target_pairs={{0,4},{4,0},{8,12},{12,8},{16,20},{20,16},{24,28},{28,24},{32,36},... | collective-permute-start | bytes 1179656 | tf_op jit(solution)/shard_map/ppermute | solution.py:495
  29.7 12.1 %collective-permute-done.1.far = f32[768,128]{1,0:T(8,128)S(1)} collective-permute-done((f32[768,128]{1,0:T(8,128)}, f32[768,128]{1,0:T(8,128)S(1)}, u32[]{:S(2)}, u32[]{:S(2)}) %collective-permute-start.1) | collective-permute-done | bytes 393248 | tf_op jit(solution)/shard_map/ppermute | solution.py:497
  41.8 0.0 collective-permute-done.near
  41.8 0.0 copy-start
  41.8 1.0 %copy-done = f32[768,128]{1,0:T(8,128)S(1)} copy-done((f32[768,128]{1,0:T(8,128)S(1)}, f32[768,128]{1,0:T(8,128)}, u32[]{:S(2)}) %copy-start) | copy-done | bytes 393240
  42.8 0.5 stencil.1
  43.3 2.6 %all-to-all-done = f32[128,4,128]{2,1,0:T(4,128)S(1)} async-done(((f32[128,4,128]{2,1,0:T(4,128)}), f32[128,4,128]{2,1,0:T(4,128)S(1)}, u32[]{:S(2)}, u32[]{:S(2)}) %all-to-all-start) | async-done | bytes 262176 | tf_op jit(solution)/shard_map/all_to_all | solution.py:491
  45.9 3.5 %momentum.1 = (f32[576,128]{1,0:T(8,128)S(1)}, f32[4,216,128]{2,1,0:T(8,128)}, f32[384,128]{1,0:T(8,128)S(1)}) custom-call(f32[512,128]{1,0:T(8,128)S(1)} %bitcast.11, f32[576,128]{1,0:T(8,128)S(1)} %get-tuple-element.12.partial, f32[384,192]{1,0:T(8,128)S(1)} %get-tuple-element.13.across, f32[24,128]{1,0:T(8,128)S(1)} %get-tuple-element.14.edges_in), custom_call_target="tpu_custom_call" | custom-call | bytes 12000000 | tf_op jit(solution)/shard_map/momentum/pallas_call | solution.py:508
  49.4 4.3 %all-to-all-start.1 = ((f32[4,216,128]{2,1,0:T(8,128)}), f32[4,216,128]{2,1,0:T(8,128)S(1)}, u32[]{:S(2)}, u32[]{:S(2)}) async-start(f32[4,216,128]{2,1,0:T(8,128)} %get-tuple-element.15), calls=%async_computation.1 | async-start | bytes 884736 | tf_op jit(solution)/shard_map/all_to_all | solution.py:528
  53.7 2.1 %place.1 = f32[16,3072]{1,0:T(8,128)} custom-call(f32[384,128]{1,0:T(8,128)S(1)} %get-tuple-element.17.moved), custom_call_target="tpu_custom_call" | custom-call | bytes 9000000 | tf_op jit(solution)/shard_map/place/pallas_call | solution.py:529
  55.8 6.8 %all-to-all-done.1.gathered = f32[4,216,128]{2,1,0:T(8,128)S(1)} async-done(((f32[4,216,128]{2,1,0:T(8,128)}), f32[4,216,128]{2,1,0:T(8,128)S(1)}, u32[]{:S(2)}, u32[]{:S(2)}) %all-to-all-start.1) | async-done | bytes 442400 | tf_op jit(solution)/shard_map/all_to_all | solution.py:528
  62.7 0.0 copy-done.1
  62.7 3.7 %project.1 = f32[576,128]{1,0:T(8,128)} custom-call(f32[4,216,128]{2,1,0:T(8,128)S(1)} %all-to-all-done.1.gathered, f32[576,128]{1,0:T(8,128)S(1)} %get-tuple-element.16.ustar, bf16[640,1024]{1,0:T(8,128)(2,1)} %constant.6.clone.transform_in, f32[9,192,384]{2,1,0:T(8,128)} %constant.7.clone.solve_in, f32[8,256]{1,0:T(8,128)S(1)} %copy-done.1), custom_call_target="tpu_custom_call" | custom-call | bytes 15000000 | tf_op jit(solution)/shard_map/project/pallas_call | solution.py:541
Async XLA Ops:
  0.6 62.0 %copy-start.1 = (f32[8,256]{1,0:T(8,128)S(1)}, f32[8,256]{1,0:T(8,128)}, u32[]{:S(2)}) copy-start(f32[8,256]{1,0:T(8,128)} %constant.8.clone.sines_in) | copy-start | bytes 24580
  4.2 41.7 %all-to-all-start = ((f32[128,4,128]{2,1,0:T(4,128)}), f32[128,4,128]{2,1,0:T(4,128)S(1)}, u32[]{:S(2)}, u32[]{:S(2)}) async-start(f32[128,4,128]{2,1,0:T(4,128)} %bitcast.14), calls=%async_computation | async-start | bytes 524288 | tf_op jit(solution)/shard_map/all_to_all | solution.py:491
  23.4 18.4 %collective-permute-start.1 = (f32[768,128]{1,0:T(8,128)}, f32[768,128]{1,0:T(8,128)S(1)}, u32[]{:S(2)}, u32[]{:S(2)}) collective-permute-start(f32[768,128]{1,0:T(8,128)} %get-tuple-element.11.fields), channel_id=1, source_target_pairs={{4,8},{12,16},{20,24},{28,32},{36,40},{44,48},{52,56},{60,64},{68,... | collective-permute-start | bytes 1179656 | tf_op jit(solution)/shard_map/ppermute | solution.py:497
  27.7 14.1 %collective-permute-start = (f32[768,128]{1,0:T(8,128)}, f32[768,128]{1,0:T(8,128)S(1)}, u32[]{:S(2)}, u32[]{:S(2)}) collective-permute-start(f32[768,128]{1,0:T(8,128)} %get-tuple-element.11.fields), channel_id=1, source_target_pairs={{0,4},{4,0},{8,12},{12,8},{16,20},{20,16},{24,28},{28,24},{32,36},... | collective-permute-start | bytes 1179656 | tf_op jit(solution)/shard_map/ppermute | solution.py:495
  41.8 1.0 %copy-start = (f32[768,128]{1,0:T(8,128)S(1)}, f32[768,128]{1,0:T(8,128)}, u32[]{:S(2)}) copy-start(f32[768,128]{1,0:T(8,128)} %get-tuple-element.11.fields) | copy-start | bytes 1179652
  49.4 13.3 %all-to-all-start.1 = ((f32[4,216,128]{2,1,0:T(8,128)}), f32[4,216,128]{2,1,0:T(8,128)S(1)}, u32[]{:S(2)}, u32[]{:S(2)}) async-start(f32[4,216,128]{2,1,0:T(8,128)} %get-tuple-element.15), calls=%async_computation.1 | async-start | bytes 884736 | tf_op jit(solution)/shard_map/all_to_all | solution.py:528

commit v3 on v2

--- a/solution.py
+++ b/solution.py
@@ -17,7 +17,8 @@
 LANES = 128
 FEATURES = 16
 SUBLANES = 8
-EDGE_ROWS = 12
+EDGE_ROWS = 16
+CORRECTION_ROWS = 64
 f32 = jnp.float32
 bf16 = jnp.bfloat16
 
@@ -28,24 +29,25 @@
 
 
 def paired_modes():
-    half = NTH // 2
-    return np.concatenate([np.arange(half), [half], NTH - np.arange(1, half)])
+    half, even, odd = NTH // 2, np.arange(0, NTH // 2, 2), np.arange(1, NTH // 2, 2)
+    return np.concatenate([even, [half], NTH - even[1:], odd, NTH - odd])
 
 
 @functools.cache
 def transform_table(ring, columns):
     modes = paired_modes()[None, :]
-    plain = cas(np.arange(NTH)[:, None] * modes)
-    last = np.arange(ring)[:, None] * columns + columns - 1
-
-    def wave(offset):
-        return cas((last + offset) * modes)
-
-    faces = np.zeros((LANES, NTH))
-    faces[ring : 2 * ring] = wave(0) - wave(1)
-    faces[2 * ring : 3 * ring] = wave(-1) - wave(1) - wave(0) + wave(2)
-    faces[8 * ring : 9 * ring] = wave(0)
-    faces[9 * ring : 10 * ring] = wave(1)
+    plain = cas(np.arange(NTH // 2)[:, None] * modes)
+    faces = np.zeros((CORRECTION_ROWS, NTH))
+    for q in range(ring):
+        last, at = q * columns + columns - 1, q * EDGE_ROWS
+
+        def wave(offset):
+            return cas((last + offset) * modes)
+
+        faces[at + 5] = wave(0) - wave(1)
+        faces[at + 6] = wave(-1) - wave(1) - wave(0) + wave(2)
+        faces[at + 8] = wave(0)
+        faces[at + 9] = wave(1)
     table = np.concatenate([plain, faces], 0)
     high = table.astype(jnp.bfloat16)
     low = (table - high.astype(np.float64)).astype(jnp.bfloat16)
@@ -84,13 +86,9 @@
         multiplier[i] = lower[i] / pivot[i - SUBLANES]
         pivot[i] = diagonal[i] - multiplier[i] * upper[i - SUBLANES]
     tables += [multiplier, 1.0 / pivot, upper / pivot]
-    return np.ascontiguousarray(np.stack(tables)[:, :, : 3 * NTH // 4]).astype(np.float32)
-
-
-@functools.cache
-def sine_row():
-    row = 2.0 * np.sin(step_angle * np.arange(NTH // 2))
-    return np.broadcast_to(row, (SUBLANES, NTH // 2)).astype(np.float32)
+    sine = 2.0 * np.sin(step_angle * paired_modes())
+    tables.append(np.broadcast_to(sine, (SUBLANES, NTH)))
+    return np.concatenate(tables, 0)[:, : 3 * NTH // 4].astype(np.float32)
 
 
 def pieces(x, count):
@@ -164,7 +162,7 @@
         slot = jnp.sum(mark * before, axis=0, keepdims=True).astype(jnp.int32)
         chosen = iota((capacity, width), 0) == slot
         hot[:, here] = mark.astype(bf16)
-        split = pieces(parcels[:, here], 3)
+        split = pieces(parcels[:, here], 2)
 
         def placed(row):
             return jnp.where(chosen, row, 0.0)
@@ -177,7 +175,7 @@
         pair = jnp.concatenate([placed(line[:, here]), placed(column[:, here])], 0)
         spread[features:total, here] = pair.astype(bf16)
     out = dot(spread[...], hot[...], ((1,), (1,)))
-    values = out[:features] + (out[total : total + features] + out[total + features :])
+    values = out[:features] + out[total:]
     filler = jnp.zeros((send.shape[0] // slabs * LANES - total, slabs), f32)
     whole = jnp.concatenate([values, out[features:total], filler], 0)
     lines = send.shape[0] // slabs
@@ -187,7 +185,7 @@
     copies[5].wait()
 
 
-def stencil_kernel(fields, near, far, partial, across, edges):
+def stencil_kernel(fields, near, far, partial, halves, edges):
     radii = fields.shape[0] // 4
     columns = fields.shape[1]
     radius = iota((radii, columns), 0).astype(f32) + (NR + 0.5)
@@ -225,7 +223,9 @@
     for c in range(4):
         put_edges(edges, own[c], c, 4 + c)
         if c < 3:
-            across[c * columns : (c + 1) * columns, :] = own[c].T
+            turned = own[c].T
+            parts = [p.astype(bf16) for p in pieces(turned, 2)]
+            halves[c * columns : (c + 1) * columns, :] = jnp.concatenate(parts, 1)
 
 
 def put_edges(edges, x, first, last):
@@ -238,7 +238,7 @@
 
 
 def momentum_kernel(
-    capacity, slabs, received, partial, across, edges_in, ustar, payload, moved, line_hot, pulled, pushed, edges
+    capacity, slabs, received, partial, halves, edges_in, ustar, payload, moved, line_hot, pulled, pushed, edges
 ):
     lines = received.shape[0] // slabs
     radii = partial.shape[0] // 3
@@ -247,7 +247,6 @@
     features = FEATURES * capacity
     line_of = turned[features : features + capacity].astype(jnp.int32) - 1
     column_of = turned[features + capacity : features + 2 * capacity].astype(jnp.int32)
-    halves = jnp.concatenate([p.astype(bf16) for p in pieces(across[...], 2)], 1)
     group = 2
     for j in range(0, capacity, group):
         here = slice(j * LANES, (j + group) * LANES)
@@ -255,7 +254,7 @@
         lane_column = jnp.concatenate([column_of[s : s + 1] for s in range(j, j + group)], 1)
         hot = (iota((radii, group * LANES), 0) == lane_line).astype(bf16)
         line_hot[:, here] = hot
-        picked = dot(halves, jnp.concatenate([hot, hot], 0))
+        picked = dot(halves[...], jnp.concatenate([hot, hot], 0))
         match = iota((columns, group * LANES), 0) == lane_column
         for c in range(3):
             got = jnp.sum(jnp.where(match, picked[c * columns : (c + 1) * columns], 0.0), axis=0, keepdims=True)
@@ -301,81 +300,92 @@
         payload[q, radii:, :] = edges[...]
 
 
-def project_kernel(gathered, ustar, transform_in, solve_in, sines_in, out, transform, solve, sines, state, sems):
+def project_kernel(gathered, ustar, transform, solve_a, solve_b, solve_c, out, solve, state, sems):
     me = lax.axis_index("pa")
-    fetches = [pltpu.make_async_copy(transform_in, transform, sems.at[0])]
-    fetches += [pltpu.make_async_copy(solve_in.at[k], solve.at[k], sems.at[1 + k]) for k in range(solve.shape[0])]
-    fetches.append(pltpu.make_async_copy(sines_in, sines, sems.at[1 + solve.shape[0]]))
+    steps = 3 * NR
+    fetches = [
+        pltpu.make_async_copy(solve_b, solve.at[:steps], sems.at[0]),
+        pltpu.make_async_copy(solve_c, solve.at[steps:], sems.at[1]),
+    ]
     for fetch in fetches:
         fetch.start()
     ring = gathered.shape[0]
     radii = out.shape[0] // 3
     columns = out.shape[1]
+    half = NTH // 2
 
     def turned(part):
         base = radii + part * EDGE_ROWS
-        rows = []
-        for c in range(10):
-            for q in range(ring):
-                source = (q + 1) % ring if c < 4 or c == 8 else q
-                rows.append(gathered[source, base + c : base + c + 1, :])
-        rows.append(jnp.zeros((LANES - len(rows), LANES), f32))
+        rows = [gathered[q % ring, base : base + EDGE_ROWS, :] for q in range(ring + 1)]
+        rows.append(jnp.zeros((LANES - (ring + 1) * EDGE_ROWS, LANES), f32))
         return jnp.concatenate(rows, 0).T
 
     sides = jnp.concatenate([turned(0), turned(1)[: radii - LANES]], 0)
     row = iota((radii, LANES), 0)
     lane = iota((radii, LANES), 1)
+    kind = lane % EDGE_ROWS
     radius = row.astype(f32) + (NR + 0.5)
     inverse = 1.0 / radius
 
     def lanes_from(x, by):
         return pltpu.roll(x, LANES - by, 1)
 
-    other = lanes_from(sides, 4 * ring)
-    both = sides + other
-    face = jnp.where(
-        lane < ring, lanes_from(both, 3 * ring), jnp.where(lane < 2 * ring, lanes_from(both, 2 * ring), lanes_from(both, ring))
-    )
+    beyond = lanes_from(sides, EDGE_ROWS - 4)
+    both = sides + beyond
+    face = jnp.where(kind == 4, lanes_from(both, 3), jnp.where(kind == 5, lanes_from(both, 2), lanes_from(both, 1)))
     arc = inverse * inverse * (0.5 * time_step / step_angle**2)
-    crossing = jnp.where(lane < 3 * ring, arc * face * (sides - other), 0.0)
+    used = lane < ring * EDGE_ROWS
+    crossing = jnp.where(used & (kind >= 4) & (kind < 7), arc * face * (beyond - sides), 0.0)
     flux = jnp.where(row < radii - 1, (radius + 0.5) * 0.5 * (crossing + shifted(crossing, -1)), 0.0)
     outward = (shifted(flux, 1) - flux) * inverse
     turning = inverse * (0.5 / step_angle)
     coefficients = jnp.where(
-        lane < 2 * ring,
+        kind == 5,
         outward,
-        jnp.where(lane < 3 * ring, -crossing * turning, jnp.where(lane < 9 * ring, -sides * turning, sides * turning)),
+        turning * jnp.where(kind == 6, -crossing, jnp.where(kind == 8, -lanes_from(sides, EDGE_ROWS), sides)),
     )
-    used = ((lane >= ring) & (lane < 3 * ring)) | ((lane >= 8 * ring) & (lane < 10 * ring))
-    coefficients = jnp.where(used, coefficients, 0.0)
+    used = used & ((kind == 5) | (kind == 6) | (kind == 8) | (kind == 9))
+    coefficients = jnp.where(used, coefficients, 0.0)[:, :CORRECTION_ROWS]
 
     width = 3 * columns
     wide_row = iota((LANES, width), 0)
     wide_lane = iota((LANES, width), 1)
     before = lax.rem(me + ring - 1, ring)
     inside = wide_lane % columns
-    at = wide_lane // columns * ring
-    pick = jnp.where((inside == columns - 1) & (wide_row == at + me), 1.0, 0.0) - jnp.where(
-        (inside == 0) & (wide_row == at + before), 1.0, 0.0
+    at = wide_lane // columns + 4
+    pick = jnp.where((inside == columns - 1) & (wide_row == at + me * EDGE_ROWS), 1.0, 0.0) - jnp.where(
+        (inside == 0) & (wide_row == at + before * EDGE_ROWS), 1.0, 0.0
     )
     pick = pick.astype(bf16)
     crossing_parts = [p.astype(bf16) for p in pieces(crossing, 2)]
     delta = dot(crossing_parts[0], pick) + dot(crossing_parts[1], pick)
 
-    values = jnp.concatenate([gathered[q, :radii, :] for q in range(ring)] + [coefficients], 1)
-    high, low = [p.astype(bf16) for p in pieces(values, 2)]
-    fetches[0].wait()
-    table_high = transform[:, :NTH]
-    table_low = transform[:, NTH:]
-    modes = dot(high, table_high) + (dot(high, table_low) + dot(low, table_high))
-
+    near = jnp.concatenate([gathered[q, :radii, :] for q in range(ring // 2)], 1)
+    distant = jnp.concatenate([gathered[q, :radii, :] for q in range(ring // 2, ring)], 1)
+
+    def product(x, rows, cols, contract=((1,), (0,))):
+        high, low = [p.astype(bf16) for p in pieces(x, 2)]
+        table_high = transform[rows, cols]
+        table_low = transform[rows, slice(cols.start + NTH, cols.stop + NTH)]
+        return dot(high, table_high, contract) + (dot(high, table_low, contract) + dot(low, table_high, contract))
+
+    angles = slice(0, half)
+    corrections = slice(half, half + CORRECTION_ROWS)
+    even = slice(0, half)
+    odd = slice(half, NTH)
+    modes_even = product(near + distant, angles, even) + product(coefficients, corrections, even)
+    modes_odd = product(near - distant, angles, odd) + product(coefficients, corrections, odd)
+    blocks = [m[:, b * LANES : (b + 1) * LANES] for m in (modes_even, modes_odd) for b in range(2)]
     total = sum(NR + i + 0.5 for i in range(NR))
-    blocks = [modes[:, b * LANES : (b + 1) * LANES] for b in range(ring)]
     mean = jnp.sum(radius * blocks[0], axis=0, keepdims=True) * (1.0 / total)
     blocks[0] = blocks[0] - jnp.where(iota((1, LANES), 1) == 0, mean, 0.0)
-    held = (0, 1, 2, 1)
-    for fetch in fetches[1:7]:
-        fetch.wait()
+    held = (0, 1, 2, 2)
+
+    def factor(k, cols):
+        at = k % 3 * radii
+        return (solve_a if k < 3 else solve)[at : at + radii, cols]
+
+    fetches[0].wait()
     for b in range(ring):
         x = blocks[b]
         cols = slice(held[b] * LANES, (held[b] + 1) * LANES)
@@ -383,29 +393,30 @@
         while stride < SUBLANES:
             x = (
                 x
-                - solve[k, :, cols] * pltpu.roll(x, stride, 0)
-                - solve[k + 1, :, cols] * pltpu.roll(x, radii - stride, 0)
+                - factor(k, cols) * pltpu.roll(x, stride, 0)
+                - factor(k + 1, cols) * pltpu.roll(x, radii - stride, 0)
             )
             stride *= 2
             k += 2
         state[:, b * LANES : (b + 1) * LANES] = x
-    for fetch in fetches[7:]:
-        fetch.wait()
-
-    def factors(k, rows):
-        return jnp.concatenate([solve[k, rows, : 3 * LANES], solve[k, rows, LANES : 2 * LANES]], 1)
+
+    fetches[1].wait()
+
+    def factors(k, v):
+        rows = slice((k - 3) * radii + v * SUBLANES, (k - 3) * radii + (v + 1) * SUBLANES)
+        return jnp.concatenate([solve[rows, : 3 * LANES], solve[rows, 2 * LANES : 3 * LANES]], 1)
 
     steps = radii // SUBLANES
     y = state[:SUBLANES, :]
     for v in range(1, steps):
         rows = slice(v * SUBLANES, (v + 1) * SUBLANES)
-        y = state[rows, :] - factors(6, rows) * y
+        y = state[rows, :] - factors(6, v) * y
         state[rows, :] = y
-    x = y * factors(7, slice((steps - 1) * SUBLANES, steps * SUBLANES))
+    x = y * factors(7, steps - 1)
     state[(steps - 1) * SUBLANES :, :] = x
     for v in range(steps - 2, -1, -1):
         rows = slice(v * SUBLANES, (v + 1) * SUBLANES)
-        x = state[rows, :] * factors(7, rows) - factors(8, rows) * x
+        x = state[rows, :] * factors(7, v) - factors(8, v) * x
         state[rows, :] = x
 
     potential = [state[:, b * LANES : (b + 1) * LANES] for b in range(ring)]
@@ -415,18 +426,15 @@
         below = jnp.where(row == 0, x, pltpu.roll(x, 1, 0))
         return above - below
 
-    half = ring // 2
-    sine = [sines[:1, b * LANES : (b + 1) * LANES] for b in range(half)]
-    turns = [-sine[b] * potential[b + half] for b in range(half)] + [sine[b] * potential[b] for b in range(half)]
-    both = jnp.concatenate(
-        [jnp.concatenate([gradient(x) for x in potential], 1), jnp.concatenate(turns, 1)], 0
-    )
-    high, low = [p.astype(bf16) for p in pieces(both, 2)]
-    mine = pl.ds(pl.multiple_of(me * columns, columns), columns)
-    own_high = transform[mine, :NTH]
-    own_low = transform[mine, NTH:]
-    across = ((1,), (1,))
-    result = dot(high, own_high, across) + (dot(high, own_low, across) + dot(low, own_high, across))
+    mine = pl.ds(pl.multiple_of(me % 2 * columns, columns), columns)
+    result = []
+    for group, cols in ((0, even), (1, odd)):
+        plain, mirror = potential[2 * group], potential[2 * group + 1]
+        sine = solve[6 * radii : 6 * radii + 1, 2 * group * LANES : (2 * group + 1) * LANES]
+        slopes = jnp.concatenate([gradient(plain), gradient(mirror)], 1)
+        turns = jnp.concatenate([-sine * mirror, sine * plain], 1)
+        result.append(product(jnp.concatenate([slopes, turns], 0), mine, cols, ((1,), (1,))))
+    result = result[0] + jnp.where(me >= ring // 2, -1.0, 1.0) * result[1]
     out[:radii, :] = ustar[:radii, :] + delta[:, :columns]
     out[radii : 2 * radii, :] = ustar[radii : 2 * radii, :] + delta[:, columns : 2 * columns] - result[:radii] * (0.5 / NTH)
     out[2 * radii :, :] = ustar[2 * radii :, :] + delta[:, 2 * columns :] - result[radii:] * (turning * (1.0 / NTH))
@@ -480,7 +488,7 @@
             pltpu.VMEM((FEATURES, block), f32),
             pltpu.VMEM((1, block), jnp.int32),
             pltpu.VMEM((1, block), jnp.int32),
-            pltpu.VMEM((3 * features + 2 * capacity, block), bf16),
+            pltpu.VMEM((2 * features + 2 * capacity, block), bf16),
             pltpu.VMEM((slabs, block), bf16),
             pltpu.SemaphoreType.DMA((6,)),
         ],
@@ -495,9 +503,15 @@
     near = lax.ppermute(fields, "gz", [(i, i ^ 1) for i in range(slabs)])
     pairs = [(i, i + 1) for i in range(1, slabs - 1, 2)]
     far = lax.ppermute(fields, "gz", pairs + [(j, i) for i, j in pairs])
-    partial, across, edges = pl.pallas_call(
+    transform = jnp.asarray(transform_table(ring, columns))
+    factors = solve_tables()
+    partial, halves, edges = pl.pallas_call(
         stencil_kernel,
-        out_shape=(shape(3 * radii, columns), shape(3 * columns, radii), shape(2 * EDGE_ROWS, LANES)),
+        out_shape=(
+            shape(3 * radii, columns),
+            jax.ShapeDtypeStruct((3 * columns, 2 * radii), bf16),
+            shape(2 * EDGE_ROWS, LANES),
+        ),
         in_specs=[vmem] * 3,
         out_specs=(vmem,) * 3,
         compiler_params=params(16),
@@ -523,7 +537,7 @@
         compiler_params=params(16),
         cost_estimate=cost(4),
         name="momentum",
-    )(received, partial, across, edges)
+    )(received, partial, halves, edges)
 
     gathered = lax.all_to_all(payload, "pa", split_axis=0, concat_axis=0, tiled=True)
     parcels_out = pl.pallas_call(
@@ -535,25 +549,20 @@
         cost_estimate=cost(3),
         name="place",
     )(moved)
-    transform = jnp.asarray(transform_table(ring, columns))
-    factors = jnp.asarray(solve_tables())
-    sines = jnp.asarray(sine_row())
     velocity_out = pl.pallas_call(
         project_kernel,
         out_shape=shape(3 * radii, columns),
-        in_specs=[vmem] * 2 + [hbm] * 3,
+        in_specs=[vmem] * 4 + [hbm] * 2,
         out_specs=vmem,
         scratch_shapes=[
-            pltpu.VMEM(transform.shape, bf16),
-            pltpu.VMEM(factors.shape, f32),
-            pltpu.VMEM(sines.shape, f32),
+            pltpu.VMEM((factors.shape[0] - 3 * radii, factors.shape[1]), f32),
             pltpu.VMEM((radii, NTH), f32),
-            pltpu.SemaphoreType.DMA((factors.shape[0] + 2,)),
+            pltpu.SemaphoreType.DMA((2,)),
         ],
-        compiler_params=params(52),
+        compiler_params=params(51.5),
         cost_estimate=cost(5),
         name="project",
-    )(gathered, ustar, transform, factors, sines)
+    )(gathered, ustar, transform, factors[: 3 * radii], factors[3 * radii : 6 * radii], factors[6 * radii :])
     return velocity_out.reshape(velocity.shape), parcels_out.T
 
 

time: 66.7 us -> 66 us (0.990)
  Pallas kernels: 12.8 us -> 11.7 us
  waiting for transfers between devices: 21.6 us -> 22.6 us
  local copies, waits for them, and re-layouts: 1 us -> 0.01 us
    unnamed x4 -> x6, local copies, waits for them, and re-layouts: 1 us -> 0.01 us
    pallas_call x1, Pallas kernels: 3.74 us -> 2.83 us  [body(): pl.pallas_call(project_kernel, out_shape=shape(3 * radii, columns), in_sp...]
    all_to_all x1, waiting for transfers between devices: 2.59 us -> 3.47 us  [body(): lax.all_to_all(send.reshape(slabs, lines, LANES), 'gz', split_axis=0, con...]
where the time goes in v3:
time: 66 us; the launch traced here: 65.6 us
  starting transfers between devices  30 us (45%)
  waiting for transfers between devices  22.6 us (34%)
  Pallas kernels  11.7 us (18%)
  between operations  1.34 us (2%)
    all_to_all x1, starting transfers between devices, body(): lax.all_to_all(send.reshape(slabs, lines, LANES), 'gz', split_axis=0, con...  19.3 us
    ppermute x1, waiting for transfers between devices, body(): far = lax.ppermute(fields, 'gz', pairs + [(j, i) for i, j in pairs])  12.1 us
    all_to_all x1, waiting for transfers between devices, body(): lax.all_to_all(payload, 'pa', split_axis=0, concat_axis=0, tiled=True)  7 us
    all_to_all x1, starting transfers between devices, body(): lax.all_to_all(payload, 'pa', split_axis=0, concat_axis=0, tiled=True)  4.42 us
    ppermute x1, starting transfers between devices, body(): far = lax.ppermute(fields, 'gz', pairs + [(j, i) for i, j in pairs])  4.33 us
    all_to_all x1, waiting for transfers between devices, body(): lax.all_to_all(send.reshape(slabs, lines, LANES), 'gz', split_axis=0, con...  3.47 us
    pallas_call x1, Pallas kernels, body(): pl.pallas_call(functools.partial(momentum_kernel, capacity, slabs), out_s...  3.42 us
    pallas_call x1, Pallas kernels, body(): pl.pallas_call(project_kernel, out_shape=shape(3 * radii, columns), in_sp...  2.83 us
  transfers between devices with their start and end apart: 4, of which 3 were waited for; matrix products, arithmetic and copies ran while one was open for 0% of the time, Pallas kernels for 4%

profile of v3, /device:TPU:32, one launch (start us, length us, event | category | flops | bytes accessed | tf_op | source)
XLA Modules:
  0.0 65.6 jit_solution(13950089971824336253)
XLA Ops:
  1.3 2.7 %pack.1 = (f32[512,128]{1,0:T(8,128)}, f32[768,128]{1,0:T(8,128)}) custom-call(s32[1]{0:T(128)S(6)} %copy.13.counts_in, f32[16,1024]{1,0:T(8,128)} %bitcast.17, s32[1,1024]{1,0:T(1,128)} %bitcast.18, s32[1,1024]{1,0:T(1,128)} %bitcast.19, f32[576,128]{1,0:T(8,128)} %bitcast.13, f32[192,128]{1,0:T(8,128)} %bitcast.16), custom_call_target="tpu_custom_call" | custom-call | bytes 9000000 | tf_op jit(solution)/shard_map/pack/pallas_call | solution.py:481
  4.0 0.0 copy-start.2
  4.0 19.3 %all-to-all-start = ((f32[128,4,128]{2,1,0:T(4,128)}), f32[128,4,128]{2,1,0:T(4,128)S(1)}, u32[]{:S(2)}, u32[]{:S(2)}) async-start(f32[128,4,128]{2,1,0:T(4,128)} %bitcast.14), calls=%async_computation | async-start | bytes 524288 | tf_op jit(solution)/shard_map/all_to_all | solution.py:499
  23.3 0.0 copy-done.2
  23.3 4.3 %collective-permute-start.1 = (f32[768,128]{1,0:T(8,128)S(1)}, f32[768,128]{1,0:T(8,128)S(1)}, u32[]{:S(2)}, u32[]{:S(2)}) collective-permute-start(f32[768,128]{1,0:T(8,128)S(1)} %copy-done.2), channel_id=1, source_target_pairs={{4,8},{12,16},{20,24},{28,32},{36,40},{44,48},{52,56},{60,64},{68,... | collective-permute-start | bytes 1179656 | tf_op jit(solution)/shard_map/ppermute | solution.py:505
  27.7 1.9 %collective-permute-start = (f32[768,128]{1,0:T(8,128)S(1)}, f32[768,128]{1,0:T(8,128)S(1)}, u32[]{:S(2)}, u32[]{:S(2)}) collective-permute-start(f32[768,128]{1,0:T(8,128)S(1)} %copy-done.2), channel_id=1, source_target_pairs={{0,4},{4,0},{8,12},{12,8},{16,20},{20,16},{24,28},{28,24},{32,36},... | collective-permute-start | bytes 1179656 | tf_op jit(solution)/shard_map/ppermute | solution.py:503
  29.6 12.1 %collective-permute-done.1.far = f32[768,128]{1,0:T(8,128)S(1)} collective-permute-done((f32[768,128]{1,0:T(8,128)S(1)}, f32[768,128]{1,0:T(8,128)S(1)}, u32[]{:S(2)}, u32[]{:S(2)}) %collective-permute-start.1) | collective-permute-done | bytes 393248 | tf_op jit(solution)/shard_map/ppermute | solution.py:505
  41.7 0.0 collective-permute-done.near
  41.7 0.6 stencil.1
  42.3 3.5 %all-to-all-done = f32[128,4,128]{2,1,0:T(4,128)S(1)} async-done(((f32[128,4,128]{2,1,0:T(4,128)}), f32[128,4,128]{2,1,0:T(4,128)S(1)}, u32[]{:S(2)}, u32[]{:S(2)}) %all-to-all-start) | async-done | bytes 262176 | tf_op jit(solution)/shard_map/all_to_all | solution.py:499
  45.8 0.0 copy-start
  45.8 3.4 %momentum.1 = (f32[576,128]{1,0:T(8,128)S(1)}, f32[4,224,128]{2,1,0:T(8,128)}, f32[384,128]{1,0:T(8,128)S(1)}) custom-call(f32[512,128]{1,0:T(8,128)S(1)} %bitcast.11, f32[576,128]{1,0:T(8,128)S(1)} %get-tuple-element.12.partial, bf16[384,384]{1,0:T(8,128)(2,1)S(1)} %get-tuple-element.13.halves, f32[32,128]{1,0:T(8,128)S(1)} %get-tuple-element.14.edges_in), custom_call_target="tpu_custom_call" | custom-call | bytes 12000000 | tf_op jit(solution)/shard_map/momentum/pallas_call | solution.py:522
  49.2 0.0 copy-start.1
  49.2 4.4 %all-to-all-start.1 = ((f32[4,224,128]{2,1,0:T(8,128)}), f32[4,224,128]{2,1,0:T(8,128)S(1)}, u32[]{:S(2)}, u32[]{:S(2)}) async-start(f32[4,224,128]{2,1,0:T(8,128)} %get-tuple-element.15), calls=%async_computation.1 | async-start | bytes 917504 | tf_op jit(solution)/shard_map/all_to_all | solution.py:542
  53.7 2.1 %place.1 = f32[16,3072]{1,0:T(8,128)} custom-call(f32[384,128]{1,0:T(8,128)S(1)} %get-tuple-element.17.moved), custom_call_target="tpu_custom_call" | custom-call | bytes 9000000 | tf_op jit(solution)/shard_map/place/pallas_call | solution.py:543
  55.8 7.0 %all-to-all-done.1.gathered = f32[4,224,128]{2,1,0:T(8,128)S(1)} async-done(((f32[4,224,128]{2,1,0:T(8,128)}), f32[4,224,128]{2,1,0:T(8,128)S(1)}, u32[]{:S(2)}, u32[]{:S(2)}) %all-to-all-start.1) | async-done | bytes 458784 | tf_op jit(solution)/shard_map/all_to_all | solution.py:542
  62.8 0.0 copy-done
  62.8 0.0 copy-done.1
  62.8 2.8 %project.1 = f32[576,128]{1,0:T(8,128)} custom-call(f32[4,224,128]{2,1,0:T(8,128)S(1)} %all-to-all-done.1.gathered, f32[576,128]{1,0:T(8,128)S(1)} %get-tuple-element.16.ustar, bf16[320,1024]{1,0:T(8,128)(2,1)S(1)} %copy-done.1, f32[576,384]{1,0:T(8,128)S(1)} %copy-done, f32[576,384]{1,0:T(8,128)} %constant.10.clone.solve_b, f32[584,384]{1,0:T(8,128)} %constant.11.clone.solve_c), custom_call_target="tpu_custom_call" | custom-call | bytes 15000000 | tf_op jit(solution)/shard_map/project/pallas_call | solution.py:552
Async XLA Ops:
  4.0 19.3 %copy-start.2 = (f32[768,128]{1,0:T(8,128)S(1)}, f32[768,128]{1,0:T(8,128)}, u32[]{:S(2)}) copy-start(f32[768,128]{1,0:T(8,128)} %get-tuple-element.11.fields) | copy-start | bytes 1179652
  4.0 41.8 %all-to-all-start = ((f32[128,4,128]{2,1,0:T(4,128)}), f32[128,4,128]{2,1,0:T(4,128)S(1)}, u32[]{:S(2)}, u32[]{:S(2)}) async-start(f32[128,4,128]{2,1,0:T(4,128)} %bitcast.14), calls=%async_computation | async-start | bytes 524288 | tf_op jit(solution)/shard_map/all_to_all | solution.py:499
  23.3 18.4 %collective-permute-start.1 = (f32[768,128]{1,0:T(8,128)S(1)}, f32[768,128]{1,0:T(8,128)S(1)}, u32[]{:S(2)}, u32[]{:S(2)}) collective-permute-start(f32[768,128]{1,0:T(8,128)S(1)} %copy-done.2), channel_id=1, source_target_pairs={{4,8},{12,16},{20,24},{28,32},{36,40},{44,48},{52,56},{60,64},{68,... | collective-permute-start | bytes 1179656 | tf_op jit(solution)/shard_map/ppermute | solution.py:505
  27.7 14.0 %collective-permute-start = (f32[768,128]{1,0:T(8,128)S(1)}, f32[768,128]{1,0:T(8,128)S(1)}, u32[]{:S(2)}, u32[]{:S(2)}) collective-permute-start(f32[768,128]{1,0:T(8,128)S(1)} %copy-done.2), channel_id=1, source_target_pairs={{0,4},{4,0},{8,12},{12,8},{16,20},{20,16},{24,28},{28,24},{32,36},... | collective-permute-start | bytes 1179656 | tf_op jit(solution)/shard_map/ppermute | solution.py:503
  45.8 17.0 %copy-start = (f32[576,384]{1,0:T(8,128)S(1)}, f32[576,384]{1,0:T(8,128)}, u32[]{:S(2)}) copy-start(f32[576,384]{1,0:T(8,128)} %constant.9.clone.solve_a) | copy-start | bytes 2654212
  49.2 13.6 %copy-start.1 = (bf16[320,1024]{1,0:T(8,128)(2,1)S(1)}, bf16[320,1024]{1,0:T(8,128)(2,1)}, u32[]{:S(2)}) copy-start(bf16[320,1024]{1,0:T(8,128)(2,1)} %constant.8.clone.transform) | copy-start | bytes 1966084
  49.2 13.6 %all-to-all-start.1 = ((f32[4,224,128]{2,1,0:T(8,128)}), f32[4,224,128]{2,1,0:T(8,128)S(1)}, u32[]{:S(2)}, u32[]{:S(2)}) async-start(f32[4,224,128]{2,1,0:T(8,128)} %get-tuple-element.15), calls=%async_computation.1 | async-start | bytes 917504 | tf_op jit(solution)/shard_map/all_to_all | solution.py:542

commit v4 on v3

--- a/solution.py
+++ b/solution.py
@@ -33,6 +33,11 @@
     return np.concatenate([even, [half], NTH - even[1:], odd, NTH - odd])
 
 
+def split_table(table):
+    high = table.astype(jnp.bfloat16)
+    return high, (table - high.astype(np.float64)).astype(jnp.bfloat16)
+
+
 @functools.cache
 def transform_table(ring, columns):
     modes = paired_modes()[None, :]
@@ -48,22 +53,20 @@
         faces[at + 6] = wave(-1) - wave(1) - wave(0) + wave(2)
         faces[at + 8] = wave(0)
         faces[at + 9] = wave(1)
-    table = np.concatenate([plain, faces], 0)
-    high = table.astype(jnp.bfloat16)
-    low = (table - high.astype(np.float64)).astype(jnp.bfloat16)
-    return np.concatenate([high, low], 1)
+    high, low = split_table(plain)
+    face_high, face_low = split_table(faces)
+    return np.concatenate([high, low, face_high, face_low, face_high], 0)
 
 
 @functools.cache
 def solve_tables():
     radius = NR + np.arange(NR) + 0.5
     arc = 1.0 / (radius * step_angle) ** 2
-    up = (radius + 0.5) / radius
-    down = (radius - 0.5) / radius
+    up, down = radius + 0.5, radius - 0.5
     up[-1] = 0.0
     down[0] = 0.0
     spectrum = 2.0 - 2.0 * np.cos(step_angle * paired_modes())
-    diagonal = shift_plane + arc[:, None] * spectrum[None, :] + up[:, None] + down[:, None]
+    diagonal = radius[:, None] * (shift_plane + arc[:, None] * spectrum[None, :]) + up[:, None] + down[:, None]
     lower = np.broadcast_to(-down[:, None], diagonal.shape)
     upper = np.broadcast_to(-up[:, None], diagonal.shape)
 
@@ -71,24 +74,27 @@
         filled = np.full((abs(by),) + x.shape[1:], fill)
         return np.concatenate([filled, x[:-by]], 0) if by > 0 else np.concatenate([x[-by:], filled], 0)
 
-    tables, stride = [], 1
+    tables, stride = [1.0 / diagonal], 1
     while stride < SUBLANES:
         low = lower / moved(diagonal, stride, 1.0)
         high = upper / moved(diagonal, -stride, 1.0)
         diagonal = diagonal - low * moved(upper, stride, 0.0) - high * moved(lower, -stride, 0.0)
         lower = -low * moved(lower, stride, 0.0)
         upper = -high * moved(upper, -stride, 0.0)
-        tables += [low, high]
+        if stride > 1:
+            tables += [low, high]
         stride *= 2
-    multiplier = np.zeros_like(diagonal)
     pivot = diagonal.copy()
     for i in range(SUBLANES, NR):
-        multiplier[i] = lower[i] / pivot[i - SUBLANES]
-        pivot[i] = diagonal[i] - multiplier[i] * upper[i - SUBLANES]
-    tables += [multiplier, 1.0 / pivot, upper / pivot]
-    sine = 2.0 * np.sin(step_angle * paired_modes())
-    tables.append(np.broadcast_to(sine, (SUBLANES, NTH)))
-    return np.concatenate(tables, 0)[:, : 3 * NTH // 4].astype(np.float32)
+        pivot[i] = diagonal[i] - upper[i - SUBLANES] ** 2 / pivot[i - SUBLANES]
+    middle = np.zeros((NR, 2 * LANES))
+    for k, table in enumerate(tables):
+        middle[:, k] = table[:, LANES]
+    reduction = np.concatenate(tables, 0)
+    reduction = np.concatenate([reduction[:, :LANES], reduction[:, 2 * LANES : 3 * LANES]], 1)
+    sine = np.broadcast_to(2.0 * np.sin(step_angle * paired_modes()), (SUBLANES, NTH))
+    elimination = np.concatenate([1.0 / pivot, upper / pivot, sine] + tables, 0)[:, : 3 * LANES]
+    return np.concatenate([reduction, middle], 0).astype(np.float32), elimination.astype(np.float32)
 
 
 def pieces(x, count):
@@ -230,11 +236,12 @@
 
 def put_edges(edges, x, first, last):
     turned = x.T
-    for part in range(2):
-        piece = turned[:, part * LANES : min((part + 1) * LANES, x.shape[0])]
-        width = piece.shape[1]
-        edges[part * EDGE_ROWS + first : part * EDGE_ROWS + first + 1, :width] = piece[:1]
-        edges[part * EDGE_ROWS + last : part * EDGE_ROWS + last + 1, :width] = piece[LANES - 1 :]
+    rest = x.shape[0] - LANES
+    for column, row in ((first, turned[:1]), (last, turned[LANES - 1 :])):
+        edges[column : column + 1, :] = row[:, :LANES]
+        at = 10 + column % 5
+        start = column // 5 * rest
+        edges[at : at + 1, start : start + rest] = row[:, LANES:]
 
 
 def momentum_kernel(
@@ -292,7 +299,7 @@
     flux = jnp.where(row < radii - 1, (radius + 0.5) * 0.5 * (stars[1] + shifted(stars[1], -1)), 0.0)
     ahead = jnp.where(lane == columns - 1, 0.0, pltpu.roll(stars[2], columns - 1, 1))
     behind = jnp.where(lane == 0, 0.0, pltpu.roll(stars[2], 1, 1))
-    source = (shifted(flux, 1) - flux - (0.5 / step_angle) * (ahead - behind)) / radius
+    source = shifted(flux, 1) - flux - (0.5 / step_angle) * (ahead - behind)
     edges[...] = edges_in[...]
     put_edges(edges, stars[2], 8, 9)
     for q in range(payload.shape[0]):
@@ -300,27 +307,25 @@
         payload[q, radii:, :] = edges[...]
 
 
-def project_kernel(gathered, ustar, transform, solve_a, solve_b, solve_c, out, solve, state, sems):
+def project_kernel(gathered, ustar, transform, reduction, elimination_in, out, elimination, state, sem):
     me = lax.axis_index("pa")
-    steps = 3 * NR
-    fetches = [
-        pltpu.make_async_copy(solve_b, solve.at[:steps], sems.at[0]),
-        pltpu.make_async_copy(solve_c, solve.at[steps:], sems.at[1]),
-    ]
-    for fetch in fetches:
-        fetch.start()
+    fetch = pltpu.make_async_copy(elimination_in.at[: elimination.shape[0]], elimination, sem)
+    fetch.start()
     ring = gathered.shape[0]
     radii = out.shape[0] // 3
     columns = out.shape[1]
     half = NTH // 2
 
-    def turned(part):
-        base = radii + part * EDGE_ROWS
-        rows = [gathered[q % ring, base : base + EDGE_ROWS, :] for q in range(ring + 1)]
-        rows.append(jnp.zeros((LANES - (ring + 1) * EDGE_ROWS, LANES), f32))
-        return jnp.concatenate(rows, 0).T
-
-    sides = jnp.concatenate([turned(0), turned(1)[: radii - LANES]], 0)
+    rows = [gathered[q % ring, radii:, :] for q in range(ring + 1)]
+    rows.append(jnp.zeros((LANES - (ring + 1) * EDGE_ROWS, LANES), f32))
+    turned = jnp.concatenate(rows, 0).T
+    rest = radii - LANES
+    fifth = iota((rest, LANES), 1) % EDGE_ROWS < 5
+    others = jnp.where(
+        fifth, pltpu.roll(turned[:rest], LANES - 10, 1), pltpu.roll(turned[rest : 2 * rest], LANES - 5, 1)
+    )
+
+    sides = jnp.concatenate([turned, others], 0)
     row = iota((radii, LANES), 0)
     lane = iota((radii, LANES), 1)
     kind = lane % EDGE_ROWS
@@ -337,8 +342,8 @@
     used = lane < ring * EDGE_ROWS
     crossing = jnp.where(used & (kind >= 4) & (kind < 7), arc * face * (beyond - sides), 0.0)
     flux = jnp.where(row < radii - 1, (radius + 0.5) * 0.5 * (crossing + shifted(crossing, -1)), 0.0)
-    outward = (shifted(flux, 1) - flux) * inverse
-    turning = inverse * (0.5 / step_angle)
+    outward = shifted(flux, 1) - flux
+    turning = 0.5 / step_angle
     coefficients = jnp.where(
         kind == 5,
         outward,
@@ -358,65 +363,59 @@
     )
     pick = pick.astype(bf16)
     crossing_parts = [p.astype(bf16) for p in pieces(crossing, 2)]
-    delta = dot(crossing_parts[0], pick) + dot(crossing_parts[1], pick)
+    delta = dot(jnp.concatenate(crossing_parts, 1), jnp.concatenate([pick, pick], 0))
 
     near = jnp.concatenate([gathered[q, :radii, :] for q in range(ring // 2)], 1)
     distant = jnp.concatenate([gathered[q, :radii, :] for q in range(ring // 2, ring)], 1)
 
-    def product(x, rows, cols, contract=((1,), (0,))):
+    def forward(x, cols):
         high, low = [p.astype(bf16) for p in pieces(x, 2)]
-        table_high = transform[rows, cols]
-        table_low = transform[rows, slice(cols.start + NTH, cols.stop + NTH)]
-        return dot(high, table_high, contract) + (dot(high, table_low, contract) + dot(low, table_high, contract))
-
-    angles = slice(0, half)
-    corrections = slice(half, half + CORRECTION_ROWS)
+        table_high, table_low = transform[:half, cols], transform[half : 2 * half, cols]
+        return dot(high, table_high) + (dot(high, table_low) + dot(low, table_high)) + dot(corrections, transform[2 * half :, cols])
+
+    parts = [p.astype(bf16) for p in pieces(coefficients, 2)]
+    corrections = jnp.concatenate([parts[0], parts[0], parts[1]], 1)
     even = slice(0, half)
     odd = slice(half, NTH)
-    modes_even = product(near + distant, angles, even) + product(coefficients, corrections, even)
-    modes_odd = product(near - distant, angles, odd) + product(coefficients, corrections, odd)
+    modes_even = forward(near + distant, even)
+    modes_odd = forward(near - distant, odd)
     blocks = [m[:, b * LANES : (b + 1) * LANES] for m in (modes_even, modes_odd) for b in range(2)]
     total = sum(NR + i + 0.5 for i in range(NR))
-    mean = jnp.sum(radius * blocks[0], axis=0, keepdims=True) * (1.0 / total)
-    blocks[0] = blocks[0] - jnp.where(iota((1, LANES), 1) == 0, mean, 0.0)
-    held = (0, 1, 2, 2)
-
-    def factor(k, cols):
-        at = k % 3 * radii
-        return (solve_a if k < 3 else solve)[at : at + radii, cols]
-
-    fetches[0].wait()
+    mean = jnp.sum(blocks[0], axis=0, keepdims=True) * (1.0 / total)
+    blocks[0] = blocks[0] - radius * jnp.where(iota((1, LANES), 1) == 0, mean, 0.0)
+    middle = reduction[5 * radii :, :LANES]
+
+    def factor(k, b):
+        table = reduction[k * radii : (k + 1) * radii, b // 2 * LANES : (b // 2 + 1) * LANES]
+        return jnp.where(lane == 0, pltpu.roll(middle, (LANES - k) % LANES, 1), table) if b == 1 else table
+
+    inner = jnp.where(row > 0, radius - 0.5, 0.0)
+    outer = jnp.where(row < radii - 1, radius + 0.5, 0.0)
     for b in range(ring):
         x = blocks[b]
-        cols = slice(held[b] * LANES, (held[b] + 1) * LANES)
-        stride, k = 1, 0
-        while stride < SUBLANES:
-            x = (
-                x
-                - factor(k, cols) * pltpu.roll(x, stride, 0)
-                - factor(k + 1, cols) * pltpu.roll(x, radii - stride, 0)
-            )
-            stride *= 2
-            k += 2
+        scaled = x * factor(0, b)
+        x = x + inner * pltpu.roll(scaled, 1, 0) + outer * pltpu.roll(scaled, radii - 1, 0)
+        for stride, k in ((2, 1), (4, 3)):
+            x = x - factor(k, b) * pltpu.roll(x, stride, 0) - factor(k + 1, b) * pltpu.roll(x, radii - stride, 0)
         state[:, b * LANES : (b + 1) * LANES] = x
-
-    fetches[1].wait()
+    fetch.wait()
 
     def factors(k, v):
-        rows = slice((k - 3) * radii + v * SUBLANES, (k - 3) * radii + (v + 1) * SUBLANES)
-        return jnp.concatenate([solve[rows, : 3 * LANES], solve[rows, 2 * LANES : 3 * LANES]], 1)
+        at = k * radii + v * SUBLANES
+        table = elimination[at : at + SUBLANES, :]
+        return jnp.concatenate([table, table[:, 2 * LANES :]], 1)
 
     steps = radii // SUBLANES
     y = state[:SUBLANES, :]
     for v in range(1, steps):
         rows = slice(v * SUBLANES, (v + 1) * SUBLANES)
-        y = state[rows, :] - factors(6, v) * y
+        y = state[rows, :] - factors(1, v - 1) * y
         state[rows, :] = y
-    x = y * factors(7, steps - 1)
+    x = y * factors(0, steps - 1)
     state[(steps - 1) * SUBLANES :, :] = x
     for v in range(steps - 2, -1, -1):
         rows = slice(v * SUBLANES, (v + 1) * SUBLANES)
-        x = state[rows, :] * factors(7, v) - factors(8, v) * x
+        x = state[rows, :] * factors(0, v) - factors(1, v) * x
         state[rows, :] = x
 
     potential = [state[:, b * LANES : (b + 1) * LANES] for b in range(ring)]
@@ -426,18 +425,21 @@
         below = jnp.where(row == 0, x, pltpu.roll(x, 1, 0))
         return above - below
 
-    mine = pl.ds(pl.multiple_of(me % 2 * columns, columns), columns)
+    mine = pl.multiple_of(me % 2 * columns, columns)
     result = []
     for group, cols in ((0, even), (1, odd)):
         plain, mirror = potential[2 * group], potential[2 * group + 1]
-        sine = solve[6 * radii : 6 * radii + 1, 2 * group * LANES : (2 * group + 1) * LANES]
+        sine = elimination[2 * radii : 2 * radii + 1, 2 * group * LANES : (2 * group + 1) * LANES]
         slopes = jnp.concatenate([gradient(plain), gradient(mirror)], 1)
         turns = jnp.concatenate([-sine * mirror, sine * plain], 1)
-        result.append(product(jnp.concatenate([slopes, turns], 0), mine, cols, ((1,), (1,))))
+        high, low = [p.astype(bf16) for p in pieces(jnp.concatenate([slopes, turns], 0), 2)]
+        own_high, own_low = transform[pl.ds(mine, columns), cols], transform[pl.ds(half + mine, columns), cols]
+        both = dot(high, jnp.concatenate([own_high, own_low], 0), ((1,), (1,)))
+        result.append(both[:, :columns] + (both[:, columns:] + dot(low, own_high, ((1,), (1,)))))
     result = result[0] + jnp.where(me >= ring // 2, -1.0, 1.0) * result[1]
     out[:radii, :] = ustar[:radii, :] + delta[:, :columns]
     out[radii : 2 * radii, :] = ustar[radii : 2 * radii, :] + delta[:, columns : 2 * columns] - result[:radii] * (0.5 / NTH)
-    out[2 * radii :, :] = ustar[2 * radii :, :] + delta[:, 2 * columns :] - result[radii:] * (turning * (1.0 / NTH))
+    out[2 * radii :, :] = ustar[2 * radii :, :] + delta[:, 2 * columns :] - result[radii:] * (inverse * (turning / NTH))
 
 
 def place_kernel(capacity, slabs, moved, out):
@@ -504,13 +506,13 @@
     pairs = [(i, i + 1) for i in range(1, slabs - 1, 2)]
     far = lax.ppermute(fields, "gz", pairs + [(j, i) for i, j in pairs])
     transform = jnp.asarray(transform_table(ring, columns))
-    factors = solve_tables()
+    reduction, elimination = [jnp.asarray(table) for table in solve_tables()]
     partial, halves, edges = pl.pallas_call(
         stencil_kernel,
         out_shape=(
             shape(3 * radii, columns),
             jax.ShapeDtypeStruct((3 * columns, 2 * radii), bf16),
-            shape(2 * EDGE_ROWS, LANES),
+            shape(EDGE_ROWS, LANES),
         ),
         in_specs=[vmem] * 3,
         out_specs=(vmem,) * 3,
@@ -523,7 +525,7 @@
         functools.partial(momentum_kernel, capacity, slabs),
         out_shape=(
             shape(3 * radii, columns),
-            shape(ring, radii + 2 * EDGE_ROWS, columns),
+            shape(ring, radii + EDGE_ROWS, columns),
             shape(features, slabs),
         ),
         in_specs=[vmem] * 4,
@@ -532,7 +534,7 @@
             pltpu.VMEM((radii, capacity * slabs), bf16),
             pltpu.VMEM((3, capacity, slabs), f32),
             pltpu.VMEM((3 * columns, capacity * slabs), bf16),
-            pltpu.VMEM((2 * EDGE_ROWS, LANES), f32),
+            pltpu.VMEM((EDGE_ROWS, LANES), f32),
         ],
         compiler_params=params(16),
         cost_estimate=cost(4),
@@ -552,17 +554,17 @@
     velocity_out = pl.pallas_call(
         project_kernel,
         out_shape=shape(3 * radii, columns),
-        in_specs=[vmem] * 4 + [hbm] * 2,
+        in_specs=[vmem] * 4 + [hbm],
         out_specs=vmem,
         scratch_shapes=[
-            pltpu.VMEM((factors.shape[0] - 3 * radii, factors.shape[1]), f32),
+            pltpu.VMEM((2 * radii + SUBLANES, elimination.shape[1]), f32),
             pltpu.VMEM((radii, NTH), f32),
-            pltpu.SemaphoreType.DMA((2,)),
+            pltpu.SemaphoreType.DMA,
         ],
-        compiler_params=params(51.5),
+        compiler_params=params(51.25),
         cost_estimate=cost(5),
         name="project",
-    )(gathered, ustar, transform, factors[: 3 * radii], factors[3 * radii : 6 * radii], factors[6 * radii :])
+    )(gathered, ustar, transform, reduction, elimination)
     return velocity_out.reshape(velocity.shape), parcels_out.T
 
 

time: 66 us -> 65.2 us (0.988)
  waiting for transfers between devices: 22.6 us -> 21.3 us
  local copies, waits for them, and re-layouts: 0.01 us -> 1.01 us
    unnamed x6, local copies, waits for them, and re-layouts: 0.01 us -> 1.01 us
    all_to_all x1, waiting for transfers between devices: 3.47 us -> 2.48 us  [body(): lax.all_to_all(send.reshape(slabs, lines, LANES), 'gz', split_axis=0, con...]
where the time goes in v4:
time: 65.2 us; the launch traced here: 64.8 us
  starting transfers between devices  29.7 us (46%)
  waiting for transfers between devices  21.3 us (33%)
  Pallas kernels  11.5 us (18%)
  between operations  1.33 us (2%)
  local copies, waits for them, and re-layouts  1.01 us (2%)
    all_to_all x1, starting transfers between devices, body(): lax.all_to_all(send.reshape(slabs, lines, LANES), 'gz', split_axis=0, con...  19.2 us
    ppermute x1, waiting for transfers between devices, body(): far = lax.ppermute(fields, 'gz', pairs + [(j, i) for i, j in pairs])  12.1 us
    all_to_all x1, waiting for transfers between devices, body(): lax.all_to_all(payload, 'pa', split_axis=0, concat_axis=0, tiled=True)  6.64 us
    ppermute x1, starting transfers between devices, body(): far = lax.ppermute(fields, 'gz', pairs + [(j, i) for i, j in pairs])  4.33 us
    all_to_all x1, starting transfers between devices, body(): lax.all_to_all(payload, 'pa', split_axis=0, concat_axis=0, tiled=True)  4.29 us
    pallas_call x1, Pallas kernels, body(): pl.pallas_call(functools.partial(momentum_kernel, capacity, slabs), out_s...  3.51 us
    pallas_call x1, Pallas kernels, body(): pl.pallas_call(functools.partial(pack_kernel, capacity, slabs), out_shape...  2.82 us
    all_to_all x1, waiting for transfers between devices, body(): lax.all_to_all(send.reshape(slabs, lines, LANES), 'gz', split_axis=0, con...  2.48 us
  transfers between devices with their start and end apart: 4, of which 3 were waited for; matrix products, arithmetic and copies ran while one was open for 0% of the time, Pallas kernels for 4%

profile of v4, /device:TPU:32, one launch (start us, length us, event | category | flops | bytes accessed | tf_op | source)
XLA Modules:
  0.0 64.8 jit_solution(16256456382812174920)
XLA Ops:
  1.3 0.0 copy-start
  1.3 0.0 copy-start.1
  1.3 2.8 %pack.1 = (f32[512,128]{1,0:T(8,128)}, f32[768,128]{1,0:T(8,128)}) custom-call(s32[1]{0:T(128)S(6)} %copy.12.counts_in, f32[16,1024]{1,0:T(8,128)} %bitcast.17, s32[1,1024]{1,0:T(1,128)} %bitcast.18, s32[1,1024]{1,0:T(1,128)} %bitcast.19, f32[576,128]{1,0:T(8,128)} %bitcast.13, f32[192,128]{1,0:T(8,128)} %bitcast.16), custom_call_target="tpu_custom_call" | custom-call | bytes 9000000 | tf_op jit(solution)/shard_map/pack/pallas_call | solution.py:483
  4.1 19.2 %all-to-all-start = ((f32[128,4,128]{2,1,0:T(4,128)}), f32[128,4,128]{2,1,0:T(4,128)S(1)}, u32[]{:S(2)}, u32[]{:S(2)}) async-start(f32[128,4,128]{2,1,0:T(4,128)} %bitcast.14), calls=%async_computation | async-start | bytes 524288 | tf_op jit(solution)/shard_map/all_to_all | solution.py:501
  23.3 4.3 %collective-permute-start.1 = (f32[768,128]{1,0:T(8,128)}, f32[768,128]{1,0:T(8,128)S(1)}, u32[]{:S(2)}, u32[]{:S(2)}) collective-permute-start(f32[768,128]{1,0:T(8,128)} %get-tuple-element.11.fields), channel_id=1, source_target_pairs={{4,8},{12,16},{20,24},{28,32},{36,40},{44,48},{52,56},{60,64},{68,... | collective-permute-start | bytes 1179656 | tf_op jit(solution)/shard_map/ppermute | solution.py:507
  27.7 1.9 %collective-permute-start = (f32[768,128]{1,0:T(8,128)}, f32[768,128]{1,0:T(8,128)S(1)}, u32[]{:S(2)}, u32[]{:S(2)}) collective-permute-start(f32[768,128]{1,0:T(8,128)} %get-tuple-element.11.fields), channel_id=1, source_target_pairs={{0,4},{4,0},{8,12},{12,8},{16,20},{20,16},{24,28},{28,24},{32,36},... | collective-permute-start | bytes 1179656 | tf_op jit(solution)/shard_map/ppermute | solution.py:505
  29.6 12.1 %collective-permute-done.1.far = f32[768,128]{1,0:T(8,128)S(1)} collective-permute-done((f32[768,128]{1,0:T(8,128)}, f32[768,128]{1,0:T(8,128)S(1)}, u32[]{:S(2)}, u32[]{:S(2)}) %collective-permute-start.1) | collective-permute-done | bytes 393248 | tf_op jit(solution)/shard_map/ppermute | solution.py:507
  41.7 0.0 collective-permute-done.near
  41.7 0.0 copy-start.2
  41.7 1.0 %copy-done.2 = f32[768,128]{1,0:T(8,128)S(1)} copy-done((f32[768,128]{1,0:T(8,128)S(1)}, f32[768,128]{1,0:T(8,128)}, u32[]{:S(2)}) %copy-start.2) | copy-done | bytes 393240
  42.7 0.6 stencil.1
  43.4 2.5 %all-to-all-done = f32[128,4,128]{2,1,0:T(4,128)S(1)} async-done(((f32[128,4,128]{2,1,0:T(4,128)}), f32[128,4,128]{2,1,0:T(4,128)S(1)}, u32[]{:S(2)}, u32[]{:S(2)}) %all-to-all-start) | async-done | bytes 262176 | tf_op jit(solution)/shard_map/all_to_all | solution.py:501
  45.8 3.5 %momentum.1 = (f32[576,128]{1,0:T(8,128)S(1)}, f32[4,208,128]{2,1,0:T(8,128)}, f32[384,128]{1,0:T(8,128)S(1)}) custom-call(f32[512,128]{1,0:T(8,128)S(1)} %bitcast.11, f32[576,128]{1,0:T(8,128)S(1)} %get-tuple-element.12.partial, bf16[384,384]{1,0:T(8,128)(2,1)S(1)} %get-tuple-element.13.halves, f32[16,128]{1,0:T(8,128)S(1)} %get-tuple-element.14.edges_in), custom_call_target="tpu_custom_call" | custom-call | bytes 12000000 | tf_op jit(solution)/shard_map/momentum/pallas_call | solution.py:524
  49.3 4.3 %all-to-all-start.1 = ((f32[4,208,128]{2,1,0:T(8,128)}), f32[4,208,128]{2,1,0:T(8,128)S(1)}, u32[]{:S(2)}, u32[]{:S(2)}) async-start(f32[4,208,128]{2,1,0:T(8,128)} %get-tuple-element.15), calls=%async_computation.1 | async-start | bytes 851968 | tf_op jit(solution)/shard_map/all_to_all | solution.py:544
  53.6 2.2 %place.1 = f32[16,3072]{1,0:T(8,128)} custom-call(f32[384,128]{1,0:T(8,128)S(1)} %get-tuple-element.17.moved), custom_call_target="tpu_custom_call" | custom-call | bytes 9000000 | tf_op jit(solution)/shard_map/place/pallas_call | solution.py:545
  55.8 6.6 %all-to-all-done.1.gathered = f32[4,208,128]{2,1,0:T(8,128)S(1)} async-done(((f32[4,208,128]{2,1,0:T(8,128)}), f32[4,208,128]{2,1,0:T(8,128)S(1)}, u32[]{:S(2)}, u32[]{:S(2)}) %all-to-all-start.1) | async-done | bytes 426016 | tf_op jit(solution)/shard_map/all_to_all | solution.py:544
  62.4 0.0 copy-done
  62.4 0.0 copy-done.1
  62.4 2.3 %project.1 = f32[576,128]{1,0:T(8,128)} custom-call(f32[4,208,128]{2,1,0:T(8,128)S(1)} %all-to-all-done.1.gathered, f32[576,128]{1,0:T(8,128)S(1)} %get-tuple-element.16.ustar, bf16[704,512]{1,0:T(8,128)(2,1)S(1)} %copy-done.1, f32[1152,256]{1,0:T(8,128)S(1)} %copy-done, f32[1352,384]{1,0:T(8,128)} %constant.8.clone.elimination_in), custom_call_target="tpu_custom_call" | custom-call | bytes 15000000 | tf_op jit(solution)/shard_map/project/pallas_call | solution.py:554
Async XLA Ops:
  1.3 61.2 %copy-start = (f32[1152,256]{1,0:T(8,128)S(1)}, f32[1152,256]{1,0:T(8,128)}, u32[]{:S(2)}) copy-start(f32[1152,256]{1,0:T(8,128)} %constant.7.clone.reduction) | copy-start | bytes 3538948
  1.3 61.1 %copy-start.1 = (bf16[704,512]{1,0:T(8,128)(2,1)S(1)}, bf16[704,512]{1,0:T(8,128)(2,1)}, u32[]{:S(2)}) copy-start(bf16[704,512]{1,0:T(8,128)(2,1)} %constant.6.clone.transform) | copy-start | bytes 2162692
  4.1 41.7 %all-to-all-start = ((f32[128,4,128]{2,1,0:T(4,128)}), f32[128,4,128]{2,1,0:T(4,128)S(1)}, u32[]{:S(2)}, u32[]{:S(2)}) async-start(f32[128,4,128]{2,1,0:T(4,128)} %bitcast.14), calls=%async_computation | async-start | bytes 524288 | tf_op jit(solution)/shard_map/all_to_all | solution.py:501
  23.3 18.4 %collective-permute-start.1 = (f32[768,128]{1,0:T(8,128)}, f32[768,128]{1,0:T(8,128)S(1)}, u32[]{:S(2)}, u32[]{:S(2)}) collective-permute-start(f32[768,128]{1,0:T(8,128)} %get-tuple-element.11.fields), channel_id=1, source_target_pairs={{4,8},{12,16},{20,24},{28,32},{36,40},{44,48},{52,56},{60,64},{68,... | collective-permute-start | bytes 1179656 | tf_op jit(solution)/shard_map/ppermute | solution.py:507
  27.7 14.1 %collective-permute-start = (f32[768,128]{1,0:T(8,128)}, f32[768,128]{1,0:T(8,128)S(1)}, u32[]{:S(2)}, u32[]{:S(2)}) collective-permute-start(f32[768,128]{1,0:T(8,128)} %get-tuple-element.11.fields), channel_id=1, source_target_pairs={{0,4},{4,0},{8,12},{12,8},{16,20},{20,16},{24,28},{28,24},{32,36},... | collective-permute-start | bytes 1179656 | tf_op jit(solution)/shard_map/ppermute | solution.py:505
  41.7 1.0 %copy-start.2 = (f32[768,128]{1,0:T(8,128)S(1)}, f32[768,128]{1,0:T(8,128)}, u32[]{:S(2)}) copy-start(f32[768,128]{1,0:T(8,128)} %get-tuple-element.11.fields) | copy-start | bytes 1179652
  49.3 13.1 %all-to-all-start.1 = ((f32[4,208,128]{2,1,0:T(8,128)}), f32[4,208,128]{2,1,0:T(8,128)S(1)}, u32[]{:S(2)}, u32[]{:S(2)}) async-start(f32[4,208,128]{2,1,0:T(8,128)} %get-tuple-element.15), calls=%async_computation.1 | async-start | bytes 851968 | tf_op jit(solution)/shard_map/all_to_all | solution.py:544

commit v5 on v4

--- a/solution.py
+++ b/solution.py
@@ -191,6 +191,10 @@
     copies[5].wait()
 
 
+def hold_kernel(fields, held):
+    held[...] = fields[...]
+
+
 def stencil_kernel(fields, near, far, partial, halves, edges):
     radii = fields.shape[0] // 4
     columns = fields.shape[1]
@@ -229,9 +233,8 @@
     for c in range(4):
         put_edges(edges, own[c], c, 4 + c)
         if c < 3:
-            turned = own[c].T
-            parts = [p.astype(bf16) for p in pieces(turned, 2)]
-            halves[c * columns : (c + 1) * columns, :] = jnp.concatenate(parts, 1)
+            parts = [p.astype(bf16) for p in pieces(own[c], 2)]
+            halves[c * radii : (c + 1) * radii, :] = jnp.concatenate(parts, 1)
 
 
 def put_edges(edges, x, first, last):
@@ -259,12 +262,12 @@
         here = slice(j * LANES, (j + group) * LANES)
         lane_line = jnp.concatenate([line_of[s : s + 1] for s in range(j, j + group)], 1)
         lane_column = jnp.concatenate([column_of[s : s + 1] for s in range(j, j + group)], 1)
-        hot = (iota((radii, group * LANES), 0) == lane_line).astype(bf16)
-        line_hot[:, here] = hot
+        match = iota((radii, group * LANES), 0) == lane_line
+        line_hot[:, here] = match.astype(bf16)
+        hot = (iota((columns, group * LANES), 0) == lane_column).astype(bf16)
         picked = dot(halves[...], jnp.concatenate([hot, hot], 0))
-        match = iota((columns, group * LANES), 0) == lane_column
         for c in range(3):
-            got = jnp.sum(jnp.where(match, picked[c * columns : (c + 1) * columns], 0.0), axis=0, keepdims=True)
+            got = jnp.sum(jnp.where(match, picked[c * radii : (c + 1) * radii], 0.0), axis=0, keepdims=True)
             for s in range(group):
                 pulled[c, j + s : j + s + 1, :] = got[:, s * LANES : (s + 1) * LANES]
     fluid = [pulled[c] for c in range(3)]
@@ -507,11 +510,20 @@
     far = lax.ppermute(fields, "gz", pairs + [(j, i) for i, j in pairs])
     transform = jnp.asarray(transform_table(ring, columns))
     reduction, elimination = [jnp.asarray(table) for table in solve_tables()]
+    held = pl.pallas_call(
+        hold_kernel,
+        out_shape=shape(*fields.shape),
+        in_specs=[vmem],
+        out_specs=vmem,
+        compiler_params=params(16),
+        cost_estimate=cost(1),
+        name="hold",
+    )(fields)
     partial, halves, edges = pl.pallas_call(
         stencil_kernel,
         out_shape=(
             shape(3 * radii, columns),
-            jax.ShapeDtypeStruct((3 * columns, 2 * radii), bf16),
+            jax.ShapeDtypeStruct((3 * radii, 2 * columns), bf16),
             shape(EDGE_ROWS, LANES),
         ),
         in_specs=[vmem] * 3,
@@ -519,7 +531,7 @@
         compiler_params=params(16),
         cost_estimate=cost(2),
         name="stencil",
-    )(fields, near, far)
+    )(held, near, far)
 
     ustar, payload, moved = pl.pallas_call(
         functools.partial(momentum_kernel, capacity, slabs),

time: 65.2 us -> 64.9 us (level)
    ppermute x1, waiting for transfers between devices: 12.1 us -> 11 us  [body(): far = lax.ppermute(fields, 'gz', pairs + [(j, i) for i, j in pairs])]
    all_to_all x1, waiting for transfers between devices: 2.48 us -> 3.4 us  [body(): lax.all_to_all(send.reshape(slabs, lines, LANES), 'gz', split_axis=0, con...]
where the time goes in v5:
time: 64.9 us; the launch traced here: 64.5 us
  starting transfers between devices  29.9 us (46%)
  waiting for transfers between devices  21.1 us (33%)
  Pallas kernels  11.3 us (17%)
  between operations  1.35 us (2%)
  local copies, waits for them, and re-layouts  1 us (2%)
    all_to_all x1, starting transfers between devices, body(): lax.all_to_all(send.reshape(slabs, lines, LANES), 'gz', split_axis=0, con...  19.2 us
    ppermute x1, waiting for transfers between devices, body(): far = lax.ppermute(fields, 'gz', pairs + [(j, i) for i, j in pairs])  11 us
    all_to_all x1, waiting for transfers between devices, body(): lax.all_to_all(payload, 'pa', split_axis=0, concat_axis=0, tiled=True)  6.66 us
    ppermute x1, starting transfers between devices, body(): far = lax.ppermute(fields, 'gz', pairs + [(j, i) for i, j in pairs])  4.46 us
    all_to_all x1, starting transfers between devices, body(): lax.all_to_all(payload, 'pa', split_axis=0, concat_axis=0, tiled=True)  4.3 us
    pallas_call x1, Pallas kernels, body(): pl.pallas_call(functools.partial(momentum_kernel, capacity, slabs), out_s...  3.42 us
    all_to_all x1, waiting for transfers between devices, body(): lax.all_to_all(send.reshape(slabs, lines, LANES), 'gz', split_axis=0, con...  3.4 us
    pallas_call x1, Pallas kernels, body(): pl.pallas_call(functools.partial(pack_kernel, capacity, slabs), out_shape...  2.69 us
  transfers between devices with their start and end apart: 4, of which 3 were waited for; matrix products, arithmetic and copies ran while one was open for 0% of the time, Pallas kernels for 4%

profile of v5, /device:TPU:32, one launch (start us, length us, event | category | flops | bytes accessed | tf_op | source)
XLA Modules:
  0.0 64.5 jit_solution(5114548643102192319)
XLA Ops:
  1.3 2.7 %pack.1 = (f32[512,128]{1,0:T(8,128)}, f32[768,128]{1,0:T(8,128)}) custom-call(s32[1]{0:T(128)S(6)} %copy.12.counts_in, f32[16,1024]{1,0:T(8,128)} %bitcast.17, s32[1,1024]{1,0:T(1,128)} %bitcast.18, s32[1,1024]{1,0:T(1,128)} %bitcast.19, f32[576,128]{1,0:T(8,128)} %bitcast.13, f32[192,128]{1,0:T(8,128)} %bitcast.16), custom_call_target="tpu_custom_call" | custom-call | bytes 9000000 | tf_op jit(solution)/shard_map/pack/pallas_call | solution.py:486
  4.0 19.2 %all-to-all-start = ((f32[128,4,128]{2,1,0:T(4,128)}), f32[128,4,128]{2,1,0:T(4,128)S(1)}, u32[]{:S(2)}, u32[]{:S(2)}) async-start(f32[128,4,128]{2,1,0:T(4,128)} %bitcast.14), calls=%async_computation | async-start | bytes 524288 | tf_op jit(solution)/shard_map/all_to_all | solution.py:504
  23.2 0.0 copy-start
  23.2 0.0 copy-start.1
  23.2 4.5 %collective-permute-start.1 = (f32[768,128]{1,0:T(8,128)}, f32[768,128]{1,0:T(8,128)S(1)}, u32[]{:S(2)}, u32[]{:S(2)}) collective-permute-start(f32[768,128]{1,0:T(8,128)} %get-tuple-element.11.fields), channel_id=1, source_target_pairs={{4,8},{12,16},{20,24},{28,32},{36,40},{44,48},{52,56},{60,64},{68,... | collective-permute-start | bytes 1179656 | tf_op jit(solution)/shard_map/ppermute | solution.py:510
  27.7 1.9 %collective-permute-start = (f32[768,128]{1,0:T(8,128)}, f32[768,128]{1,0:T(8,128)S(1)}, u32[]{:S(2)}, u32[]{:S(2)}) collective-permute-start(f32[768,128]{1,0:T(8,128)} %get-tuple-element.11.fields), channel_id=1, source_target_pairs={{0,4},{4,0},{8,12},{12,8},{16,20},{20,16},{24,28},{28,24},{32,36},... | collective-permute-start | bytes 1179656 | tf_op jit(solution)/shard_map/ppermute | solution.py:508
  29.6 0.0 copy-start.2
  29.6 1.0 %copy-done.2 = f32[768,128]{1,0:T(8,128)S(1)} copy-done((f32[768,128]{1,0:T(8,128)S(1)}, f32[768,128]{1,0:T(8,128)}, u32[]{:S(2)}) %copy-start.2) | copy-done | bytes 393240
  30.6 11.0 %collective-permute-done.1.far = f32[768,128]{1,0:T(8,128)S(1)} collective-permute-done((f32[768,128]{1,0:T(8,128)}, f32[768,128]{1,0:T(8,128)S(1)}, u32[]{:S(2)}, u32[]{:S(2)}) %collective-permute-start.1) | collective-permute-done | bytes 393248 | tf_op jit(solution)/shard_map/ppermute | solution.py:510
  41.6 0.0 collective-permute-done.near
  41.6 0.6 %stencil.1 = (f32[576,128]{1,0:T(8,128)S(1)}, bf16[576,256]{1,0:T(8,128)(2,1)S(1)}, f32[16,128]{1,0:T(8,128)S(1)}) custom-call(f32[768,128]{1,0:T(8,128)S(1)} %hold.1.fields, f32[768,128]{1,0:T(8,128)S(1)} %collective-permute-done.near, f32[768,128]{1,0:T(8,128)S(1)} %collective-permute-done.1.far), custom_call_target="tpu_custom_call" | custom-call | bytes 6000000 | tf_op jit(solution)/shard_map/stencil/pallas_call | solution.py:522
  42.3 3.4 %all-to-all-done = f32[128,4,128]{2,1,0:T(4,128)S(1)} async-done(((f32[128,4,128]{2,1,0:T(4,128)}), f32[128,4,128]{2,1,0:T(4,128)S(1)}, u32[]{:S(2)}, u32[]{:S(2)}) %all-to-all-start) | async-done | bytes 262176 | tf_op jit(solution)/shard_map/all_to_all | solution.py:504
  45.7 3.4 %momentum.1 = (f32[576,128]{1,0:T(8,128)S(1)}, f32[4,208,128]{2,1,0:T(8,128)}, f32[384,128]{1,0:T(8,128)S(1)}) custom-call(f32[512,128]{1,0:T(8,128)S(1)} %bitcast.11, f32[576,128]{1,0:T(8,128)S(1)} %get-tuple-element.12.partial, bf16[576,256]{1,0:T(8,128)(2,1)S(1)} %get-tuple-element.13.halves, f32[16,128]{1,0:T(8,128)S(1)} %get-tuple-element.14.edges_in), custom_call_target="tpu_custom_call" | custom-call | bytes 12000000 | tf_op jit(solution)/shard_map/momentum/pallas_call | solution.py:536
  49.1 4.3 %all-to-all-start.1 = ((f32[4,208,128]{2,1,0:T(8,128)}), f32[4,208,128]{2,1,0:T(8,128)S(1)}, u32[]{:S(2)}, u32[]{:S(2)}) async-start(f32[4,208,128]{2,1,0:T(8,128)} %get-tuple-element.15), calls=%async_computation.1 | async-start | bytes 851968 | tf_op jit(solution)/shard_map/all_to_all | solution.py:556
  53.4 2.1 %place.1 = f32[16,3072]{1,0:T(8,128)} custom-call(f32[384,128]{1,0:T(8,128)S(1)} %get-tuple-element.17.moved), custom_call_target="tpu_custom_call" | custom-call | bytes 9000000 | tf_op jit(solution)/shard_map/place/pallas_call | solution.py:557
  55.5 6.7 %all-to-all-done.1.gathered = f32[4,208,128]{2,1,0:T(8,128)S(1)} async-done(((f32[4,208,128]{2,1,0:T(8,128)}), f32[4,208,128]{2,1,0:T(8,128)S(1)}, u32[]{:S(2)}, u32[]{:S(2)}) %all-to-all-start.1) | async-done | bytes 426016 | tf_op jit(solution)/shard_map/all_to_all | solution.py:556
  62.2 0.0 copy-done
  62.2 0.0 copy-done.1
  62.2 2.3 %project.1 = f32[576,128]{1,0:T(8,128)} custom-call(f32[4,208,128]{2,1,0:T(8,128)S(1)} %all-to-all-done.1.gathered, f32[576,128]{1,0:T(8,128)S(1)} %get-tuple-element.16.ustar, bf16[704,512]{1,0:T(8,128)(2,1)S(1)} %copy-done.1, f32[1152,256]{1,0:T(8,128)S(1)} %copy-done, f32[1352,384]{1,0:T(8,128)} %constant.8.clone.elimination_in), custom_call_target="tpu_custom_call" | custom-call | bytes 15000000 | tf_op jit(solution)/shard_map/project/pallas_call | solution.py:566
  (1 shorter events, 0.0 us)
Async XLA Ops:
  4.0 41.7 %all-to-all-start = ((f32[128,4,128]{2,1,0:T(4,128)}), f32[128,4,128]{2,1,0:T(4,128)S(1)}, u32[]{:S(2)}, u32[]{:S(2)}) async-start(f32[128,4,128]{2,1,0:T(4,128)} %bitcast.14), calls=%async_computation | async-start | bytes 524288 | tf_op jit(solution)/shard_map/all_to_all | solution.py:504
  23.2 39.0 %copy-start = (f32[1152,256]{1,0:T(8,128)S(1)}, f32[1152,256]{1,0:T(8,128)}, u32[]{:S(2)}) copy-start(f32[1152,256]{1,0:T(8,128)} %constant.7.clone.reduction) | copy-start | bytes 3538948
  23.2 39.0 %copy-start.1 = (bf16[704,512]{1,0:T(8,128)(2,1)S(1)}, bf16[704,512]{1,0:T(8,128)(2,1)}, u32[]{:S(2)}) copy-start(bf16[704,512]{1,0:T(8,128)(2,1)} %constant.6.clone.transform) | copy-start | bytes 2162692
  23.2 18.4 %collective-permute-start.1 = (f32[768,128]{1,0:T(8,128)}, f32[768,128]{1,0:T(8,128)S(1)}, u32[]{:S(2)}, u32[]{:S(2)}) collective-permute-start(f32[768,128]{1,0:T(8,128)} %get-tuple-element.11.fields), channel_id=1, source_target_pairs={{4,8},{12,16},{20,24},{28,32},{36,40},{44,48},{52,56},{60,64},{68,... | collective-permute-start | bytes 1179656 | tf_op jit(solution)/shard_map/ppermute | solution.py:510
  27.7 14.0 %collective-permute-start = (f32[768,128]{1,0:T(8,128)}, f32[768,128]{1,0:T(8,128)S(1)}, u32[]{:S(2)}, u32[]{:S(2)}) collective-permute-start(f32[768,128]{1,0:T(8,128)} %get-tuple-element.11.fields), channel_id=1, source_target_pairs={{0,4},{4,0},{8,12},{12,8},{16,20},{20,16},{24,28},{28,24},{32,36},... | collective-permute-start | bytes 1179656 | tf_op jit(solution)/shard_map/ppermute | solution.py:508
  29.6 1.0 %copy-start.2 = (f32[768,128]{1,0:T(8,128)S(1)}, f32[768,128]{1,0:T(8,128)}, u32[]{:S(2)}) copy-start(f32[768,128]{1,0:T(8,128)} %get-tuple-element.11.fields) | copy-start | bytes 1179652
  49.1 13.1 %all-to-all-start.1 = ((f32[4,208,128]{2,1,0:T(8,128)}), f32[4,208,128]{2,1,0:T(8,128)S(1)}, u32[]{:S(2)}, u32[]{:S(2)}) async-start(f32[4,208,128]{2,1,0:T(8,128)} %get-tuple-element.15), calls=%async_computation.1 | async-start | bytes 851968 | tf_op jit(solution)/shard_map/all_to_all | solution.py:556

commit v6 on v5

--- a/solution.py
+++ b/solution.py
@@ -145,8 +145,9 @@
     width = 256
     earlier = (iota((width, width), 0) < iota((width, width), 1)).astype(bf16)
     ones = jnp.ones((width, width), bf16)
-    features = FEATURES * capacity
-    total = features + 2 * capacity
+    thirds = capacity // SUBLANES
+    features = FEATURES * SUBLANES
+    total = features + 2 * SUBLANES
     copies[0].wait()
     copies[1].wait()
     live = iota((1, rows), 1) < counts[0]
@@ -166,8 +167,9 @@
             before = before + dot(passed.astype(bf16), ones)
         passed = mark if passed is None else passed + mark
         slot = jnp.sum(mark * before, axis=0, keepdims=True).astype(jnp.int32)
-        chosen = iota((capacity, width), 0) == slot
-        hot[:, here] = mark.astype(bf16)
+        chosen = iota((SUBLANES, width), 0) == slot % SUBLANES
+        for h in range(thirds):
+            hot[h * slabs : (h + 1) * slabs, here] = jnp.where(slot // SUBLANES == h, mark, 0.0).astype(bf16)
         split = pieces(parcels[:, here], 2)
 
         def placed(row):
@@ -177,14 +179,17 @@
             base = 0 if k == 0 else total + (k - 1) * features
             for f in range(0, FEATURES, 2):
                 pair = jnp.concatenate([placed(part[f : f + 1]), placed(part[f + 1 : f + 2])], 0)
-                spread[base + f * capacity : base + (f + 2) * capacity, here] = pair.astype(bf16)
+                spread[base + f * SUBLANES : base + (f + 2) * SUBLANES, here] = pair.astype(bf16)
         pair = jnp.concatenate([placed(line[:, here]), placed(column[:, here])], 0)
         spread[features:total, here] = pair.astype(bf16)
     out = dot(spread[...], hot[...], ((1,), (1,)))
-    values = out[:features] + out[total:]
-    filler = jnp.zeros((send.shape[0] // slabs * LANES - total, slabs), f32)
-    whole = jnp.concatenate([values, out[features:total], filler], 0)
+    values = jnp.concatenate([out[:features] + out[total:], out[features:total]], 0)
+    words = [
+        values[at : at + SUBLANES, h * slabs : (h + 1) * slabs] for at in range(0, total, SUBLANES) for h in range(thirds)
+    ]
     lines = send.shape[0] // slabs
+    words.append(jnp.zeros((lines * LANES - total * thirds, slabs), f32))
+    whole = jnp.concatenate(words, 0)
     for c in range(lines):
         send[pl.ds(c, slabs, stride=lines), :] = whole[c * LANES : (c + 1) * LANES].T
     copies[4].wait()
@@ -310,9 +315,9 @@
         payload[q, radii:, :] = edges[...]
 
 
-def project_kernel(gathered, ustar, transform, reduction, elimination_in, out, elimination, state, sem):
+def project_kernel(gathered, ustar, transform, reduction, elimination_in, out_hbm, elimination, state, out, sems):
     me = lax.axis_index("pa")
-    fetch = pltpu.make_async_copy(elimination_in.at[: elimination.shape[0]], elimination, sem)
+    fetch = pltpu.make_async_copy(elimination_in.at[: elimination.shape[0]], elimination, sems.at[0])
     fetch.start()
     ring = gathered.shape[0]
     radii = out.shape[0] // 3
@@ -368,6 +373,9 @@
     crossing_parts = [p.astype(bf16) for p in pieces(crossing, 2)]
     delta = dot(jnp.concatenate(crossing_parts, 1), jnp.concatenate([pick, pick], 0))
 
+    out[:radii, :] = ustar[:radii, :] + delta[:, :columns]
+    whole = [pltpu.make_async_copy(out.at[k : k + radii], out_hbm.at[k : k + radii], sems.at[1 + k // radii]) for k in range(0, 3 * radii, radii)]
+    whole[0].start()
     near = jnp.concatenate([gathered[q, :radii, :] for q in range(ring // 2)], 1)
     distant = jnp.concatenate([gathered[q, :radii, :] for q in range(ring // 2, ring)], 1)
 
@@ -440,9 +448,12 @@
         both = dot(high, jnp.concatenate([own_high, own_low], 0), ((1,), (1,)))
         result.append(both[:, :columns] + (both[:, columns:] + dot(low, own_high, ((1,), (1,)))))
     result = result[0] + jnp.where(me >= ring // 2, -1.0, 1.0) * result[1]
-    out[:radii, :] = ustar[:radii, :] + delta[:, :columns]
     out[radii : 2 * radii, :] = ustar[radii : 2 * radii, :] + delta[:, columns : 2 * columns] - result[:radii] * (0.5 / NTH)
+    whole[1].start()
     out[2 * radii :, :] = ustar[2 * radii :, :] + delta[:, 2 * columns :] - result[radii:] * (inverse * (turning / NTH))
+    whole[2].start()
+    for copy in whole:
+        copy.wait()
 
 
 def place_kernel(capacity, slabs, moved, out):
@@ -493,8 +504,8 @@
             pltpu.VMEM((FEATURES, block), f32),
             pltpu.VMEM((1, block), jnp.int32),
             pltpu.VMEM((1, block), jnp.int32),
-            pltpu.VMEM((2 * features + 2 * capacity, block), bf16),
-            pltpu.VMEM((slabs, block), bf16),
+            pltpu.VMEM((2 * (FEATURES + 1) * SUBLANES, block), bf16),
+            pltpu.VMEM((capacity // SUBLANES * slabs, block), bf16),
             pltpu.SemaphoreType.DMA((6,)),
         ],
         compiler_params=params(60),
@@ -567,11 +578,12 @@
         project_kernel,
         out_shape=shape(3 * radii, columns),
         in_specs=[vmem] * 4 + [hbm],
-        out_specs=vmem,
+        out_specs=hbm,
         scratch_shapes=[
             pltpu.VMEM((2 * radii + SUBLANES, elimination.shape[1]), f32),
             pltpu.VMEM((radii, NTH), f32),
-            pltpu.SemaphoreType.DMA,
+            pltpu.VMEM((3 * radii, columns), f32),
+            pltpu.SemaphoreType.DMA((4,)),
         ],
         compiler_params=params(51.25),
         cost_estimate=cost(5),

time: 64.9 us -> 64.7 us (level)
  no operation moved by 1% of the time
where the time goes in v6:
time: 64.7 us; the launch traced here: 64.3 us
  starting transfers between devices  29.8 us (46%)
  waiting for transfers between devices  21 us (32%)
  Pallas kernels  11.1 us (17%)
  between operations  1.35 us (2%)
  local copies, waits for them, and re-layouts  1 us (2%)
    all_to_all x1, starting transfers between devices, body(): lax.all_to_all(send.reshape(slabs, lines, LANES), 'gz', split_axis=0, con...  19.2 us
    ppermute x1, waiting for transfers between devices, body(): far = lax.ppermute(fields, 'gz', pairs + [(j, i) for i, j in pairs])  11 us
    all_to_all x1, waiting for transfers between devices, body(): lax.all_to_all(payload, 'pa', split_axis=0, concat_axis=0, tiled=True)  6.65 us
    ppermute x1, starting transfers between devices, body(): far = lax.ppermute(fields, 'gz', pairs + [(j, i) for i, j in pairs])  4.46 us
    all_to_all x1, starting transfers between devices, body(): lax.all_to_all(payload, 'pa', split_axis=0, concat_axis=0, tiled=True)  4.28 us
    pallas_call x1, Pallas kernels, body(): pl.pallas_call(functools.partial(momentum_kernel, capacity, slabs), out_s...  3.43 us
    all_to_all x1, waiting for transfers between devices, body(): lax.all_to_all(send.reshape(slabs, lines, LANES), 'gz', split_axis=0, con...  3.4 us
    pallas_call x1, Pallas kernels, body(): pl.pallas_call(functools.partial(pack_kernel, capacity, slabs), out_shape...  2.57 us
  transfers between devices with their start and end apart: 4, of which 3 were waited for; matrix products, arithmetic and copies ran while one was open for 0% of the time, Pallas kernels for 4%

profile of v6, /device:TPU:32, one launch (start us, length us, event | category | flops | bytes accessed | tf_op | source)
XLA Modules:
  0.0 64.3 jit_solution(8480516555222028025)
XLA Ops:
  1.3 2.6 %pack.1 = (f32[512,128]{1,0:T(8,128)}, f32[768,128]{1,0:T(8,128)}) custom-call(s32[1]{0:T(128)S(6)} %copy.12.counts_in, f32[16,1024]{1,0:T(8,128)} %bitcast.17, s32[1,1024]{1,0:T(1,128)} %bitcast.18, s32[1,1024]{1,0:T(1,128)} %bitcast.19, f32[576,128]{1,0:T(8,128)} %bitcast.13, f32[192,128]{1,0:T(8,128)} %bitcast.16), custom_call_target="tpu_custom_call" | custom-call | bytes 9000000 | tf_op jit(solution)/shard_map/pack/pallas_call | solution.py:497
  3.9 19.2 %all-to-all-start = ((f32[128,4,128]{2,1,0:T(4,128)}), f32[128,4,128]{2,1,0:T(4,128)S(1)}, u32[]{:S(2)}, u32[]{:S(2)}) async-start(f32[128,4,128]{2,1,0:T(4,128)} %bitcast.14), calls=%async_computation | async-start | bytes 524288 | tf_op jit(solution)/shard_map/all_to_all | solution.py:515
  23.0 0.0 copy-start
  23.1 0.0 copy-start.1
  23.1 4.5 %collective-permute-start.1 = (f32[768,128]{1,0:T(8,128)}, f32[768,128]{1,0:T(8,128)S(1)}, u32[]{:S(2)}, u32[]{:S(2)}) collective-permute-start(f32[768,128]{1,0:T(8,128)} %get-tuple-element.11.fields), channel_id=1, source_target_pairs={{4,8},{12,16},{20,24},{28,32},{36,40},{44,48},{52,56},{60,64},{68,... | collective-permute-start | bytes 1179656 | tf_op jit(solution)/shard_map/ppermute | solution.py:521
  27.5 1.9 %collective-permute-start = (f32[768,128]{1,0:T(8,128)}, f32[768,128]{1,0:T(8,128)S(1)}, u32[]{:S(2)}, u32[]{:S(2)}) collective-permute-start(f32[768,128]{1,0:T(8,128)} %get-tuple-element.11.fields), channel_id=1, source_target_pairs={{0,4},{4,0},{8,12},{12,8},{16,20},{20,16},{24,28},{28,24},{32,36},... | collective-permute-start | bytes 1179656 | tf_op jit(solution)/shard_map/ppermute | solution.py:519
  29.5 0.0 copy-start.2
  29.5 1.0 %copy-done.2 = f32[768,128]{1,0:T(8,128)S(1)} copy-done((f32[768,128]{1,0:T(8,128)S(1)}, f32[768,128]{1,0:T(8,128)}, u32[]{:S(2)}) %copy-start.2) | copy-done | bytes 393240
  30.5 11.0 %collective-permute-done.1.far = f32[768,128]{1,0:T(8,128)S(1)} collective-permute-done((f32[768,128]{1,0:T(8,128)}, f32[768,128]{1,0:T(8,128)S(1)}, u32[]{:S(2)}, u32[]{:S(2)}) %collective-permute-start.1) | collective-permute-done | bytes 393248 | tf_op jit(solution)/shard_map/ppermute | solution.py:521
  41.5 0.0 collective-permute-done.near
  41.5 0.6 %stencil.1 = (f32[576,128]{1,0:T(8,128)S(1)}, bf16[576,256]{1,0:T(8,128)(2,1)S(1)}, f32[16,128]{1,0:T(8,128)S(1)}) custom-call(f32[768,128]{1,0:T(8,128)S(1)} %hold.1.fields, f32[768,128]{1,0:T(8,128)S(1)} %collective-permute-done.near, f32[768,128]{1,0:T(8,128)S(1)} %collective-permute-done.1.far), custom_call_target="tpu_custom_call" | custom-call | bytes 6000000 | tf_op jit(solution)/shard_map/stencil/pallas_call | solution.py:533
  42.2 3.4 %all-to-all-done = f32[128,4,128]{2,1,0:T(4,128)S(1)} async-done(((f32[128,4,128]{2,1,0:T(4,128)}), f32[128,4,128]{2,1,0:T(4,128)S(1)}, u32[]{:S(2)}, u32[]{:S(2)}) %all-to-all-start) | async-done | bytes 262176 | tf_op jit(solution)/shard_map/all_to_all | solution.py:515
  45.6 3.4 %momentum.1 = (f32[576,128]{1,0:T(8,128)S(1)}, f32[4,208,128]{2,1,0:T(8,128)}, f32[384,128]{1,0:T(8,128)S(1)}) custom-call(f32[512,128]{1,0:T(8,128)S(1)} %bitcast.11, f32[576,128]{1,0:T(8,128)S(1)} %get-tuple-element.12.partial, bf16[576,256]{1,0:T(8,128)(2,1)S(1)} %get-tuple-element.13.halves, f32[16,128]{1,0:T(8,128)S(1)} %get-tuple-element.14.edges_in), custom_call_target="tpu_custom_call" | custom-call | bytes 12000000 | tf_op jit(solution)/shard_map/momentum/pallas_call | solution.py:547
  49.0 4.3 %all-to-all-start.1 = ((f32[4,208,128]{2,1,0:T(8,128)}), f32[4,208,128]{2,1,0:T(8,128)S(1)}, u32[]{:S(2)}, u32[]{:S(2)}) async-start(f32[4,208,128]{2,1,0:T(8,128)} %get-tuple-element.15), calls=%async_computation.1 | async-start | bytes 851968 | tf_op jit(solution)/shard_map/all_to_all | solution.py:567
  53.3 2.1 %place.1 = f32[16,3072]{1,0:T(8,128)} custom-call(f32[384,128]{1,0:T(8,128)S(1)} %get-tuple-element.17.moved), custom_call_target="tpu_custom_call" | custom-call | bytes 9000000 | tf_op jit(solution)/shard_map/place/pallas_call | solution.py:568
  55.4 6.7 %all-to-all-done.1.gathered = f32[4,208,128]{2,1,0:T(8,128)S(1)} async-done(((f32[4,208,128]{2,1,0:T(8,128)}), f32[4,208,128]{2,1,0:T(8,128)S(1)}, u32[]{:S(2)}, u32[]{:S(2)}) %all-to-all-start.1) | async-done | bytes 426016 | tf_op jit(solution)/shard_map/all_to_all | solution.py:567
  62.1 0.0 copy-done
  62.1 0.0 copy-done.1
  62.1 2.3 %project.1 = f32[576,128]{1,0:T(8,128)} custom-call(f32[4,208,128]{2,1,0:T(8,128)S(1)} %all-to-all-done.1.gathered, f32[576,128]{1,0:T(8,128)S(1)} %get-tuple-element.16.ustar, bf16[704,512]{1,0:T(8,128)(2,1)S(1)} %copy-done.1, f32[1152,256]{1,0:T(8,128)S(1)} %copy-done, f32[1352,384]{1,0:T(8,128)} %constant.8.clone.elimination_in), custom_call_target="tpu_custom_call" | custom-call | bytes 15000000 | tf_op jit(solution)/shard_map/project/pallas_call | solution.py:577
  (1 shorter events, 0.0 us)
Async XLA Ops:
  3.9 41.7 %all-to-all-start = ((f32[128,4,128]{2,1,0:T(4,128)}), f32[128,4,128]{2,1,0:T(4,128)S(1)}, u32[]{:S(2)}, u32[]{:S(2)}) async-start(f32[128,4,128]{2,1,0:T(4,128)} %bitcast.14), calls=%async_computation | async-start | bytes 524288 | tf_op jit(solution)/shard_map/all_to_all | solution.py:515
  23.0 39.0 %copy-start = (f32[1152,256]{1,0:T(8,128)S(1)}, f32[1152,256]{1,0:T(8,128)}, u32[]{:S(2)}) copy-start(f32[1152,256]{1,0:T(8,128)} %constant.7.clone.reduction) | copy-start | bytes 3538948
  23.1 39.0 %copy-start.1 = (bf16[704,512]{1,0:T(8,128)(2,1)S(1)}, bf16[704,512]{1,0:T(8,128)(2,1)}, u32[]{:S(2)}) copy-start(bf16[704,512]{1,0:T(8,128)(2,1)} %constant.6.clone.transform) | copy-start | bytes 2162692
  23.1 18.4 %collective-permute-start.1 = (f32[768,128]{1,0:T(8,128)}, f32[768,128]{1,0:T(8,128)S(1)}, u32[]{:S(2)}, u32[]{:S(2)}) collective-permute-start(f32[768,128]{1,0:T(8,128)} %get-tuple-element.11.fields), channel_id=1, source_target_pairs={{4,8},{12,16},{20,24},{28,32},{36,40},{44,48},{52,56},{60,64},{68,... | collective-permute-start | bytes 1179656 | tf_op jit(solution)/shard_map/ppermute | solution.py:521
  27.5 14.0 %collective-permute-start = (f32[768,128]{1,0:T(8,128)}, f32[768,128]{1,0:T(8,128)S(1)}, u32[]{:S(2)}, u32[]{:S(2)}) collective-permute-start(f32[768,128]{1,0:T(8,128)} %get-tuple-element.11.fields), channel_id=1, source_target_pairs={{0,4},{4,0},{8,12},{12,8},{16,20},{20,16},{24,28},{28,24},{32,36},... | collective-permute-start | bytes 1179656 | tf_op jit(solution)/shard_map/ppermute | solution.py:519
  29.5 1.0 %copy-start.2 = (f32[768,128]{1,0:T(8,128)S(1)}, f32[768,128]{1,0:T(8,128)}, u32[]{:S(2)}) copy-start(f32[768,128]{1,0:T(8,128)} %get-tuple-element.11.fields) | copy-start | bytes 1179652
  49.0 13.1 %all-to-all-start.1 = ((f32[4,208,128]{2,1,0:T(8,128)}), f32[4,208,128]{2,1,0:T(8,128)S(1)}, u32[]{:S(2)}, u32[]{:S(2)}) async-start(f32[4,208,128]{2,1,0:T(8,128)} %get-tuple-element.15), calls=%async_computation.1 | async-start | bytes 851968 | tf_op jit(solution)/shard_map/all_to_all | solution.py:567

commit v7 on v6

--- a/solution.py
+++ b/solution.py
@@ -262,7 +262,7 @@
     features = FEATURES * capacity
     line_of = turned[features : features + capacity].astype(jnp.int32) - 1
     column_of = turned[features + capacity : features + 2 * capacity].astype(jnp.int32)
-    group = 2
+    group = 4
     for j in range(0, capacity, group):
         here = slice(j * LANES, (j + group) * LANES)
         lane_line = jnp.concatenate([line_of[s : s + 1] for s in range(j, j + group)], 1)
@@ -459,11 +459,11 @@
 def place_kernel(capacity, slabs, moved, out):
     rows = slabs * capacity
     width = 768
-    split = jnp.concatenate([p.astype(bf16) for p in pieces(moved[...], 3)], 1)
+    split = jnp.concatenate([p.astype(bf16) for p in pieces(moved[...], 2)], 1)
     for start in range(0, rows, width):
         place = start + iota((slabs, width), 1)
         hot = (place // capacity == iota((slabs, width), 0)).astype(bf16)
-        spread = dot(split, jnp.concatenate([hot, hot, hot], 0))
+        spread = dot(split, jnp.concatenate([hot, hot], 0))
         match = (start + iota((capacity, width), 1)) % capacity == iota((capacity, width), 0)
         for f in range(FEATURES):
             block = spread[f * capacity : (f + 1) * capacity]

time: 64.7 us -> 64.7 us (level)
  no operation moved by 1% of the time
where the time goes in v7:
time: 64.7 us; the launch traced here: 64.4 us
  starting transfers between devices  29.9 us (46%)
  waiting for transfers between devices  21.4 us (33%)
  Pallas kernels  10.8 us (17%)
  between operations  1.35 us (2%)
  local copies, waits for them, and re-layouts  1 us (2%)
    all_to_all x1, starting transfers between devices, body(): lax.all_to_all(send.reshape(slabs, lines, LANES), 'gz', split_axis=0, con...  19.2 us
    ppermute x1, waiting for transfers between devices, body(): far = lax.ppermute(fields, 'gz', pairs + [(j, i) for i, j in pairs])  11 us
    all_to_all x1, waiting for transfers between devices, body(): lax.all_to_all(payload, 'pa', split_axis=0, concat_axis=0, tiled=True)  7 us
    ppermute x1, starting transfers between devices, body(): far = lax.ppermute(fields, 'gz', pairs + [(j, i) for i, j in pairs])  4.46 us
    all_to_all x1, starting transfers between devices, body(): lax.all_to_all(payload, 'pa', split_axis=0, concat_axis=0, tiled=True)  4.28 us
    pallas_call x1, Pallas kernels, body(): pl.pallas_call(functools.partial(momentum_kernel, capacity, slabs), out_s...  3.44 us
    all_to_all x1, waiting for transfers between devices, body(): lax.all_to_all(send.reshape(slabs, lines, LANES), 'gz', split_axis=0, con...  3.4 us
    pallas_call x1, Pallas kernels, body(): pl.pallas_call(functools.partial(pack_kernel, capacity, slabs), out_shape...  2.57 us
  transfers between devices with their start and end apart: 4, of which 3 were waited for; matrix products, arithmetic and copies ran while one was open for 0% of the time, Pallas kernels for 4%

profile of v7, /device:TPU:32, one launch (start us, length us, event | category | flops | bytes accessed | tf_op | source)
XLA Modules:
  0.0 64.4 jit_solution(4769987645453500007)
XLA Ops:
  1.3 2.6 %pack.1 = (f32[512,128]{1,0:T(8,128)}, f32[768,128]{1,0:T(8,128)}) custom-call(s32[1]{0:T(128)S(6)} %copy.12.counts_in, f32[16,1024]{1,0:T(8,128)} %bitcast.17, s32[1,1024]{1,0:T(1,128)} %bitcast.18, s32[1,1024]{1,0:T(1,128)} %bitcast.19, f32[576,128]{1,0:T(8,128)} %bitcast.13, f32[192,128]{1,0:T(8,128)} %bitcast.16), custom_call_target="tpu_custom_call" | custom-call | bytes 9000000 | tf_op jit(solution)/shard_map/pack/pallas_call | solution.py:497
  3.9 19.2 %all-to-all-start = ((f32[128,4,128]{2,1,0:T(4,128)}), f32[128,4,128]{2,1,0:T(4,128)S(1)}, u32[]{:S(2)}, u32[]{:S(2)}) async-start(f32[128,4,128]{2,1,0:T(4,128)} %bitcast.14), calls=%async_computation | async-start | bytes 524288 | tf_op jit(solution)/shard_map/all_to_all | solution.py:515
  23.0 0.0 copy-start
  23.1 0.0 copy-start.1
  23.1 4.5 %collective-permute-start.1 = (f32[768,128]{1,0:T(8,128)}, f32[768,128]{1,0:T(8,128)S(1)}, u32[]{:S(2)}, u32[]{:S(2)}) collective-permute-start(f32[768,128]{1,0:T(8,128)} %get-tuple-element.11.fields), channel_id=1, source_target_pairs={{4,8},{12,16},{20,24},{28,32},{36,40},{44,48},{52,56},{60,64},{68,... | collective-permute-start | bytes 1179656 | tf_op jit(solution)/shard_map/ppermute | solution.py:521
  27.5 1.9 %collective-permute-start = (f32[768,128]{1,0:T(8,128)}, f32[768,128]{1,0:T(8,128)S(1)}, u32[]{:S(2)}, u32[]{:S(2)}) collective-permute-start(f32[768,128]{1,0:T(8,128)} %get-tuple-element.11.fields), channel_id=1, source_target_pairs={{0,4},{4,0},{8,12},{12,8},{16,20},{20,16},{24,28},{28,24},{32,36},... | collective-permute-start | bytes 1179656 | tf_op jit(solution)/shard_map/ppermute | solution.py:519
  29.5 0.0 copy-start.2
  29.5 1.0 %copy-done.2 = f32[768,128]{1,0:T(8,128)S(1)} copy-done((f32[768,128]{1,0:T(8,128)S(1)}, f32[768,128]{1,0:T(8,128)}, u32[]{:S(2)}) %copy-start.2) | copy-done | bytes 393240
  30.5 11.0 %collective-permute-done.1.far = f32[768,128]{1,0:T(8,128)S(1)} collective-permute-done((f32[768,128]{1,0:T(8,128)}, f32[768,128]{1,0:T(8,128)S(1)}, u32[]{:S(2)}, u32[]{:S(2)}) %collective-permute-start.1) | collective-permute-done | bytes 393248 | tf_op jit(solution)/shard_map/ppermute | solution.py:521
  41.5 0.0 collective-permute-done.near
  41.5 0.6 %stencil.1 = (f32[576,128]{1,0:T(8,128)S(1)}, bf16[576,256]{1,0:T(8,128)(2,1)S(1)}, f32[16,128]{1,0:T(8,128)S(1)}) custom-call(f32[768,128]{1,0:T(8,128)S(1)} %hold.1.fields, f32[768,128]{1,0:T(8,128)S(1)} %collective-permute-done.near, f32[768,128]{1,0:T(8,128)S(1)} %collective-permute-done.1.far), custom_call_target="tpu_custom_call" | custom-call | bytes 6000000 | tf_op jit(solution)/shard_map/stencil/pallas_call | solution.py:533
  42.2 3.4 %all-to-all-done = f32[128,4,128]{2,1,0:T(4,128)S(1)} async-done(((f32[128,4,128]{2,1,0:T(4,128)}), f32[128,4,128]{2,1,0:T(4,128)S(1)}, u32[]{:S(2)}, u32[]{:S(2)}) %all-to-all-start) | async-done | bytes 262176 | tf_op jit(solution)/shard_map/all_to_all | solution.py:515
  45.6 3.4 %momentum.1 = (f32[576,128]{1,0:T(8,128)S(1)}, f32[4,208,128]{2,1,0:T(8,128)}, f32[384,128]{1,0:T(8,128)S(1)}) custom-call(f32[512,128]{1,0:T(8,128)S(1)} %bitcast.11, f32[576,128]{1,0:T(8,128)S(1)} %get-tuple-element.12.partial, bf16[576,256]{1,0:T(8,128)(2,1)S(1)} %get-tuple-element.13.halves, f32[16,128]{1,0:T(8,128)S(1)} %get-tuple-element.14.edges_in), custom_call_target="tpu_custom_call" | custom-call | bytes 12000000 | tf_op jit(solution)/shard_map/momentum/pallas_call | solution.py:547
  49.0 4.3 %all-to-all-start.1 = ((f32[4,208,128]{2,1,0:T(8,128)}), f32[4,208,128]{2,1,0:T(8,128)S(1)}, u32[]{:S(2)}, u32[]{:S(2)}) async-start(f32[4,208,128]{2,1,0:T(8,128)} %get-tuple-element.15), calls=%async_computation.1 | async-start | bytes 851968 | tf_op jit(solution)/shard_map/all_to_all | solution.py:567
  53.3 1.8 %place.1 = f32[16,3072]{1,0:T(8,128)} custom-call(f32[384,128]{1,0:T(8,128)S(1)} %get-tuple-element.17.moved), custom_call_target="tpu_custom_call" | custom-call | bytes 9000000 | tf_op jit(solution)/shard_map/place/pallas_call | solution.py:568
  55.1 7.0 %all-to-all-done.1.gathered = f32[4,208,128]{2,1,0:T(8,128)S(1)} async-done(((f32[4,208,128]{2,1,0:T(8,128)}), f32[4,208,128]{2,1,0:T(8,128)S(1)}, u32[]{:S(2)}, u32[]{:S(2)}) %all-to-all-start.1) | async-done | bytes 426016 | tf_op jit(solution)/shard_map/all_to_all | solution.py:567
  62.1 0.0 copy-done
  62.1 0.0 copy-done.1
  62.1 2.3 %project.1 = f32[576,128]{1,0:T(8,128)} custom-call(f32[4,208,128]{2,1,0:T(8,128)S(1)} %all-to-all-done.1.gathered, f32[576,128]{1,0:T(8,128)S(1)} %get-tuple-element.16.ustar, bf16[704,512]{1,0:T(8,128)(2,1)S(1)} %copy-done.1, f32[1152,256]{1,0:T(8,128)S(1)} %copy-done, f32[1352,384]{1,0:T(8,128)} %constant.8.clone.elimination_in), custom_call_target="tpu_custom_call" | custom-call | bytes 15000000 | tf_op jit(solution)/shard_map/project/pallas_call | solution.py:577
  (1 shorter events, 0.0 us)
Async XLA Ops:
  3.9 41.7 %all-to-all-start = ((f32[128,4,128]{2,1,0:T(4,128)}), f32[128,4,128]{2,1,0:T(4,128)S(1)}, u32[]{:S(2)}, u32[]{:S(2)}) async-start(f32[128,4,128]{2,1,0:T(4,128)} %bitcast.14), calls=%async_computation | async-start | bytes 524288 | tf_op jit(solution)/shard_map/all_to_all | solution.py:515
  23.0 39.0 %copy-start = (f32[1152,256]{1,0:T(8,128)S(1)}, f32[1152,256]{1,0:T(8,128)}, u32[]{:S(2)}) copy-start(f32[1152,256]{1,0:T(8,128)} %constant.7.clone.reduction) | copy-start | bytes 3538948
  23.1 39.0 %copy-start.1 = (bf16[704,512]{1,0:T(8,128)(2,1)S(1)}, bf16[704,512]{1,0:T(8,128)(2,1)}, u32[]{:S(2)}) copy-start(bf16[704,512]{1,0:T(8,128)(2,1)} %constant.6.clone.transform) | copy-start | bytes 2162692
  23.1 18.4 %collective-permute-start.1 = (f32[768,128]{1,0:T(8,128)}, f32[768,128]{1,0:T(8,128)S(1)}, u32[]{:S(2)}, u32[]{:S(2)}) collective-permute-start(f32[768,128]{1,0:T(8,128)} %get-tuple-element.11.fields), channel_id=1, source_target_pairs={{4,8},{12,16},{20,24},{28,32},{36,40},{44,48},{52,56},{60,64},{68,... | collective-permute-start | bytes 1179656 | tf_op jit(solution)/shard_map/ppermute | solution.py:521
  27.5 14.0 %collective-permute-start = (f32[768,128]{1,0:T(8,128)}, f32[768,128]{1,0:T(8,128)S(1)}, u32[]{:S(2)}, u32[]{:S(2)}) collective-permute-start(f32[768,128]{1,0:T(8,128)} %get-tuple-element.11.fields), channel_id=1, source_target_pairs={{0,4},{4,0},{8,12},{12,8},{16,20},{20,16},{24,28},{28,24},{32,36},... | collective-permute-start | bytes 1179656 | tf_op jit(solution)/shard_map/ppermute | solution.py:519
  29.5 1.0 %copy-start.2 = (f32[768,128]{1,0:T(8,128)S(1)}, f32[768,128]{1,0:T(8,128)}, u32[]{:S(2)}) copy-start(f32[768,128]{1,0:T(8,128)} %get-tuple-element.11.fields) | copy-start | bytes 1179652
  49.0 13.1 %all-to-all-start.1 = ((f32[4,208,128]{2,1,0:T(8,128)}), f32[4,208,128]{2,1,0:T(8,128)S(1)}, u32[]{:S(2)}, u32[]{:S(2)}) async-start(f32[4,208,128]{2,1,0:T(8,128)} %get-tuple-element.15), calls=%async_computation.1 | async-start | bytes 851968 | tf_op jit(solution)/shard_map/all_to_all | solution.py:567

commit v8 on v7

--- a/solution.py
+++ b/solution.py
@@ -361,7 +361,7 @@
     coefficients = jnp.where(used, coefficients, 0.0)[:, :CORRECTION_ROWS]
 
     width = 3 * columns
-    wide_row = iota((LANES, width), 0)
+    wide_row = iota((LANES, width), 0) % (ring * EDGE_ROWS)
     wide_lane = iota((LANES, width), 1)
     before = lax.rem(me + ring - 1, ring)
     inside = wide_lane % columns
@@ -370,8 +370,8 @@
         (inside == 0) & (wide_row == at + before * EDGE_ROWS), 1.0, 0.0
     )
     pick = pick.astype(bf16)
-    crossing_parts = [p.astype(bf16) for p in pieces(crossing, 2)]
-    delta = dot(jnp.concatenate(crossing_parts, 1), jnp.concatenate([pick, pick], 0))
+    crossing_high, crossing_low = pieces(crossing, 2)
+    delta = dot((crossing_high + pltpu.roll(crossing_low, ring * EDGE_ROWS, 1)).astype(bf16), pick)
 
     out[:radii, :] = ustar[:radii, :] + delta[:, :columns]
     whole = [pltpu.make_async_copy(out.at[k : k + radii], out_hbm.at[k : k + radii], sems.at[1 + k // radii]) for k in range(0, 3 * radii, radii)]

time: 64.7 us -> 64.8 us (level)
  no operation moved by 1% of the time
where the time goes in v8:
time: 64.8 us; the launch traced here: 64.5 us
  starting transfers between devices  29.9 us (46%)
  waiting for transfers between devices  21.4 us (33%)
  Pallas kernels  10.9 us (17%)
  between operations  1.35 us (2%)
  local copies, waits for them, and re-layouts  1 us (2%)
    all_to_all x1, starting transfers between devices, body(): lax.all_to_all(send.reshape(slabs, lines, LANES), 'gz', split_axis=0, con...  19.2 us
    ppermute x1, waiting for transfers between devices, body(): far = lax.ppermute(fields, 'gz', pairs + [(j, i) for i, j in pairs])  11 us
    all_to_all x1, waiting for transfers between devices, body(): lax.all_to_all(payload, 'pa', split_axis=0, concat_axis=0, tiled=True)  7 us
    ppermute x1, starting transfers between devices, body(): far = lax.ppermute(fields, 'gz', pairs + [(j, i) for i, j in pairs])  4.46 us
    all_to_all x1, starting transfers between devices, body(): lax.all_to_all(payload, 'pa', split_axis=0, concat_axis=0, tiled=True)  4.28 us
    pallas_call x1, Pallas kernels, body(): pl.pallas_call(functools.partial(momentum_kernel, capacity, slabs), out_s...  3.44 us
    all_to_all x1, waiting for transfers between devices, body(): lax.all_to_all(send.reshape(slabs, lines, LANES), 'gz', split_axis=0, con...  3.4 us
    pallas_call x1, Pallas kernels, body(): pl.pallas_call(functools.partial(pack_kernel, capacity, slabs), out_shape...  2.57 us
  transfers between devices with their start and end apart: 4, of which 3 were waited for; matrix products, arithmetic and copies ran while one was open for 0% of the time, Pallas kernels for 4%

profile of v8, /device:TPU:32, one launch (start us, length us, event | category | flops | bytes accessed | tf_op | source)
XLA Modules:
  0.0 64.5 jit_solution(10142636702558997633)
XLA Ops:
  1.3 2.6 %pack.1 = (f32[512,128]{1,0:T(8,128)}, f32[768,128]{1,0:T(8,128)}) custom-call(s32[1]{0:T(128)S(6)} %copy.12.counts_in, f32[16,1024]{1,0:T(8,128)} %bitcast.17, s32[1,1024]{1,0:T(1,128)} %bitcast.18, s32[1,1024]{1,0:T(1,128)} %bitcast.19, f32[576,128]{1,0:T(8,128)} %bitcast.13, f32[192,128]{1,0:T(8,128)} %bitcast.16), custom_call_target="tpu_custom_call" | custom-call | bytes 9000000 | tf_op jit(solution)/shard_map/pack/pallas_call | solution.py:497
  3.9 19.2 %all-to-all-start = ((f32[128,4,128]{2,1,0:T(4,128)}), f32[128,4,128]{2,1,0:T(4,128)S(1)}, u32[]{:S(2)}, u32[]{:S(2)}) async-start(f32[128,4,128]{2,1,0:T(4,128)} %bitcast.14), calls=%async_computation | async-start | bytes 524288 | tf_op jit(solution)/shard_map/all_to_all | solution.py:515
  23.0 0.0 copy-start
  23.1 0.0 copy-start.1
  23.1 4.5 %collective-permute-start.1 = (f32[768,128]{1,0:T(8,128)}, f32[768,128]{1,0:T(8,128)S(1)}, u32[]{:S(2)}, u32[]{:S(2)}) collective-permute-start(f32[768,128]{1,0:T(8,128)} %get-tuple-element.11.fields), channel_id=1, source_target_pairs={{4,8},{12,16},{20,24},{28,32},{36,40},{44,48},{52,56},{60,64},{68,... | collective-permute-start | bytes 1179656 | tf_op jit(solution)/shard_map/ppermute | solution.py:521
  27.5 1.9 %collective-permute-start = (f32[768,128]{1,0:T(8,128)}, f32[768,128]{1,0:T(8,128)S(1)}, u32[]{:S(2)}, u32[]{:S(2)}) collective-permute-start(f32[768,128]{1,0:T(8,128)} %get-tuple-element.11.fields), channel_id=1, source_target_pairs={{0,4},{4,0},{8,12},{12,8},{16,20},{20,16},{24,28},{28,24},{32,36},... | collective-permute-start | bytes 1179656 | tf_op jit(solution)/shard_map/ppermute | solution.py:519
  29.5 0.0 copy-start.2
  29.5 1.0 %copy-done.2 = f32[768,128]{1,0:T(8,128)S(1)} copy-done((f32[768,128]{1,0:T(8,128)S(1)}, f32[768,128]{1,0:T(8,128)}, u32[]{:S(2)}) %copy-start.2) | copy-done | bytes 393240
  30.5 11.0 %collective-permute-done.1.far = f32[768,128]{1,0:T(8,128)S(1)} collective-permute-done((f32[768,128]{1,0:T(8,128)}, f32[768,128]{1,0:T(8,128)S(1)}, u32[]{:S(2)}, u32[]{:S(2)}) %collective-permute-start.1) | collective-permute-done | bytes 393248 | tf_op jit(solution)/shard_map/ppermute | solution.py:521
  41.5 0.0 collective-permute-done.near
  41.5 0.6 %stencil.1 = (f32[576,128]{1,0:T(8,128)S(1)}, bf16[576,256]{1,0:T(8,128)(2,1)S(1)}, f32[16,128]{1,0:T(8,128)S(1)}) custom-call(f32[768,128]{1,0:T(8,128)S(1)} %hold.1.fields, f32[768,128]{1,0:T(8,128)S(1)} %collective-permute-done.near, f32[768,128]{1,0:T(8,128)S(1)} %collective-permute-done.1.far), custom_call_target="tpu_custom_call" | custom-call | bytes 6000000 | tf_op jit(solution)/shard_map/stencil/pallas_call | solution.py:533
  42.2 3.4 %all-to-all-done = f32[128,4,128]{2,1,0:T(4,128)S(1)} async-done(((f32[128,4,128]{2,1,0:T(4,128)}), f32[128,4,128]{2,1,0:T(4,128)S(1)}, u32[]{:S(2)}, u32[]{:S(2)}) %all-to-all-start) | async-done | bytes 262176 | tf_op jit(solution)/shard_map/all_to_all | solution.py:515
  45.6 3.4 %momentum.1 = (f32[576,128]{1,0:T(8,128)S(1)}, f32[4,208,128]{2,1,0:T(8,128)}, f32[384,128]{1,0:T(8,128)S(1)}) custom-call(f32[512,128]{1,0:T(8,128)S(1)} %bitcast.11, f32[576,128]{1,0:T(8,128)S(1)} %get-tuple-element.12.partial, bf16[576,256]{1,0:T(8,128)(2,1)S(1)} %get-tuple-element.13.halves, f32[16,128]{1,0:T(8,128)S(1)} %get-tuple-element.14.edges_in), custom_call_target="tpu_custom_call" | custom-call | bytes 12000000 | tf_op jit(solution)/shard_map/momentum/pallas_call | solution.py:547
  49.0 4.3 %all-to-all-start.1 = ((f32[4,208,128]{2,1,0:T(8,128)}), f32[4,208,128]{2,1,0:T(8,128)S(1)}, u32[]{:S(2)}, u32[]{:S(2)}) async-start(f32[4,208,128]{2,1,0:T(8,128)} %get-tuple-element.15), calls=%async_computation.1 | async-start | bytes 851968 | tf_op jit(solution)/shard_map/all_to_all | solution.py:567
  53.3 1.8 %place.1 = f32[16,3072]{1,0:T(8,128)} custom-call(f32[384,128]{1,0:T(8,128)S(1)} %get-tuple-element.17.moved), custom_call_target="tpu_custom_call" | custom-call | bytes 9000000 | tf_op jit(solution)/shard_map/place/pallas_call | solution.py:568
  55.1 7.0 %all-to-all-done.1.gathered = f32[4,208,128]{2,1,0:T(8,128)S(1)} async-done(((f32[4,208,128]{2,1,0:T(8,128)}), f32[4,208,128]{2,1,0:T(8,128)S(1)}, u32[]{:S(2)}, u32[]{:S(2)}) %all-to-all-start.1) | async-done | bytes 426016 | tf_op jit(solution)/shard_map/all_to_all | solution.py:567
  62.1 0.0 copy-done
  62.1 0.0 copy-done.1
  62.1 2.4 %project.1 = f32[576,128]{1,0:T(8,128)} custom-call(f32[4,208,128]{2,1,0:T(8,128)S(1)} %all-to-all-done.1.gathered, f32[576,128]{1,0:T(8,128)S(1)} %get-tuple-element.16.ustar, bf16[704,512]{1,0:T(8,128)(2,1)S(1)} %copy-done.1, f32[1152,256]{1,0:T(8,128)S(1)} %copy-done, f32[1352,384]{1,0:T(8,128)} %constant.8.clone.elimination_in), custom_call_target="tpu_custom_call" | custom-call | bytes 15000000 | tf_op jit(solution)/shard_map/project/pallas_call | solution.py:577
  (1 shorter events, 0.0 us)
Async XLA Ops:
  3.9 41.7 %all-to-all-start = ((f32[128,4,128]{2,1,0:T(4,128)}), f32[128,4,128]{2,1,0:T(4,128)S(1)}, u32[]{:S(2)}, u32[]{:S(2)}) async-start(f32[128,4,128]{2,1,0:T(4,128)} %bitcast.14), calls=%async_computation | async-start | bytes 524288 | tf_op jit(solution)/shard_map/all_to_all | solution.py:515
  23.0 39.0 %copy-start = (f32[1152,256]{1,0:T(8,128)S(1)}, f32[1152,256]{1,0:T(8,128)}, u32[]{:S(2)}) copy-start(f32[1152,256]{1,0:T(8,128)} %constant.7.clone.reduction) | copy-start | bytes 3538948
  23.1 39.0 %copy-start.1 = (bf16[704,512]{1,0:T(8,128)(2,1)S(1)}, bf16[704,512]{1,0:T(8,128)(2,1)}, u32[]{:S(2)}) copy-start(bf16[704,512]{1,0:T(8,128)(2,1)} %constant.6.clone.transform) | copy-start | bytes 2162692
  23.1 18.4 %collective-permute-start.1 = (f32[768,128]{1,0:T(8,128)}, f32[768,128]{1,0:T(8,128)S(1)}, u32[]{:S(2)}, u32[]{:S(2)}) collective-permute-start(f32[768,128]{1,0:T(8,128)} %get-tuple-element.11.fields), channel_id=1, source_target_pairs={{4,8},{12,16},{20,24},{28,32},{36,40},{44,48},{52,56},{60,64},{68,... | collective-permute-start | bytes 1179656 | tf_op jit(solution)/shard_map/ppermute | solution.py:521
  27.5 14.0 %collective-permute-start = (f32[768,128]{1,0:T(8,128)}, f32[768,128]{1,0:T(8,128)S(1)}, u32[]{:S(2)}, u32[]{:S(2)}) collective-permute-start(f32[768,128]{1,0:T(8,128)} %get-tuple-element.11.fields), channel_id=1, source_target_pairs={{0,4},{4,0},{8,12},{12,8},{16,20},{20,16},{24,28},{28,24},{32,36},... | collective-permute-start | bytes 1179656 | tf_op jit(solution)/shard_map/ppermute | solution.py:519
  29.5 1.0 %copy-start.2 = (f32[768,128]{1,0:T(8,128)S(1)}, f32[768,128]{1,0:T(8,128)}, u32[]{:S(2)}) copy-start(f32[768,128]{1,0:T(8,128)} %get-tuple-element.11.fields) | copy-start | bytes 1179652
  49.0 13.1 %all-to-all-start.1 = ((f32[4,208,128]{2,1,0:T(8,128)}), f32[4,208,128]{2,1,0:T(8,128)S(1)}, u32[]{:S(2)}, u32[]{:S(2)}) async-start(f32[4,208,128]{2,1,0:T(8,128)} %get-tuple-element.15), calls=%async_computation.1 | async-start | bytes 851968 | tf_op jit(solution)/shard_map/all_to_all | solution.py:567
